TPU v7x, 32 devices: a whole 2x2x4 slice. The times are simulated.
32 devices in a mesh: group: 4 (over z), tile: 8 (over y, x, core).
Axes of the slice: x: 2, y: 2, z: 4, core: 2. Of those that a mesh axis runs over, the one named last changes fastest.
Arguments:
- potential: float32 [64, 8192], P('group', 'tile'), may hold values from -6 to 6
- species_inputs: bfloat16 [7, 64, 8192], P(None, 'group', 'tile'), may hold values from -6 to 6
- diffusion: float32 [4, 8192], P(None, 'tile'), may hold values from 0.02 to 0.2
- neighbours: int32 [4, 8192], P(None, 'tile'), may hold values from 0 to 1535, as said below
- sunlit_column_index: int32 [4, 8, 256], P('group', 'tile'), may hold values from 0 to 255, each once within a row
- day_count: int32 [4, 8], P('group', 'tile'), may hold values from 0 to 256, as said below
- zenith: bfloat16 [4, 8, 256], P('group', 'tile'), may hold values from 0.099609375 to 1
- lw_first: bfloat16 [8, 64], replicated, may hold values from -2 to 2
- lw_bias: float32 [64], replicated, may hold values from -3 to 3
- lw_second: bfloat16 [64, 64], replicated, may hold values from -0.75 to 0.75
- lw_depth: bfloat16 [64, 256], replicated, may hold values from -0.75 to 0.75
- lw_fraction: bfloat16 [64, 256], replicated, may hold values from -0.75 to 0.75
- sw_first: bfloat16 [8, 64], replicated, may hold values from -2 to 2
- sw_bias: float32 [64], replicated, may hold values from -3 to 3
- sw_second: bfloat16 [64, 64], replicated, may hold values from -0.75 to 0.75
- sw_depth: bfloat16 [64, 224], replicated, may hold values from -0.75 to 0.75
- solar_flux: float32 [224], replicated, may hold values from 0.5 to 2
Outputs:
- evolved: float32 [64, 8192], P('group', 'tile')
Inputs may be any that keep to these rules, and one draw needn't show every extreme that they name: neighbours[k, c] - 256 - (c mod 1024) is a nonzero offset between -256 and 256. `sunlit_column_index`: each list [g, t, :] is a permutation of 0 .. 255. day_count[g, 2 i] + day_count[g, 2 i + 1] = 256 for every g and i.
All inputs are finite; a program needn't handle non-finite values.
Results may differ from a plain program's by a relative error of at most 0.0003.
Values may be sent and summed in bfloat16 or wider, within the bound.
No kernel may reach another device: no remote copies, remote signals or barrier semaphores. Data moves between devices by JAX's collectives and lax.ppermute only.
A program may use at most 128 MiB of HBM per device.

v0:
```python
import jax
import jax.numpy as jnp
from jax import lax
from jax.sharding import PartitionSpec as P

COL_DEV = 256
HW = 256


depth_scale = 0.1
heat_scale = 12.0


def extended(cells, sides, width):
    for axis, dim in sides:
        count = lax.axis_size(axis)
        head = lax.slice_in_dim(cells, 0, width, axis=dim)
        tail = lax.slice_in_dim(cells, cells.shape[dim] - width, cells.shape[dim], axis=dim)
        cells = jnp.concatenate(
            [
                lax.ppermute(tail, axis, [(i, (i + 1) % count) for i in range(count)]),
                cells,
                lax.ppermute(head, axis, [((i + 1) % count, i) for i in range(count)]),
            ],
            axis=dim,
        )
    return cells


def swapped(value, axis, stride):
    return lax.ppermute(value, axis, [(i, i ^ 1 << stride) for i in range(lax.axis_size(axis))])


def tendency(framed, base_at, offsets, weights, lower_at):
    span_cols = offsets.shape[1]
    centre = lower_at - base_at + jnp.arange(span_cols, dtype=jnp.int32)
    middle = lax.slice_in_dim(framed, lower_at - base_at, lower_at - base_at + span_cols, axis=1)
    outcome_state = jnp.zeros_like(middle)
    for branch in range(offsets.shape[0]):
        nearby = jnp.take(framed, centre + offsets[branch], axis=1)
        outcome_state = outcome_state + weights[branch] * (nearby - middle)
    return outcome_state


def hidden_layers(inputs, w_first, bias, w_second):
    flat_in = inputs.reshape(inputs.shape[0], -1)
    layer_one = jax.nn.silu(
        jnp.dot(w_first.T, flat_in, preferred_element_type=jnp.float32) + bias[:, None]
    ).astype(jnp.bfloat16)
    return jax.nn.silu(jnp.dot(w_second.T, layer_one, preferred_element_type=jnp.float32)).astype(
        jnp.bfloat16
    )


def longwave(inputs, weights):
    w_first, bias, w_second, w_depth, w_fraction = weights
    vertical_levels, col_count = (inputs.shape[1], inputs.shape[2])
    hidden = hidden_layers(inputs, w_first, bias, w_second)
    depth = depth_scale * jax.nn.softplus(
        jnp.dot(w_depth.T, hidden, preferred_element_type=jnp.float32)
    ).reshape(-1, vertical_levels, col_count)
    fraction = jax.nn.softplus(
        jnp.dot(w_fraction.T, hidden, preferred_element_type=jnp.float32)
    ).reshape(-1, vertical_levels, col_count)
    above = jnp.cumsum(depth, axis=1) - depth
    planck = jnp.exp(0.25 * inputs[0].astype(jnp.float32))
    emitted = jnp.sum(fraction * (1.0 - jnp.exp(-depth)) * jnp.exp(-above), axis=0)
    return -(heat_scale / depth.shape[0]) * planck * emitted


def shortwave(inputs, cosine, weights):
    w_first, bias, w_second, w_depth, solar_flux = weights
    vertical_levels, col_count = (inputs.shape[1], inputs.shape[2])
    hidden = hidden_layers(inputs, w_first, bias, w_second)
    depth = depth_scale * jax.nn.softplus(
        jnp.dot(w_depth.T, hidden, preferred_element_type=jnp.float32)
    ).reshape(-1, vertical_levels, col_count)
    above = jnp.cumsum(depth, axis=1) - depth
    slant = 1.0 / cosine
    beam = (
        solar_flux[:, None, None]
        * cosine
        * jnp.exp(-above * slant)
        * (1.0 - jnp.exp(-depth * slant))
    )
    return heat_scale / depth.shape[0] * jnp.sum(beam, axis=0)


def blockwise(kernel, inputs, cosine, weights):
    span_cols = inputs.shape[2]
    block_cols = 128

    def one_block(begin_at):
        part_in = lax.dynamic_slice_in_dim(inputs, begin_at, block_cols, 2)
        if cosine is None:
            return kernel(part_in, weights)
        return kernel(part_in, cosine, weights)

    starts = jnp.arange(span_cols // block_cols, dtype=jnp.int32) * block_cols
    stacked = lax.map(one_block, starts)
    return jnp.transpose(stacked, (1, 0, 2)).reshape(stacked.shape[1], span_cols)


def per_device(
    potential,
    species_inputs,
    diffusion,
    neighbours,
    sunlit_column_index,
    day_count,
    zenith,
    lw_first,
    lw_bias,
    lw_second,
    lw_depth,
    lw_fraction,
    sw_first,
    sw_bias,
    sw_second,
    sw_depth,
    solar_flux,
):
    tile_cols = potential.shape[1]
    positions = jnp.arange(tile_cols, dtype=jnp.int32)
    offsets = neighbours - HW - positions[None, :]
    precise = lax.Precision.HIGHEST
    gas_columns = lax.all_to_all(species_inputs, "group", split_axis=2, concat_axis=1, tiled=True)

    def section_update(field):
        framed = extended(field, (("tile", 1),), HW)
        return tendency(framed, 0, offsets, diffusion, HW)

    first = potential + section_update(potential)
    second = 0.75 * potential + 0.25 * (first + section_update(first))
    tertile_portion = potential / 3.0 + 2.0 / 3.0 * (second + section_update(second))
    kinetic_warmth_field = tertile_portion.astype(jnp.bfloat16)[None]
    temp_columns = lax.all_to_all(
        kinetic_warmth_field, "group", split_axis=2, concat_axis=1, tiled=True
    )
    columns = jnp.concatenate([temp_columns, gas_columns], axis=0)
    long_weights = (lw_first, lw_bias, lw_second, lw_depth, lw_fraction)
    short_weights = (sw_first, sw_bias, sw_second, sw_depth, solar_flux)
    zenith_cosine_halves = zenith[0, 0]
    listing = sunlit_column_index[0, 0]
    daylit_count = day_count[0, 0]
    profile_labels = jnp.arange(COL_DEV, dtype=jnp.int32)
    half_column_count = COL_DEV // 2
    slot_ids = jnp.arange(half_column_count, dtype=jnp.int32)
    kept = (
        (listing[:half_column_count][None, :] == profile_labels[:, None])
        & (slot_ids[None, :] < daylit_count)
    ).astype(jnp.bfloat16)
    sent = (
        (listing[half_column_count:][None, :] == profile_labels[:, None])
        & (slot_ids[None, :] + half_column_count < daylit_count)
    ).astype(jnp.bfloat16)
    placed = (slot_ids[None, :] - daylit_count == slot_ids[:, None]).astype(jnp.bfloat16)
    outgoing = jnp.dot(columns, sent, preferred_element_type=jnp.float32).astype(jnp.bfloat16)
    out_cosine = jnp.dot(zenith_cosine_halves, sent, preferred_element_type=jnp.float32).astype(
        jnp.bfloat16
    )
    incoming, in_cosine = swapped((outgoing, out_cosine), "tile", 0)
    work_cols = (
        jnp.dot(columns, kept, preferred_element_type=jnp.float32)
        + jnp.dot(incoming, placed, preferred_element_type=jnp.float32)
    ).astype(jnp.bfloat16)
    work_cosine = jnp.dot(zenith_cosine_halves, kept, preferred_element_type=jnp.float32) + jnp.dot(
        in_cosine, placed, preferred_element_type=jnp.float32
    )
    longwave_heating_rate = blockwise(longwave, columns, None, long_weights)
    work_heat = blockwise(shortwave, work_cols, work_cosine, short_weights)
    back_heat = jnp.dot(work_heat, placed.astype(jnp.float32).T, precision=precise)
    returned = swapped(back_heat, "tile", 0)
    short_heat = jnp.dot(work_heat, kept.astype(jnp.float32).T, precision=precise) + jnp.dot(
        returned, sent.astype(jnp.float32).T, precision=precise
    )
    heating = longwave_heating_rate + short_heat
    slab_heat = lax.all_to_all(heating, "group", split_axis=0, concat_axis=1, tiled=True)
    closing_snapshot = extended(tertile_portion, (("tile", 1),), HW)
    return tertile_portion + tendency(closing_snapshot, 0, offsets, diffusion, HW) + slab_heat


def solution(mesh):
    return jax.shard_map(
        per_device,
        mesh=mesh,
        in_specs=(
            P("group", "tile"),
            P(None, "group", "tile"),
            P(None, "tile"),
            P(None, "tile"),
            P("group", "tile", None),
            P("group", "tile"),
            P("group", "tile", None),
            P(),
            P(),
            P(),
            P(),
            P(),
            P(),
            P(),
            P(),
            P(),
            P(),
        ),
        out_specs=P("group", "tile"),
        check_vma=False,
    )
```

profile of v0, /device:TPU:0, one launch (start us, length us, event | category | flops | bytes accessed | tf_op | source)
XLA Modules:
  0.0 201.5 jit_solution(9993585865450976756)
XLA Ops:
  3.4 3.6 %collective-permute-start.1 = (f32[16,256]{1,0:T(8,128)S(1)}, f32[16,256]{1,0:T(8,128)S(1)}, u32[]{:S(2)}, u32[]{:S(2)}) collective-permute-start(f32[16,256]{1,0:T(8,128)S(1)} %get-tuple-element.108), channel_id=1, source_target_pairs={{1,0},{2,1},{3,2},{4,3},{5,4},{6,5},{7,6},{0,7},{9,8},{10,9},{11,1... | collective-permute-start | bytes 49160 | tf_op jit(solution)/shard_map/ppermute | solution.py:23
  7.9 0.9 fusion.121
  9.6 1.4 collective-permute-done
  12.1 2.8 %gather_fusion.3 = f32[1024,16]{1,0:T(8,128)S(1)} fusion(f32[16,1536]{0,1:T(8,128)S(1)} %copy.206, s32[1024]{0:T(1024)S(1)} %fusion.109), kind=kCustom, calls=%fused_computation.3.clone | custom fusion | bytes 135168 | tf_op jit(solution)/shard_map/jit(_take)/gather | solution.py:40
  15.1 2.8 %gather_fusion.2 = f32[1024,16]{1,0:T(8,128)S(1)} fusion(f32[16,1536]{0,1:T(8,128)S(1)} %copy.206, s32[1024]{0:T(1024)S(1)} %fusion.108), kind=kCustom, calls=%fused_computation.2.clone | custom fusion | bytes 135168 | tf_op jit(solution)/shard_map/jit(_take)/gather | solution.py:40
  18.1 2.8 %gather_fusion.1 = f32[1024,16]{1,0:T(8,128)S(1)} fusion(f32[16,1536]{0,1:T(8,128)S(1)} %copy.206, s32[1024]{0:T(1024)S(1)} %fusion.107), kind=kCustom, calls=%fused_computation.1.clone | custom fusion | bytes 135168 | tf_op jit(solution)/shard_map/jit(_take)/gather | solution.py:40
  21.1 2.8 %gather_fusion = f32[1024,16]{1,0:T(8,128)S(1)} fusion(f32[16,1536]{0,1:T(8,128)S(1)} %copy.206, s32[1024]{0:T(1024)S(1)} %fusion.106), kind=kCustom, calls=%fused_computation.clone | custom fusion | bytes 135168 | tf_op jit(solution)/shard_map/jit(_take)/gather | solution.py:40
  24.1 0.9 fusion.76
  25.0 1.3 collective-permute-start.3
  26.4 2.5 %copy.241 = bf16[7,16,1024]{1,0,2:T(8,128)(2,1)S(1)} copy(bf16[7,16,1024]{2,1,0:T(8,128)(2,1)} %param.22) | data formatting | bytes 458752 | tf_op args[1]
  28.8 2.3 %reshape.281 = bf16[4,2,14336]{2,1,0:T(2,128)(2,1)} reshape(bf16[1024,7,16]{2,1,0:T(8,128)(2,1)S(1)} %bitcast.351) | data formatting | bytes 458752
  31.4 2.8 %gather_fusion.7 = f32[1024,16]{1,0:T(8,128)S(1)} fusion(f32[16,1536]{0,1:T(8,128)S(1)} %copy.214, s32[1024]{0:T(1024)S(1)} %fusion.109), kind=kCustom, calls=%fused_computation.7.clone | custom fusion | bytes 135168 | tf_op jit(solution)/shard_map/jit(_take)/gather | solution.py:40
  34.2 2.8 %gather_fusion.6 = f32[1024,16]{1,0:T(8,128)S(1)} fusion(f32[16,1536]{0,1:T(8,128)S(1)} %copy.214, s32[1024]{0:T(1024)S(1)} %fusion.108), kind=kCustom, calls=%fused_computation.6.clone | custom fusion | bytes 135168 | tf_op jit(solution)/shard_map/jit(_take)/gather | solution.py:40
  37.0 2.8 %gather_fusion.5 = f32[1024,16]{1,0:T(8,128)S(1)} fusion(f32[16,1536]{0,1:T(8,128)S(1)} %copy.214, s32[1024]{0:T(1024)S(1)} %fusion.107), kind=kCustom, calls=%fused_computation.5.clone | custom fusion | bytes 135168 | tf_op jit(solution)/shard_map/jit(_take)/gather | solution.py:40
  39.9 2.8 %gather_fusion.4 = f32[1024,16]{1,0:T(8,128)S(1)} fusion(f32[16,1536]{0,1:T(8,128)S(1)} %copy.214, s32[1024]{0:T(1024)S(1)} %fusion.106), kind=kCustom, calls=%fused_computation.4.clone | custom fusion | bytes 135168 | tf_op jit(solution)/shard_map/jit(_take)/gather | solution.py:40
  43.5 2.7 %collective-permute-start.5 = (f32[16,256]{1,0:T(8,128)S(1)}, f32[16,256]{1,0:T(8,128)S(1)}, u32[]{:S(2)}, u32[]{:S(2)}) collective-permute-start(f32[16,256]{1,0:T(8,128)S(1)} %get-tuple-element.104), channel_id=1, source_target_pairs={{1,0},{2,1},{3,2},{4,3},{5,4},{6,5},{7,6},{0,7},{9,8},{10,9},{11,1... | collective-permute-start | bytes 49160 | tf_op jit(solution)/shard_map/ppermute | solution.py:23
  46.3 1.3 collective-permute-done.5
  47.6 2.6 %collective-permute-done.4 = f32[16,256]{1,0:T(8,128)S(1)} collective-permute-done((f32[16,256]{1,0:T(8,128)S(1)}, f32[16,256]{1,0:T(8,128)S(1)}, u32[]{:S(2)}, u32[]{:S(2)}) %collective-permute-start.4) | collective-permute-done | bytes 16416 | tf_op jit(solution)/shard_map/ppermute | solution.py:21
  50.6 2.8 %gather_fusion.11 = f32[1024,16]{1,0:T(8,128)S(1)} fusion(f32[16,1536]{0,1:T(8,128)S(1)} %copy.222, s32[1024]{0:T(1024)S(1)} %fusion.109), kind=kCustom, calls=%fused_computation.11.clone | custom fusion | bytes 135168 | tf_op jit(solution)/shard_map/jit(_take)/gather | solution.py:40
  53.4 2.8 %gather_fusion.10 = f32[1024,16]{1,0:T(8,128)S(1)} fusion(f32[16,1536]{0,1:T(8,128)S(1)} %copy.222, s32[1024]{0:T(1024)S(1)} %fusion.108), kind=kCustom, calls=%fused_computation.10.clone | custom fusion | bytes 135168 | tf_op jit(solution)/shard_map/jit(_take)/gather | solution.py:40
  56.2 2.8 %gather_fusion.9 = f32[1024,16]{1,0:T(8,128)S(1)} fusion(f32[16,1536]{0,1:T(8,128)S(1)} %copy.222, s32[1024]{0:T(1024)S(1)} %fusion.107), kind=kCustom, calls=%fused_computation.9.clone | custom fusion | bytes 135168 | tf_op jit(solution)/shard_map/jit(_take)/gather | solution.py:40
  59.0 2.8 %gather_fusion.8 = f32[1024,16]{1,0:T(8,128)S(1)} fusion(f32[16,1536]{0,1:T(8,128)S(1)} %copy.222, s32[1024]{0:T(1024)S(1)} %fusion.106), kind=kCustom, calls=%fused_computation.8.clone | custom fusion | bytes 135168 | tf_op jit(solution)/shard_map/jit(_take)/gather | solution.py:40
  63.6 2.3 %reduce.2 = bf16[1024,16]{1,0:T(8,128)(2,1)S(1)} reduce(bf16[1024,1,16]{2,1,0:T(2,128)(2,1)S(1)} %bitcast.352, bf16[]{:T(256)} %broadcast.284), dimensions={1}, to_apply=%bitcast.278.reduce_sub_computation | reduce | bytes 65538
  65.9 0.9 reshape.283
  66.8 4.9 %all-to-all-start = ((bf16[4,2,2048]{2,1,0:T(2,128)(2,1)}), bf16[4,2,2048]{2,1,0:T(2,128)(2,1)S(1)}, u32[]{:S(2)}, u32[]{:S(2)}) async-start(bf16[4,2,2048]{2,1,0:T(2,128)(2,1)} %reshape.283), calls=%async_computation | async-start | bytes 65536 | tf_op jit(solution)/shard_map/all_to_all | solution.py:137
  72.4 4.9 %all-to-all-done = bf16[4,2,2048]{2,1,0:T(2,128)(2,1)S(1)} async-done(((bf16[4,2,2048]{2,1,0:T(2,128)(2,1)}), bf16[4,2,2048]{2,1,0:T(2,128)(2,1)S(1)}, u32[]{:S(2)}, u32[]{:S(2)}) %all-to-all-start) | async-done | bytes 32800 | tf_op jit(solution)/shard_map/all_to_all | solution.py:137
  77.3 3.4 %all-to-all-start.1 = ((bf16[4,2,14336]{2,1,0:T(2,128)(2,1)}), bf16[4,2,14336]{2,1,0:T(2,128)(2,1)S(1)}, u32[]{:S(2)}, u32[]{:S(2)}) async-start(bf16[4,2,14336]{2,1,0:T(2,128)(2,1)} %reshape.281), calls=%async_computation.1 | async-start | bytes 458752 | tf_op jit(solution)/shard_map/all_to_all | solution.py:127
  83.2 4.0 %all-to-all-done.1 = bf16[4,2,14336]{2,1,0:T(2,128)(2,1)S(1)} async-done(((bf16[4,2,14336]{2,1,0:T(2,128)(2,1)}), bf16[4,2,14336]{2,1,0:T(2,128)(2,1)S(1)}, u32[]{:S(2)}, u32[]{:S(2)}) %all-to-all-start.1) | async-done | bytes 229408 | tf_op jit(solution)/shard_map/all_to_all | solution.py:127
  87.2 1.7 reshape.282
  88.9 1.3 copy.242
  90.6 61.4 %while.2 = (s32[]{:T(128)}, f32[2,64,128]{2,1,0:T(8,128)S(1)}, s32[2]{0:T(128)S(1)}, bf16[8,64,256]{2,1,0:T(8,128)(2,1)S(1)}, bf16[8,64]{1,0:T(8,128)(2,1)S(1)},...) while((s32[]{:T(128)}, f32[2,64,128]{2,1,0:T(8,128)S(1)}, ...), condition=%wide.region_3.5_spmd, body=%wide.region_0.4_spmd.sunk | while | flops 792223744 | bytes 45671864 | solution.py:100
  93.2 1.5 multiply_convert_fusion.5
  94.7 8.5 %fusion.164 = f32[256,8192]{1,0:T(8,128)} fusion(bf16[64,8192]{1,0:T(8,128)(2,1)S(1)} %multiply_convert_fusion.5, bf16[64,256]{1,0:T(8,128)(2,1)S(1)} %get-tuple-element.212), kind=kOutput, calls=%fused_computation.26.clone.1 | convolution fusion | flops 283115520 | bytes 9469952 | tf_op jit(solution)/shard_map/while/body/eval_jaxpr/dot_general | solution.py:60
  103.2 7.2 %fusion.165 = f32[256,64,128]{2,0,1:T(8,128)} fusion(f32[256,8192]{1,0:T(8,128)} %fusion.164), kind=kOutput, calls=%fused_computation.30.clone.1 | output fusion | flops 132120576 | bytes 16777216 | tf_op jit(solution)/shard_map/while/body/eval_jaxpr/jit(cumsum)/reduce_window_sum | solution.py:65
  110.5 10.7 %fusion.166 = f32[8192]{0:T(1024)S(1)} fusion(f32[256,8192]{1,0:T(8,128)} %fusion.164, bf16[64,8192]{1,0:T(8,128)(2,1)S(1)} %multiply_convert_fusion.5, bf16[64,256]{1,0:T(8,128)(2,1)S(1)} %get-tuple-element.211, f32[256,64,128]{2,0,1:T(8,128)} %fusion.165), kind=kOutput, calls=%fused_computation.25.clone.1 | convolution fusion | flops 295690240 | bytes 17891328 | tf_op jit(solution)/shard_map/while/body/eval_jaxpr/dot_general | solution.py:63
  123.7 1.5 multiply_convert_fusion.5
  125.2 8.5 %fusion.164 = f32[256,8192]{1,0:T(8,128)} fusion(bf16[64,8192]{1,0:T(8,128)(2,1)S(1)} %multiply_convert_fusion.5, bf16[64,256]{1,0:T(8,128)(2,1)S(1)} %get-tuple-element.212), kind=kOutput, calls=%fused_computation.26.clone.1 | convolution fusion | flops 283115520 | bytes 9469952 | tf_op jit(solution)/shard_map/while/body/eval_jaxpr/dot_general | solution.py:60
  133.7 7.2 %fusion.165 = f32[256,64,128]{2,0,1:T(8,128)} fusion(f32[256,8192]{1,0:T(8,128)} %fusion.164), kind=kOutput, calls=%fused_computation.30.clone.1 | output fusion | flops 132120576 | bytes 16777216 | tf_op jit(solution)/shard_map/while/body/eval_jaxpr/jit(cumsum)/reduce_window_sum | solution.py:65
  141.0 10.7 %fusion.166 = f32[8192]{0:T(1024)S(1)} fusion(f32[256,8192]{1,0:T(8,128)} %fusion.164, bf16[64,8192]{1,0:T(8,128)(2,1)S(1)} %multiply_convert_fusion.5, bf16[64,256]{1,0:T(8,128)(2,1)S(1)} %get-tuple-element.211, f32[256,64,128]{2,0,1:T(8,128)} %fusion.165), kind=kOutput, calls=%fused_computation.25.clone.1 | convolution fusion | flops 295690240 | bytes 17891328 | tf_op jit(solution)/shard_map/while/body/eval_jaxpr/dot_general | solution.py:63
  153.3 8.1 %fusion.17 = f32[224,8192]{1,0:T(8,128)} fusion(bf16[64,224]{1,0:T(8,128)(2,1)S(1)} %copy-done, bf16[64,8192]{1,0:T(8,128)(2,1)S(1)} %multiply_convert_fusion.3, bf16[64,64]{1,0:T(8,128)(2,1)S(1)} %copy-done.45), kind=kOutput, calls=%fused_computation.46 | convolution fusion | flops 317456384 | bytes 8425472 | tf_op jit(solution)/shard_map/while/body/eval_jaxpr/dot_general | solution.py:76
  161.4 6.6 %fusion.23 = f32[224,64,128]{2,0,1:T(8,128)} fusion(f32[224,8192]{1,0:T(8,128)} %fusion.17), kind=kOutput, calls=%fused_computation.54 | output fusion | flops 115605504 | bytes 14680064 | tf_op jit(solution)/shard_map/while/body/eval_jaxpr/jit(cumsum)/reduce_window_sum | solution.py:78
  168.5 2.6 %copy-done.1 = f32[224,8192]{1,0:T(8,128)S(1)} copy-done((f32[224,8192]{1,0:T(8,128)S(1)}, f32[224,8192]{1,0:T(8,128)}, u32[]{:S(2)}) %copy-start.1) | copy-done | bytes 7340056
  171.3 10.5 %fusion.19 = f32[8192]{0:T(1024)S(1)} fusion(f32[28,8,64,128]{3,2,1,0:T(8,128)S(1)} %bitcast.349, f32[224,8192]{1,0:T(8,128)S(1)} %copy-done.1, f32[8192]{0:T(1024)S(1)} %copy-done.6, f32[224,64,128]{2,0,1:T(8,128)} %fusion.23), kind=kLoop, calls=%fused_computation.49 | loop fusion | flops 16506880 | bytes 22085632 | tf_op jit(solution)/shard_map/while/body/eval_jaxpr/reduce_sum | solution.py:86
  184.3 3.3 %all-to-all-start.2 = ((f32[4,16,256]{2,1,0:T(8,128)}), f32[4,16,256]{2,1,0:T(8,128)S(1)}, u32[]{:S(2)}, u32[]{:S(2)}) async-start(f32[4,16,256]{2,1,0:T(8,128)} %bitcast.52), calls=%async_computation.2 | async-start | bytes 131072 | tf_op jit(solution)/shard_map/all_to_all | solution.py:178
  188.7 2.8 %gather_fusion.15 = f32[1024,16]{1,0:T(8,128)S(1)} fusion(f32[16,1536]{0,1:T(8,128)S(1)} %copy.230, s32[1024]{0:T(1024)S(1)} %copy-done.10), kind=kCustom, calls=%fused_computation.15.clone | custom fusion | bytes 135168 | tf_op jit(solution)/shard_map/jit(_take)/gather | solution.py:40
  191.5 2.8 %gather_fusion.14 = f32[1024,16]{1,0:T(8,128)S(1)} fusion(f32[16,1536]{0,1:T(8,128)S(1)} %copy.230, s32[1024]{0:T(1024)S(1)} %copy-done.8), kind=kCustom, calls=%fused_computation.14.clone | custom fusion | bytes 135168 | tf_op jit(solution)/shard_map/jit(_take)/gather | solution.py:40
  194.3 2.8 %gather_fusion.13 = f32[1024,16]{1,0:T(8,128)S(1)} fusion(f32[16,1536]{0,1:T(8,128)S(1)} %copy.230, s32[1024]{0:T(1024)S(1)} %copy-done.12), kind=kCustom, calls=%fused_computation.13.clone | custom fusion | bytes 135168 | tf_op jit(solution)/shard_map/jit(_take)/gather | solution.py:40
  197.2 2.8 %gather_fusion.12 = f32[1024,16]{1,0:T(8,128)S(1)} fusion(f32[16,1536]{0,1:T(8,128)S(1)} %copy.230, s32[1024]{0:T(1024)S(1)} %copy-done.14), kind=kCustom, calls=%fused_computation.12.clone | custom fusion | bytes 135168 | tf_op jit(solution)/shard_map/jit(_take)/gather | solution.py:40
  (188 shorter events, 21.1 us)
Async XLA Ops:
  0.0 153.3 %copy-start = (bf16[64,224]{1,0:T(8,128)(2,1)S(1)}, bf16[64,224]{1,0:T(8,128)(2,1)}, u32[]{:S(2)}) copy-start(bf16[64,224]{1,0:T(8,128)(2,1)} %param.36) | copy-start | bytes 86020
  0.7 89.5 %copy-start.33 = (s32[128]{0:T(128)}, s32[128]{0:T(128)S(1)}, u32[]{:S(2)}) copy-start(s32[128]{0:T(128)S(1)} %get-tuple-element.117) | copy-start | bytes 1540
  1.4 88.8 %copy-start.38 = (pred[128]{0:T(512)(128)(4,1)}, pred[128]{0:T(512)(128)(4,1)S(1)}, u32[]{:S(2)}) copy-start(pred[128]{0:T(512)(128)(4,1)S(1)} %add_compare_fusion) | copy-start | bytes 388
  2.2 43.9 %collective-permute-start.8 = (bf16[128]{0:T(256)(128)(2,1)S(1)}, bf16[128]{0:T(256)(128)(2,1)S(1)}, u32[]{:S(2)}, u32[]{:S(2)}) collective-permute-start(bf16[128]{0:T(256)(128)(2,1)S(1)} %fusion.29), channel_id=1, source_target_pairs={{0,1},{1,0},{2,3},{3,2},{4,5},{5,4},{6,7},{7,6},{8,9},{9,8},{10,11... | collective-permute-start | bytes 776 | tf_op jit(solution)/shard_map/ppermute | solution.py:31
  3.4 6.3 %collective-permute-start.1 = (f32[16,256]{1,0:T(8,128)S(1)}, f32[16,256]{1,0:T(8,128)S(1)}, u32[]{:S(2)}, u32[]{:S(2)}) collective-permute-start(f32[16,256]{1,0:T(8,128)S(1)} %get-tuple-element.108), channel_id=1, source_target_pairs={{1,0},{2,1},{3,2},{4,3},{5,4},{6,5},{7,6},{0,7},{9,8},{10,9},{11,1... | collective-permute-start | bytes 49160 | tf_op jit(solution)/shard_map/ppermute | solution.py:23
  6.9 4.1 %collective-permute-start = (f32[16,256]{1,0:T(8,128)S(1)}, f32[16,256]{1,0:T(8,128)S(1)}, u32[]{:S(2)}, u32[]{:S(2)}) collective-permute-start(f32[16,256]{1,0:T(8,128)S(1)} %get-tuple-element.107), channel_id=1, source_target_pairs={{0,1},{1,2},{2,3},{3,4},{4,5},{5,6},{6,7},{7,0},{8,9},{9,10},{10,1... | collective-permute-start | bytes 49160 | tf_op jit(solution)/shard_map/ppermute | solution.py:21
  7.7 42.8 %copy-start.9 = (s32[1024]{0:T(1024)}, s32[1024]{0:T(1024)S(1)}, u32[]{:S(2)}) copy-start(s32[1024]{0:T(1024)S(1)} %fusion.109) | copy-start | bytes 12292
  7.7 45.6 %copy-start.7 = (s32[1024]{0:T(1024)}, s32[1024]{0:T(1024)S(1)}, u32[]{:S(2)}) copy-start(s32[1024]{0:T(1024)S(1)} %fusion.108) | copy-start | bytes 12292
  7.8 54.8 %copy-start.23 = (pred[1024]{0:T(1024)(128)(4,1)}, pred[1024]{0:T(1024)(128)(4,1)S(1)}, u32[]{:S(2)}) copy-start(pred[1024]{0:T(1024)(128)(4,1)S(1)} %get-tuple-element.121) | copy-start | bytes 3076
  7.8 54.8 %copy-start.25 = (pred[1024]{0:T(1024)(128)(4,1)}, pred[1024]{0:T(1024)(128)(4,1)S(1)}, u32[]{:S(2)}) copy-start(pred[1024]{0:T(1024)(128)(4,1)S(1)} %get-tuple-element.122) | copy-start | bytes 3076
  7.8 48.4 %copy-start.11 = (s32[1024]{0:T(1024)}, s32[1024]{0:T(1024)S(1)}, u32[]{:S(2)}) copy-start(s32[1024]{0:T(1024)S(1)} %fusion.107) | copy-start | bytes 12292
  7.8 51.2 %copy-start.13 = (s32[1024]{0:T(1024)}, s32[1024]{0:T(1024)S(1)}, u32[]{:S(2)}) copy-start(s32[1024]{0:T(1024)S(1)} %fusion.106) | copy-start | bytes 12292
  7.8 54.7 %copy-start.27 = (pred[1024]{0:T(1024)(128)(4,1)}, pred[1024]{0:T(1024)(128)(4,1)S(1)}, u32[]{:S(2)}) copy-start(pred[1024]{0:T(1024)(128)(4,1)S(1)} %get-tuple-element.123) | copy-start | bytes 3076
  7.8 54.7 %copy-start.29 = (pred[1024]{0:T(1024)(128)(4,1)}, pred[1024]{0:T(1024)(128)(4,1)S(1)}, u32[]{:S(2)}) copy-start(pred[1024]{0:T(1024)(128)(4,1)S(1)} %get-tuple-element.124) | copy-start | bytes 3076
  8.8 53.8 %copy-start.15 = (f32[1,1024]{1,0:T(1,128)}, f32[1,1024]{1,0:T(1,128)S(1)}, u32[]{:S(2)}) copy-start(f32[1,1024]{1,0:T(1,128)S(1)} %get-tuple-element.109) | copy-start | bytes 12292
  8.8 53.8 %copy-start.17 = (f32[1,1024]{1,0:T(1,128)}, f32[1,1024]{1,0:T(1,128)S(1)}, u32[]{:S(2)}) copy-start(f32[1,1024]{1,0:T(1,128)S(1)} %get-tuple-element.110) | copy-start | bytes 12292
  8.8 53.8 %copy-start.19 = (f32[1,1024]{1,0:T(1,128)}, f32[1,1024]{1,0:T(1,128)S(1)}, u32[]{:S(2)}) copy-start(f32[1,1024]{1,0:T(1,128)S(1)} %get-tuple-element.111) | copy-start | bytes 12292
  8.8 53.8 %copy-start.21 = (f32[1,1024]{1,0:T(1,128)}, f32[1,1024]{1,0:T(1,128)S(1)}, u32[]{:S(2)}) copy-start(f32[1,1024]{1,0:T(1,128)S(1)} %get-tuple-element.112) | copy-start | bytes 12292
  25.0 6.1 %collective-permute-start.3 = (f32[16,256]{1,0:T(8,128)S(1)}, f32[16,256]{1,0:T(8,128)S(1)}, u32[]{:S(2)}, u32[]{:S(2)}) collective-permute-start(f32[16,256]{1,0:T(8,128)S(1)} %get-tuple-element.106), channel_id=1, source_target_pairs={{1,0},{2,1},{3,2},{4,3},{5,4},{6,5},{7,6},{0,7},{9,8},{10,9},{11,1... | collective-permute-start | bytes 49160 | tf_op jit(solution)/shard_map/ppermute | solution.py:23
  26.3 4.8 %collective-permute-start.2 = (f32[16,256]{1,0:T(8,128)S(1)}, f32[16,256]{1,0:T(8,128)S(1)}, u32[]{:S(2)}, u32[]{:S(2)}) collective-permute-start(f32[16,256]{1,0:T(8,128)S(1)} %get-tuple-element.105), channel_id=1, source_target_pairs={{0,1},{1,2},{2,3},{3,4},{4,5},{5,6},{6,7},{7,0},{8,9},{9,10},{10,1... | collective-permute-start | bytes 49160 | tf_op jit(solution)/shard_map/ppermute | solution.py:21
  26.3 35.7 %copy-start.31 = (s32[128]{0:T(128)}, s32[128]{0:T(128)S(1)}, u32[]{:S(2)}) copy-start(s32[128]{0:T(128)S(1)} %iota_subtract_fusion.1) | copy-start | bytes 1540
  31.1 40.5 %copy-start.37 = (f32[224]{0:T(256)S(1)}, f32[224]{0:T(256)}, u32[]{:S(2)}) copy-start(f32[224]{0:T(256)} %param.37) | copy-start | bytes 2692
  43.5 4.1 %collective-permute-start.5 = (f32[16,256]{1,0:T(8,128)S(1)}, f32[16,256]{1,0:T(8,128)S(1)}, u32[]{:S(2)}, u32[]{:S(2)}) collective-permute-start(f32[16,256]{1,0:T(8,128)S(1)} %get-tuple-element.104), channel_id=1, source_target_pairs={{1,0},{2,1},{3,2},{4,3},{5,4},{6,5},{7,6},{0,7},{9,8},{10,9},{11,1... | collective-permute-start | bytes 49160 | tf_op jit(solution)/shard_map/ppermute | solution.py:23
  46.1 4.1 %collective-permute-start.4 = (f32[16,256]{1,0:T(8,128)S(1)}, f32[16,256]{1,0:T(8,128)S(1)}, u32[]{:S(2)}, u32[]{:S(2)}) collective-permute-start(f32[16,256]{1,0:T(8,128)S(1)} %get-tuple-element.103), channel_id=1, source_target_pairs={{0,1},{1,2},{2,3},{3,4},{4,5},{5,6},{6,7},{7,0},{8,9},{9,10},{10,1... | collective-permute-start | bytes 49160 | tf_op jit(solution)/shard_map/ppermute | solution.py:21
  50.5 40.0 %copy-start.42 = (bf16[64,256]{1,0:T(8,128)(2,1)S(1)}, bf16[64,256]{1,0:T(8,128)(2,1)}, u32[]{:S(2)}) copy-start(bf16[64,256]{1,0:T(8,128)(2,1)} %param.32) | copy-start | bytes 98308
  50.5 40.0 %copy-start.43 = (bf16[64,256]{1,0:T(8,128)(2,1)S(1)}, bf16[64,256]{1,0:T(8,128)(2,1)}, u32[]{:S(2)}) copy-start(bf16[64,256]{1,0:T(8,128)(2,1)} %param.31) | copy-start | bytes 98308
  50.5 40.0 %copy-start.44 = (bf16[64,64]{1,0:T(8,128)(2,1)S(1)}, bf16[64,64]{1,0:T(8,128)(2,1)}, u32[]{:S(2)}) copy-start(bf16[64,64]{1,0:T(8,128)(2,1)} %param.30) | copy-start | bytes 24580
  50.5 40.0 %copy-start.46 = (bf16[8,64]{1,0:T(8,128)(2,1)S(1)}, bf16[8,64]{1,0:T(8,128)(2,1)}, u32[]{:S(2)}) copy-start(bf16[8,64]{1,0:T(8,128)(2,1)} %param.28) | copy-start | bytes 3076
  50.5 40.0 %copy-start.48 = (f32[64]{0:T(128)S(1)}, f32[64]{0:T(128)}, u32[]{:S(2)}) copy-start(f32[64]{0:T(128)} %param.29) | copy-start | bytes 772
  66.8 10.5 %all-to-all-start = ((bf16[4,2,2048]{2,1,0:T(2,128)(2,1)}), bf16[4,2,2048]{2,1,0:T(2,128)(2,1)S(1)}, u32[]{:S(2)}, u32[]{:S(2)}) async-start(bf16[4,2,2048]{2,1,0:T(2,128)(2,1)} %reshape.283), calls=%async_computation | async-start | bytes 65536 | tf_op jit(solution)/shard_map/all_to_all | solution.py:137
  77.3 9.9 %all-to-all-start.1 = ((bf16[4,2,14336]{2,1,0:T(2,128)(2,1)}), bf16[4,2,14336]{2,1,0:T(2,128)(2,1)S(1)}, u32[]{:S(2)}, u32[]{:S(2)}) async-start(bf16[4,2,14336]{2,1,0:T(2,128)(2,1)} %reshape.281), calls=%async_computation.1 | async-start | bytes 458752 | tf_op jit(solution)/shard_map/all_to_all | solution.py:127
  81.9 105.7 %collective-permute-start.7 = (f32[16,256]{1,0:T(8,128)}, f32[16,256]{1,0:T(8,128)}, u32[]{:S(2)}, u32[]{:S(2)}) collective-permute-start(f32[16,256]{1,0:T(8,128)} %get-tuple-element.102), channel_id=1, source_target_pairs={{1,0},{2,1},{3,2},{4,3},{5,4},{6,5},{7,6},{0,7},{9,8},{10,9},{11,1... | collective-permute-start | bytes 49160 | tf_op jit(solution)/shard_map/ppermute | solution.py:23
  81.9 105.7 %collective-permute-start.6 = (f32[16,256]{1,0:T(8,128)}, f32[16,256]{1,0:T(8,128)}, u32[]{:S(2)}, u32[]{:S(2)}) collective-permute-start(f32[16,256]{1,0:T(8,128)} %get-tuple-element.101), channel_id=1, source_target_pairs={{0,1},{1,2},{2,3},{3,4},{4,5},{5,6},{6,7},{7,0},{8,9},{9,10},{10,1... | collective-permute-start | bytes 49160 | tf_op jit(solution)/shard_map/ppermute | solution.py:21
  90.5 61.8 %collective-permute-start.9 = (bf16[8,64,128]{2,1,0:T(8,128)(2,1)S(1)}, bf16[8,64,128]{2,1,0:T(8,128)(2,1)S(1)}, u32[]{:S(2)}, u32[]{:S(2)}) collective-permute-start(bf16[8,64,128]{2,1,0:T(8,128)(2,1)S(1)} %convolution_convert_fusion), channel_id=1, source_target_pairs={{0,1},{1,0},{2,3},{3,2},{4,5},{5,4},{6,7},{7,6},{8,9},{9,8},{10,11... | collective-permute-start | bytes 393224 | tf_op jit(solution)/shard_map/ppermute | solution.py:31
  90.6 61.4 %copy-start.36 = (s32[128]{0:T(128)S(1)}, s32[128]{0:T(128)}, u32[]{:S(2)}) copy-start(s32[128]{0:T(128)} %copy-done.35) | copy-start | bytes 1540
  90.6 61.4 %copy-start.41 = (pred[128]{0:T(512)(128)(4,1)S(1)}, pred[128]{0:T(512)(128)(4,1)}, u32[]{:S(2)}) copy-start(pred[128]{0:T(512)(128)(4,1)} %copy-done.40) | copy-start | bytes 388
  90.6 61.7 %copy-start.32 = (s32[128]{0:T(128)S(1)}, s32[128]{0:T(128)}, u32[]{:S(2)}) copy-start(s32[128]{0:T(128)} %copy-done.31) | copy-start | bytes 1540
  90.6 61.9 %copy-start.47 = (bf16[8,64]{1,0:T(8,128)(2,1)S(1)}, bf16[8,64]{1,0:T(8,128)(2,1)}, u32[]{:S(2)}) copy-start(bf16[8,64]{1,0:T(8,128)(2,1)} %param.33) | copy-start | bytes 3076
  90.6 61.9 %copy-start.49 = (f32[64]{0:T(128)S(1)}, f32[64]{0:T(128)}, u32[]{:S(2)}) copy-start(f32[64]{0:T(128)} %param.34) | copy-start | bytes 772
  171.2 29.5 %copy-start.16 = (f32[1,1024]{1,0:T(1,128)S(1)}, f32[1,1024]{1,0:T(1,128)}, u32[]{:S(2)}) copy-start(f32[1,1024]{1,0:T(1,128)} %copy-done.15) | copy-start | bytes 12292
  171.2 29.5 %copy-start.18 = (f32[1,1024]{1,0:T(1,128)S(1)}, f32[1,1024]{1,0:T(1,128)}, u32[]{:S(2)}) copy-start(f32[1,1024]{1,0:T(1,128)} %copy-done.17) | copy-start | bytes 12292
  171.2 29.5 %copy-start.20 = (f32[1,1024]{1,0:T(1,128)S(1)}, f32[1,1024]{1,0:T(1,128)}, u32[]{:S(2)}) copy-start(f32[1,1024]{1,0:T(1,128)} %copy-done.19) | copy-start | bytes 12292
  171.2 29.5 %copy-start.22 = (f32[1,1024]{1,0:T(1,128)S(1)}, f32[1,1024]{1,0:T(1,128)}, u32[]{:S(2)}) copy-start(f32[1,1024]{1,0:T(1,128)} %copy-done.21) | copy-start | bytes 12292
  171.2 29.5 %copy-start.24 = (pred[1024]{0:T(1024)(128)(4,1)S(1)}, pred[1024]{0:T(1024)(128)(4,1)}, u32[]{:S(2)}) copy-start(pred[1024]{0:T(1024)(128)(4,1)} %copy-done.23) | copy-start | bytes 3076
  171.2 29.5 %copy-start.26 = (pred[1024]{0:T(1024)(128)(4,1)S(1)}, pred[1024]{0:T(1024)(128)(4,1)}, u32[]{:S(2)}) copy-start(pred[1024]{0:T(1024)(128)(4,1)} %copy-done.25) | copy-start | bytes 3076
  171.2 29.5 %copy-start.28 = (pred[1024]{0:T(1024)(128)(4,1)S(1)}, pred[1024]{0:T(1024)(128)(4,1)}, u32[]{:S(2)}) copy-start(pred[1024]{0:T(1024)(128)(4,1)} %copy-done.27) | copy-start | bytes 3076
  182.0 1.4 collective-permute-start.10
  184.3 16.4 %all-to-all-start.2 = ((f32[4,16,256]{2,1,0:T(8,128)}), f32[4,16,256]{2,1,0:T(8,128)S(1)}, u32[]{:S(2)}, u32[]{:S(2)}) async-start(f32[4,16,256]{2,1,0:T(8,128)} %bitcast.52), calls=%async_computation.2 | async-start | bytes 131072 | tf_op jit(solution)/shard_map/all_to_all | solution.py:178
  (16 other events, 267.0 us)
where the time goes:
time: 202 us; the launch traced here: 201 us
  local copies, waits for them, and re-layouts  67.3 us (33%)
  matrix products  54 us (27%)
  other arithmetic  39 us (19%)
  starting transfers between devices  20.8 us (10%)
  waiting for transfers between devices  14.8 us (7%)
  loops' own time  3.85 us (2%)
    gather x32, local copies, waits for them, and re-layouts, tendency(): nearby = jnp.take(framed, centre + offsets[branch], axis=1)  47.7 us
    dot_general x2, matrix products, longwave(): jnp.dot(w_fraction.T, hidden, preferred_element_type=jnp.float32)  21.4 us
    dot_general x2, matrix products, longwave(): jnp.dot(w_depth.T, hidden, preferred_element_type=jnp.float32)  17 us
    another operation x2, other arithmetic, longwave(): above = jnp.cumsum(depth, axis=1) - depth  14.5 us
    unnamed x106, local copies, waits for them, and re-layouts  11.1 us
    reduce_sum x1, other arithmetic, shortwave(): return heat_scale / depth.shape[0] * jnp.sum(beam, axis=0)  10.5 us
    dot_general x1, matrix products, shortwave(): jnp.dot(w_depth.T, hidden, preferred_element_type=jnp.float32)  8.1 us
    ppermute x4, starting transfers between devices, extended(): lax.ppermute(head, axis, [((i + 1) % count, i) for i in range(count)])  7.57 us
  transfers between devices with their start and end apart: 14, of which 6 were waited for; matrix products, arithmetic and copies ran while one was open for 69% of the time, Pallas kernels for 0%

commit v1 on v0

v1 whole, which is shorter than its diff:
```python
import functools
import math

import jax
import jax.numpy as jnp
from jax import lax
from jax.experimental import pallas as pl
from jax.experimental.pallas import tpu as pltpu
from jax.sharding import PartitionSpec as P

HW = 256
LANES = 128
SUBS = 8
STEP_LEVELS = SUBS // 2

depth_scale = 0.1
heat_scale = 12.0
LOG2E = 1.4426950408889634

F32 = jnp.float32
BF16 = jnp.bfloat16
VMEM = pl.BlockSpec(memory_space=pltpu.VMEM)
SMEM = pl.BlockSpec(memory_space=pltpu.SMEM)
PARAMS = pltpu.CompilerParams(vmem_limit_bytes=48 * 1024 * 1024)


def call(body, outs, ins, scratch=(), flops=0, trans=0, specs=None):
    return pl.pallas_call(
        body,
        out_shape=outs,
        in_specs=specs or [SMEM if a.size == 1 else VMEM for a in ins],
        out_specs=[VMEM for _ in outs],
        scratch_shapes=list(scratch),
        compiler_params=PARAMS,
        cost_estimate=pl.CostEstimate(
            flops=flops,
            transcendentals=trans,
            bytes_accessed=sum(a.size * a.dtype.itemsize for a in list(ins) + list(outs)),
        ),
    )(*ins)


def shaped(shape, dtype):
    return jax.ShapeDtypeStruct(shape, dtype)


def iota(shape, dim):
    return lax.broadcasted_iota(jnp.int32, shape, dim)


def mm(a, b):
    return jnp.dot(a, b, preferred_element_type=F32)


def lane_take(x, idx):
    return jnp.take_along_axis(x, idx, axis=1, mode="promise_in_bounds")


def diffused(src, src_at, table, weight, within, at):
    reach = HW // LANES
    wide = 2 * reach + 1
    rows = src.shape[0]
    groups = range(0, rows, SUBS)
    base = at - src_at
    middle = [src[r : r + SUBS, base : base + LANES] for r in groups]
    total = [jnp.zeros_like(m) for m in middle]
    for k in range(table.shape[0]):
        place = jnp.broadcast_to(table[k : k + 1, within : within + LANES], (SUBS, LANES)) - within
        lane = place & (LANES - 1)
        which = place >> (LANES.bit_length() - 1)
        factor = jnp.broadcast_to(weight[k : k + 1, within : within + LANES], (SUBS, LANES))
        tests = [which == w for w in range(1, wide)]
        for n, r in enumerate(groups):
            near = None
            for w in range(wide):
                lo = base + (w - reach) * LANES
                got = lane_take(src[r : r + SUBS, lo : lo + LANES], lane)
                near = got if w == 0 else jnp.where(tests[w - 1], got, near)
            total[n] = total[n] + factor * (near - middle[n])
    return [(r, m, m + t) for r, m, t in zip(groups, middle, total)]


def sections_body(
    n_group, me, left, own, right, nl, n0, nr, dl, d0, dr, third_out, *rest
):
    pieces, (frame, first, second) = rest[:n_group], rest[n_group:]
    tile = own.shape[1]
    cols = tile // n_group
    frame[:, 0:tile] = left[...]
    frame[:, tile : 2 * tile] = own[...]
    frame[:, 2 * tile :] = right[...]
    tables, weights = (nl, n0, nr), (dl, d0, dr)

    def run(src, src_at, halo, put):
        for at in range(tile - halo, 2 * tile + halo, LANES):
            t = at // tile
            for r, _, value in diffused(src, src_at, tables[t], weights[t], at - t * tile, at):
                put(r, at, value)

    def put_first(r, at, value):
        first[r : r + SUBS, at : at + LANES] = value

    def put_second(r, at, value):
        start = frame[r : r + SUBS, at : at + LANES]
        second[r : r + SUBS, at : at + LANES] = 0.75 * start + 0.25 * value

    def put_third(r, at, value):
        start = frame[r : r + SUBS, at : at + LANES]
        lo = at - tile + HW
        third_out[r : r + SUBS, lo : lo + LANES] = start / 3.0 + (2.0 / 3.0) * value

    run(frame, 0, 3 * HW, put_first)
    run(first, 0, 2 * HW, put_second)
    run(second, 0, HW, put_third)
    mine = me[0]
    for s in range(n_group):
        goal = lax.rem(mine + s, n_group)
        lo = pl.multiple_of(HW + goal * cols, LANES)
        pieces[s][...] = third_out[:, pl.ds(lo, cols)].astype(BF16)


def closing_body(third, table, weight, out):
    tile = out.shape[1]
    for at in range(0, tile, LANES):
        for r, _, value in diffused(third, -HW, table, weight, at, at):
            out[r : r + SUBS, at : at + LANES] = value


def gas_cut_body(n_group, me, species, *outs):
    cols = outs[0].shape[2]
    for s in range(1, n_group):
        goal = lax.rem(me[0] + s, n_group)
        outs[s - 1][...] = species[:, :, pl.ds(pl.multiple_of(goal * cols, LANES), cols)]


def one_hots(listing, count):
    cols = listing.shape[-1]
    half = cols // 2
    label = iota((cols, half), 0)
    slot = iota((cols, half), 1)
    first = jnp.broadcast_to(listing[0, :, 0:half], (cols, half))
    last = jnp.broadcast_to(listing[0, :, half:cols], (cols, half))
    kept = jnp.where((first == label) & (slot < count), 1.0, 0.0)
    sent = jnp.where((last == label) & (slot + half < count), 1.0, 0.0)
    return first == label, last == label, kept.astype(BF16), sent.astype(BF16)


def gas_join_body(
    n_group, me, count, species, *rest
):
    arrived, rest = rest[: n_group - 1], rest[n_group - 1 :]
    listing, zenith, packed, outgoing, kept_x, kept_cos, slot_of, spread = rest
    gases, slab, _ = species.shape
    cols = packed.shape[2]
    half = cols // 2
    spread[...] = jnp.zeros_like(spread)
    for s in range(n_group):
        source = lax.rem(me[0] + n_group - s, n_group)
        for lo in range(0, cols, LANES):
            for f in range(gases):
                if s == 0:
                    at = pl.multiple_of(me[0] * cols + lo, LANES)
                    value = species[f, :, pl.ds(at, LANES)]
                else:
                    value = arrived[s - 1][f, :, lo : lo + LANES]
                spread[(f + 1) * slab : (f + 2) * slab, :] = value.astype(F32)
            for l in range(slab):
                packed[source * slab + l, :, lo : lo + LANES] = spread[pl.ds(l, SUBS, stride=slab), :]
    hit_first, hit_last, kept, sent = one_hots(listing, count[0, 0])
    levels = packed.shape[0]
    flat = packed[...].reshape(levels * SUBS, cols).astype(BF16)
    outgoing[0 : levels * SUBS, :] = mm(flat, sent).astype(BF16)
    kept_x[...] = mm(flat, kept)
    cosine = jnp.broadcast_to(zenith[0].astype(F32), (2 * SUBS, cols)).astype(BF16)
    outgoing[levels * SUBS :, :] = mm(cosine, sent).astype(BF16)
    kept_cos[...] = mm(cosine, kept)[0:SUBS]
    hits = jnp.concatenate([hit_first, hit_last], axis=1)
    hits = jnp.where(hits, 1.0, 0.0).astype(BF16)
    numbers = iota((2 * SUBS, cols), 1).astype(F32).astype(BF16)
    found = lax.dot_general(
        numbers, hits, (((1,), (1,)), ((), ())), preferred_element_type=F32
    )
    slot_of[...] = found[0:SUBS].astype(jnp.int32)


def warm_join_body(n_group, me, count, *rest):
    pieces, (listing, warm, outgoing, kept_warm) = rest[:n_group], rest[n_group:]
    slab = pieces[0].shape[0]
    for s in range(n_group):
        source = lax.rem(me[0] + n_group - s, n_group)
        lo = pl.multiple_of(source * slab, SUBS)
        warm[pl.ds(lo, slab), :] = pieces[s][...].astype(F32)
    _, _, kept, sent = one_hots(listing, count[0, 0])
    flat = warm[...].astype(BF16)
    outgoing[...] = mm(flat, sent).astype(BF16)
    kept_warm[...] = mm(flat, kept)


def softplus(z):
    return jnp.maximum(z, jnp.log(1.0 + jnp.exp(jnp.minimum(z, 80.0))))


def sweep(x_at, warm_at, first, bias, second, heads, gpts, rate, both, buffers, levels):
    hid_a, hid_b, z_a, z_b, trans, parts = buffers
    steps = levels // STEP_LEVELS
    top = iota((SUBS, LANES), 0) == 0

    def hidden(pair, odd, out):
        pair = jnp.minimum(pair, steps // 2 - 1)
        warm = warm_at(pl.multiple_of(pair * SUBS, SUBS))
        tiles = []
        for i in range(odd * STEP_LEVELS, (odd + 1) * STEP_LEVELS):
            row = jnp.broadcast_to(warm[i : i + 1], (SUBS, LANES))
            tiles.append(jnp.where(top, row, x_at(pair * SUBS + i)))
        x = jnp.concatenate(tiles, axis=1).astype(BF16)
        v = mm(first[...], x) + bias[...]
        one = (v + v * jnp.tanh(v)).astype(BF16)
        v = mm(second[...], one)
        out[...] = (v + v * jnp.tanh(v)).astype(BF16)

    def optics(hid, out):
        out[...] = mm(heads[...], hid[...])

    def consume(t, z):
        total = [None] * STEP_LEVELS
        for lo in range(0, gpts, SUBS):
            carry = trans[lo : lo + SUBS, :]
            for i in range(STEP_LEVELS):
                at = i * LANES
                depth = softplus(z[lo : lo + SUBS, at : at + LANES])
                following = carry * jnp.exp2(depth * rate)
                drop = carry - following
                if both:
                    drop = drop * softplus(z[gpts + lo : gpts + lo + SUBS, at : at + LANES])
                total[i] = drop if total[i] is None else total[i] + drop
                carry = following
            trans[lo : lo + SUBS, :] = carry
        for i in range(STEP_LEVELS):
            at = pl.multiple_of((t * STEP_LEVELS + i) * SUBS, SUBS)
            parts[pl.ds(at, SUBS), :] = total[i]

    hidden(0, 0, hid_a)
    optics(hid_a, z_a)
    hidden(0, 1, hid_b)

    def two(i, _):
        t = 2 * i
        consume(t, z_a)
        optics(hid_b, z_b)
        hidden(i + 1, 0, hid_a)
        consume(t + 1, z_b)
        optics(hid_a, z_a)
        hidden(i + 1, 1, hid_b)
        return 0

    lax.fori_loop(0, steps // 2, two, 0)
    emitted = parts[pl.ds(0, levels, stride=SUBS), :]
    for s in range(1, SUBS):
        emitted = emitted + parts[pl.ds(s, levels, stride=SUBS), :]
    return emitted


def sweep_scratch(hid, rows, gpts, levels):
    wide = STEP_LEVELS * LANES
    return [
        pltpu.VMEM((hid, wide), BF16),
        pltpu.VMEM((hid, wide), BF16),
        pltpu.VMEM((rows, wide), F32),
        pltpu.VMEM((rows, wide), F32),
        pltpu.VMEM((gpts, LANES), F32),
        pltpu.VMEM((levels * SUBS, LANES), F32),
    ]


def longwave_part(lo, packed, warm, first, bias, second, heads, buffers):
    gpts = heads.shape[0] // 2
    levels = packed.shape[0]
    buffers[4][...] = jnp.ones_like(buffers[4])
    emitted = sweep(
        lambda l: packed[l, :, lo : lo + LANES],
        lambda l: warm[pl.ds(l, SUBS), lo : lo + LANES],
        first, bias, second, heads, gpts, -depth_scale * LOG2E, True, buffers, levels,
    )
    planck = jnp.exp(0.25 * warm[:, lo : lo + LANES])
    return -(heat_scale / gpts) * planck * emitted


def longwave_body(packed, warm, first, bias, second, heads, out, *buffers):
    out[...] = longwave_part(0, packed, warm, first, bias, second, heads, buffers)


def shortwave_body(
    count, kept_x, kept_warm, kept_cos, in_x, in_warm, first, bias, second, heads, flux, out,
    work_x, work_warm, *buffers
):
    levels = kept_warm.shape[0]
    half = kept_warm.shape[1]
    gpts = heads.shape[0]
    slot = iota((half, half), 1) - count[0, 0]
    placed = jnp.where(slot == iota((half, half), 0), 1.0, 0.0).astype(BF16)
    cells = levels * SUBS
    work_x[...] = kept_x[...] + mm(in_x[0:cells, :], placed)
    work_warm[...] = kept_warm[...] + mm(in_warm[...], placed)
    cosine = kept_cos[...] + mm(in_x[cells:, :], placed)[0:SUBS]
    cosine = jnp.where(cosine > 0.0, cosine, 1.0)
    buffers[4][...] = jnp.broadcast_to(flux[...], buffers[4].shape)
    emitted = sweep(
        lambda l: work_x[pl.ds(pl.multiple_of(l * SUBS, SUBS), SUBS), :],
        lambda l: work_warm[pl.ds(l, SUBS), :],
        first, bias, second, heads, gpts, (-depth_scale * LOG2E) / cosine, False, buffers, levels,
    )
    out[...] = (heat_scale / gpts) * cosine[0:1] * emitted


def finish_body(
    n_group, me, count, packed, warm, first, bias, second, heads, long_first, work, partner, slot_of,
    *rest
):
    pieces, heat, buffers = rest[:n_group], rest[n_group], rest[n_group + 1 :]
    levels, cols = heat.shape
    half = cols // 2
    slab = pieces[0].shape[0]
    sunlit = count[0, 0]
    long_last = longwave_part(half, packed, warm, first, bias, second, heads, buffers)
    for lo, long in ((0, long_first[...]), (half, long_last)):
        slot = slot_of[:, lo : lo + half]
        here = slot < half
        place = jnp.where(here, slot, slot + half - sunlit) & (half - 1)
        lit = slot < sunlit
        for r in range(0, levels, SUBS):
            near = lane_take(work[r : r + SUBS, :], place)
            far = lane_take(partner[r : r + SUBS, :], place)
            short = jnp.where(lit, jnp.where(here, near, far), 0.0)
            heat[r : r + SUBS, lo : lo + half] = long[r : r + SUBS] + short
    for s in range(n_group):
        goal = lax.rem(me[0] + s, n_group)
        pieces[s][...] = heat[pl.ds(pl.multiple_of(goal * slab, SUBS), slab), :]


def add_body(n_group, me, closed, *rest):
    pieces, out = rest[:n_group], rest[n_group]
    cols = pieces[0].shape[1]
    for s in range(n_group):
        source = lax.rem(me[0] + n_group - s, n_group)
        at = pl.ds(pl.multiple_of(source * cols, LANES), cols)
        out[:, at] = closed[:, at] + pieces[s][...]


def per_device(
    potential, species, diffusion, neighbours, listing, day_count, zenith,
    lw_first, lw_bias, lw_second, lw_depth, lw_fraction,
    sw_first, sw_bias, sw_second, sw_depth, solar_flux,
):
    n_group = lax.axis_size("group")
    n_tile = lax.axis_size("tile")
    me = lax.axis_index("group").astype(jnp.int32).reshape(1)
    slab, tile = potential.shape
    gases = species.shape[0]
    cols = tile // n_group
    half = cols // 2
    levels = slab * n_group

    def turned(value, by):
        return lax.ppermute(value, "tile", [(i, (i + by) % n_tile) for i in range(n_tile)])

    def along(value, by):
        return lax.ppermute(value, "group", [(i, (i + by) % n_group) for i in range(n_group)])

    def paired(value):
        return lax.ppermute(value, "tile", [(i, i ^ 1) for i in range(n_tile)])

    framing = (potential, neighbours, diffusion)
    left = [turned(a, 1) for a in framing]
    right = [turned(a, -1) for a in framing]

    cuts = call(
        functools.partial(gas_cut_body, n_group),
        [shaped((gases, slab, cols), BF16)] * (n_group - 1),
        [me, species],
    )
    arrived = [along(c, s + 1) for s, c in enumerate(cuts)]

    lw_one = (0.5 * lw_first).T
    lw_two = (0.5 * lw_second).T
    lw_heads = jnp.concatenate([lw_depth, lw_fraction], axis=1).T
    lw_shift = (0.5 * lw_bias)[:, None]
    sw_one = (0.5 * sw_first).T
    sw_two = (0.5 * sw_second).T
    sw_heads = sw_depth.T
    sw_shift = (0.5 * sw_bias)[:, None]
    flux = solar_flux[:, None]
    hid = lw_first.shape[1]
    long_weights = [lw_one, lw_shift, lw_two, lw_heads]
    short_weights = [sw_one, sw_shift, sw_two, sw_heads, flux]

    third, *warm_cuts = call(
        functools.partial(sections_body, n_group),
        [shaped((slab, tile + 2 * HW), F32)] + [shaped((slab, cols), BF16)] * n_group,
        [me, left[0], potential, right[0], left[1], neighbours, right[1], left[2], diffusion, right[2]],
        [pltpu.VMEM((slab, 3 * tile), F32)] * 3,
        flops=10_000_000,
    )
    warm_pieces = [warm_cuts[0]] + [along(c, s + 1) for s, c in enumerate(warm_cuts[1:])]

    packed, out_x, kept_x, kept_cos, slot_of = call(
        functools.partial(gas_join_body, n_group),
        [
            shaped((levels, SUBS, cols), F32),
            shaped((levels * SUBS + 2 * SUBS, half), BF16),
            shaped((levels * SUBS, half), F32),
            shaped((SUBS, half), F32),
            shaped((SUBS, cols), jnp.int32),
        ],
        [me, day_count, species, *arrived, listing, zenith],
        [pltpu.VMEM((SUBS * slab, LANES), F32)],
    )
    in_x = paired(out_x)

    (closed,) = call(
        closing_body, [shaped((slab, tile), F32)], [third, neighbours, diffusion], flops=2_000_000
    )

    warm, out_warm, kept_warm = call(
        functools.partial(warm_join_body, n_group),
        [
            shaped((levels, cols), F32),
            shaped((levels, half), BF16),
            shaped((levels, half), F32),
        ],
        [me, day_count, *warm_pieces, listing],
    )
    in_warm = paired(out_warm)

    lw_rows = lw_heads.shape[0]
    lw_scratch = sweep_scratch(hid, lw_rows, lw_rows // 2, levels)
    lw_cells = levels * half
    (long_first,) = call(
        longwave_body,
        [shaped((levels, half), F32)],
        [packed, warm, *long_weights],
        lw_scratch,
        flops=2 * lw_cells * hid * lw_rows,
        trans=5 * lw_cells * lw_rows // 2,
    )
    sw_rows = sw_heads.shape[0]
    (work,) = call(
        shortwave_body,
        [shaped((levels, half), F32)],
        [day_count, kept_x, kept_warm, kept_cos, in_x, in_warm, *short_weights],
        [pltpu.VMEM((levels * SUBS, half), F32), pltpu.VMEM((levels, half), F32)]
        + sweep_scratch(hid, sw_rows, sw_rows, levels),
        flops=2 * lw_cells * hid * sw_rows,
        trans=3 * lw_cells * sw_rows,
    )
    partner = paired(work)
    heat_cuts = call(
        functools.partial(finish_body, n_group),
        [shaped((slab, cols), F32)] * n_group,
        [me, day_count, packed, warm, *long_weights, long_first, work, partner, slot_of],
        [pltpu.VMEM((levels, cols), F32)] + lw_scratch,
        flops=2 * lw_cells * hid * lw_rows,
        trans=5 * lw_cells * lw_rows // 2,
    )
    heat_pieces = [heat_cuts[0]] + [along(c, s + 1) for s, c in enumerate(heat_cuts[1:])]
    (evolved,) = call(
        functools.partial(add_body, n_group),
        [shaped((slab, tile), F32)],
        [me, closed, *heat_pieces],
    )
    return evolved


def solution(mesh):
    return jax.shard_map(
        per_device,
        mesh=mesh,
        in_specs=(
            P("group", "tile"),
            P(None, "group", "tile"),
            P(None, "tile"),
            P(None, "tile"),
            P("group", "tile", None),
            P("group", "tile"),
            P("group", "tile", None),
            *([P()] * 10),
        ),
        out_specs=P("group", "tile"),
        check_vma=False,
    )
```

time: 202 us -> 66.8 us (0.33)
  local copies, waits for them, and re-layouts: 67.3 us -> 5.21 us
  matrix products: 54 us -> 0 us
  other arithmetic: 39 us -> 0.05 us
  Pallas kernels: 0 us -> 33.2 us
  waiting for transfers between devices: 14.8 us -> 6.44 us
  loops' own time: 3.85 us -> 0 us
    dot_general x17 -> x0, matrix products: 54 us -> none  [the longest x2 21.4 us: longwave(): jnp.dot(w_fraction.T, hidden, preferred_element_type=jnp.float32)]
    gather x32 -> x0, local copies, waits for them, and re-layouts: 47.7 us -> none  [tendency(): nearby = jnp.take(framed, centre + offsets[branch], axis=1)]
    pallas_call x0 -> x9, Pallas kernels: none -> 33.2 us  [call(): pl.pallas_call(body, out_shape=outs, in_specs=specs or [SMEM if a.size ==...]
    another operation x3 -> x0, other arithmetic: 21.1 us -> none  [the longest x2 14.5 us: longwave(): above = jnp.cumsum(depth, axis=1) - depth]
    all_to_all x3 -> x0, starting transfers between devices: 11.6 us -> none  [the longest x1 4.87 us: per_device(): lax.all_to_all(kinetic_warmth_field, 'group', split_axis=2, concat_axis=1...]
    ppermute x11 -> x18, starting transfers between devices: 9.14 us -> 20.5 us  [the longest x9 12.6 us: along(): lax.ppermute(value, 'group', [(i, (i + by) % n_group) for i in range(n_gr...]
    reduce_sum x1 -> x0, other arithmetic: 10.5 us -> none  [shortwave(): return heat_scale / depth.shape[0] * jnp.sum(beam, axis=0)]
    all_to_all x3 -> x0, waiting for transfers between devices: 8.88 us -> none  [the longest x1 4.92 us: per_device(): lax.all_to_all(kinetic_warmth_field, 'group', split_axis=2, concat_axis=1...]
  transfers between devices with their start and end apart: 14 -> 18, of which waited for: 6 -> 6; matrix products, arithmetic and copies ran while one was open for 69% -> 3% of each run, Pallas kernels for 0% -> 21%
where the time goes in v1:
time: 66.8 us; the launch traced here: 66.4 us
  Pallas kernels  33.2 us (50%)
  starting transfers between devices  20.5 us (31%)
  waiting for transfers between devices  6.44 us (10%)
  local copies, waits for them, and re-layouts  5.21 us (8%)
  between operations  0.95 us (1%)
    pallas_call x9, Pallas kernels, call(): pl.pallas_call(body, out_shape=outs, in_specs=specs or [SMEM if a.size ==...  33.2 us
    ppermute x9, starting transfers between devices, along(): lax.ppermute(value, 'group', [(i, (i + by) % n_group) for i in range(n_gr...  12.6 us
    ppermute x6, starting transfers between devices, turned(): lax.ppermute(value, 'tile', [(i, (i + by) % n_tile) for i in range(n_tile)])  7.29 us
    ppermute x9, waiting for transfers between devices, along(): lax.ppermute(value, 'group', [(i, (i + by) % n_group) for i in range(n_gr...  6.32 us
    unnamed x37, local copies, waits for them, and re-layouts  4.69 us
  transfers between devices with their start and end apart: 18, of which 6 were waited for; matrix products, arithmetic and copies ran while one was open for 3% of the time, Pallas kernels for 21%

profile of v1, /device:TPU:0, one launch (start us, length us, event | category | flops | bytes accessed | tf_op | source)
XLA Modules:
  0.0 66.4 jit_solution(18012946077278837182)
XLA Ops:
  0.0 0.5 collective-permute-start
  0.5 2.6 %collective-permute-start.2 = (s32[4,1024]{1,0:T(4,128)}, s32[4,1024]{1,0:T(4,128)S(1)}, u32[]{:S(2)}, u32[]{:S(2)}) collective-permute-start(s32[4,1024]{1,0:T(4,128)} %table.1), channel_id=1, source_target_pairs={{0,1},{1,2},{2,3},{3,4},{4,5},{5,6},{6,7},{7,0},{8,9},{9,10},{10,1... | collective-permute-start | bytes 49160 | tf_op jit(solution)/shard_map/ppermute | solution.py:364
  3.1 0.9 %copy-done = bf16[7,16,1024]{2,1,0:T(8,128)(2,1)S(1)} copy-done((bf16[7,16,1024]{2,1,0:T(8,128)(2,1)S(1)}, bf16[7,16,1024]{2,1,0:T(8,128)(2,1)}, u32[]{:S(2)}) %copy-start) | copy-done | bytes 229400
  4.0 1.6 %collective-permute-start.6 = (bf16[7,16,256]{2,1,0:T(8,128)(2,1)S(1)}, bf16[7,16,256]{2,1,0:T(8,128)(2,1)S(1)}, u32[]{:S(2)}, u32[]{:S(2)}) collective-permute-start(bf16[7,16,256]{2,1,0:T(8,128)(2,1)S(1)} %get-tuple-element.26), channel_id=1, source_target_pairs={{0,8},{8,16},{16,24},{24,0},{1,9},{9,17},{17,25},{25,1},{2,10},{10... | collective-permute-start | bytes 172040 | tf_op jit(solution)/shard_map/ppermute | solution.py:367
  5.7 2.6 %collective-permute-start.7 = (bf16[7,16,256]{2,1,0:T(8,128)(2,1)S(1)}, bf16[7,16,256]{2,1,0:T(8,128)(2,1)S(1)}, u32[]{:S(2)}, u32[]{:S(2)}) collective-permute-start(bf16[7,16,256]{2,1,0:T(8,128)(2,1)S(1)} %get-tuple-element.27), channel_id=1, source_target_pairs={{0,16},{8,24},{16,0},{24,8},{1,17},{9,25},{17,1},{25,9},{2,18},{10... | collective-permute-start | bytes 172040 | tf_op jit(solution)/shard_map/ppermute | solution.py:367
  8.2 1.3 %collective-permute-start.8 = (bf16[7,16,256]{2,1,0:T(8,128)(2,1)S(1)}, bf16[7,16,256]{2,1,0:T(8,128)(2,1)S(1)}, u32[]{:S(2)}, u32[]{:S(2)}) collective-permute-start(bf16[7,16,256]{2,1,0:T(8,128)(2,1)S(1)} %get-tuple-element.28), channel_id=1, source_target_pairs={{0,24},{8,0},{16,8},{24,16},{1,25},{9,1},{17,9},{25,17},{2,26},{10... | collective-permute-start | bytes 172040 | tf_op jit(solution)/shard_map/ppermute | solution.py:367
  9.6 0.8 %copy.49 = bf16[64,64]{0,1:T(8,128)(2,1)S(1)} copy(bf16[64,64]{1,0:T(8,128)(2,1)} %param.31) | data formatting | bytes 16384 | tf_op args[14]
  10.5 0.1 copy.44
  10.5 0.0 copy-start.2
  10.6 0.5 copy-done.12
  11.2 0.3 collective-permute-start.1
  11.4 1.3 %collective-permute-start.3 = (s32[4,1024]{1,0:T(4,128)S(1)}, s32[4,1024]{1,0:T(4,128)S(1)}, u32[]{:S(2)}, u32[]{:S(2)}) collective-permute-start(s32[4,1024]{1,0:T(4,128)S(1)} %copy-done.2), channel_id=1, source_target_pairs={{0,7},{1,0},{2,1},{3,2},{4,3},{5,4},{6,5},{7,6},{8,15},{9,8},{10,9... | collective-permute-start | bytes 49160 | tf_op jit(solution)/shard_map/ppermute | solution.py:364
  12.8 2.6 %collective-permute-start.5 = (f32[4,1024]{1,0:T(4,128)S(1)}, f32[4,1024]{1,0:T(4,128)S(1)}, u32[]{:S(2)}, u32[]{:S(2)}) collective-permute-start(f32[4,1024]{1,0:T(4,128)S(1)} %copy-done.3), channel_id=1, source_target_pairs={{0,7},{1,0},{2,1},{3,2},{4,3},{5,4},{6,5},{7,6},{8,15},{9,8},{10,9... | collective-permute-start | bytes 49160 | tf_op jit(solution)/shard_map/ppermute | solution.py:364
  16.1 0.5 shard_map.166
  16.7 0.1 collective-permute-start.12
  16.8 0.1 collective-permute-done.4.dl
  16.8 0.0 collective-permute-done.5.dr
  16.9 2.7 %shard_map.163 = (f32[16,1536]{1,0:T(8,128)S(1)}, bf16[16,256]{1,0:T(8,128)(2,1)S(1)}, bf16[16,256]{1,0:T(8,128)(2,1)S(1)}, bf16[16,256]{1,0:T(8,128)(2,1)S(1)}, bf16[16,256]{1,0:T(8,128)(2,1)S(1)}) custom-call(s32[1]{0:T(128)} %bitcast.me, f32[16,1024]{1,0:T(8,128)S(1)} %collective-permute-done.left, f32[16,1024]{1,0:T(8,128)S(1)} %copy-done.4, ...), custom_call_target="tpu_custom_call" | custom-call | flops 10000000 | bytes 425988 | tf_op jit(solution)/shard_map/pallas_call | solution.py:28
  19.6 1.1 %collective-permute-start.10 = (bf16[16,256]{1,0:T(8,128)(2,1)S(1)}, bf16[16,256]{1,0:T(8,128)(2,1)S(1)}, u32[]{:S(2)}, u32[]{:S(2)}) collective-permute-start(bf16[16,256]{1,0:T(8,128)(2,1)S(1)} %get-tuple-element.32), channel_id=1, source_target_pairs={{0,16},{8,24},{16,0},{24,8},{1,17},{9,25},{17,1},{25,9},{2,18},{10... | collective-permute-start | bytes 24584 | tf_op jit(solution)/shard_map/ppermute | solution.py:367
  20.7 2.0 %collective-permute-start.11 = (bf16[16,256]{1,0:T(8,128)(2,1)S(1)}, bf16[16,256]{1,0:T(8,128)(2,1)S(1)}, u32[]{:S(2)}, u32[]{:S(2)}) collective-permute-start(bf16[16,256]{1,0:T(8,128)(2,1)S(1)} %get-tuple-element.33), channel_id=1, source_target_pairs={{0,24},{8,0},{16,8},{24,16},{1,25},{9,1},{17,9},{25,17},{2,26},{10... | collective-permute-start | bytes 24584 | tf_op jit(solution)/shard_map/ppermute | solution.py:367
  22.7 0.0 collective-permute-start.9
  22.8 0.1 copy.45
  22.9 0.6 copy-done.8
  23.5 0.1 copy.46
  23.6 0.6 collective-permute-done.10.rest_2_
  24.2 0.1 collective-permute-done.11.rest_3_
  24.4 3.8 %collective-permute-done.9.rest_1_ = bf16[16,256]{1,0:T(8,128)(2,1)S(1)} collective-permute-done((bf16[16,256]{1,0:T(8,128)(2,1)S(1)}, bf16[16,256]{1,0:T(8,128)(2,1)S(1)}, u32[]{:S(2)}, u32[]{:S(2)}) %collective-permute-start.9) | collective-permute-done | bytes 8224 | tf_op jit(solution)/shard_map/ppermute | solution.py:367
  28.2 0.1 shard_map.167
  28.3 0.1 collective-permute-start.13
  28.5 0.7 %copy-done.13 = f32[224]{0:T(256)S(1)} copy-done((f32[224]{0:T(256)S(1)}, f32[224]{0:T(256)}, u32[]{:S(2)}) %copy-start.13) | copy-done | bytes 920
  29.1 0.1 copy.52.flux
  29.3 0.6 copy-done.9
  29.9 0.1 copy.50
  30.0 0.1 copy.51.bias
  30.1 0.1 copy.48
  30.2 0.1 copy.53.bias
  30.3 0.1 copy.43
  30.4 7.9 %shard_map.169.work = f32[64,128]{1,0:T(8,128)S(1)} custom-call(s32[1,1]{1,0:T(1,128)S(6)} %copy.54.count, f32[512,128]{1,0:T(8,128)S(1)} %get-tuple-element.35.kept_x, f32[64,128]{1,0:T(8,128)S(1)} %get-tuple-element.36.kept_warm, f32[8,128]{1,0:T(8,128)S(1)} %get-tuple-element.37.kept_cos, bf16[528,128]{1,0:T(8,128)(2,1)S(1)} %collective-permute-done.12.in_x, ...), custom_call_target="tpu_custom_call" | custom-call | flops 234881024 | bytes 522372 | tf_op jit(solution)/shard_map/pallas_call | solution.py:28
  38.3 0.6 collective-permute-start.14
  38.9 10.3 %shard_map.168.long_first = f32[64,128]{1,0:T(8,128)S(1)} custom-call(f32[64,8,256]{2,1,0:T(8,128)S(1)} %get-tuple-element.29.packed, f32[64,256]{1,0:T(8,128)S(1)} %get-tuple-element.34.warm, bf16[64,8]{1,0:T(8,128)(2,1)S(1)} %bitcast.16, f32[64,1]{1,0:T(8,128)S(1)} %copy.53.bias, bf16[64,64]{1,0:T(8,128)(2,1)S(1)} %multiply_bitcast_fusion.1.second, ...), custom_call_target="tpu_custom_call" | custom-call | flops 536870912 | bytes 697600 | tf_op jit(solution)/shard_map/pallas_call | solution.py:28
  49.2 10.4 %shard_map.170 = (f32[16,256]{1,0:T(8,128)S(1)}, f32[16,256]{1,0:T(8,128)S(1)}, f32[16,256]{1,0:T(8,128)S(1)}, f32[16,256]{1,0:T(8,128)S(1)}) custom-call(s32[1]{0:T(128)} %bitcast.me, s32[1,1]{1,0:T(1,128)S(6)} %copy.54.count, f32[64,8,256]{2,1,0:T(8,128)S(1)} %get-tuple-element.29.packed, f32[64,256]{1,0:T(8,128)S(1)} %get-tuple-element.34.warm, ...), custom_call_target="tpu_custom_call" | custom-call | flops 536870912 | bytes 836872 | tf_op jit(solution)/shard_map/pallas_call | solution.py:28
  59.6 0.1 collective-permute-start.15
  59.6 0.6 collective-permute-start.16
  60.2 3.3 %collective-permute-start.17 = (f32[16,256]{1,0:T(8,128)S(1)}, f32[16,256]{1,0:T(8,128)S(1)}, u32[]{:S(2)}, u32[]{:S(2)}) collective-permute-start(f32[16,256]{1,0:T(8,128)S(1)} %get-tuple-element.44), channel_id=1, source_target_pairs={{0,24},{8,0},{16,8},{24,16},{1,25},{9,1},{17,9},{25,17},{2,26},{10... | collective-permute-start | bytes 49160 | tf_op jit(solution)/shard_map/ppermute | solution.py:367
  63.4 0.5 shard_map.164.closed
  64.0 1.2 %collective-permute-done.15.rest_1_ = f32[16,256]{1,0:T(8,128)S(1)} collective-permute-done((f32[16,256]{1,0:T(8,128)S(1)}, f32[16,256]{1,0:T(8,128)S(1)}, u32[]{:S(2)}, u32[]{:S(2)}) %collective-permute-start.15) | collective-permute-done | bytes 16416 | tf_op jit(solution)/shard_map/ppermute | solution.py:367
  65.2 0.6 collective-permute-done.17.rest_3_
  65.7 0.6 shard_map.171
  (46 shorter events, 0.2 us)
Async XLA Ops:
  0.0 16.9 %collective-permute-start = (f32[16,1024]{1,0:T(8,128)}, f32[16,1024]{1,0:T(8,128)S(1)}, u32[]{:S(2)}, u32[]{:S(2)}) collective-permute-start(f32[16,1024]{1,0:T(8,128)} %own.1), channel_id=1, source_target_pairs={{0,1},{1,2},{2,3},{3,4},{4,5},{5,6},{6,7},{7,0},{8,9},{9,10},{10,1... | collective-permute-start | bytes 196616 | tf_op jit(solution)/shard_map/ppermute | solution.py:364
  0.5 10.7 %collective-permute-start.2 = (s32[4,1024]{1,0:T(4,128)}, s32[4,1024]{1,0:T(4,128)S(1)}, u32[]{:S(2)}, u32[]{:S(2)}) collective-permute-start(s32[4,1024]{1,0:T(4,128)} %table.1), channel_id=1, source_target_pairs={{0,1},{1,2},{2,3},{3,4},{4,5},{5,6},{6,7},{7,0},{8,9},{9,10},{10,1... | collective-permute-start | bytes 49160 | tf_op jit(solution)/shard_map/ppermute | solution.py:364
  3.1 0.9 %copy-start = (bf16[7,16,1024]{2,1,0:T(8,128)(2,1)S(1)}, bf16[7,16,1024]{2,1,0:T(8,128)(2,1)}, u32[]{:S(2)}) copy-start(bf16[7,16,1024]{2,1,0:T(8,128)(2,1)} %species.3) | copy-start | bytes 688132
  4.0 12.1 %copy-start.1 = (bf16[7,16,1024]{2,1,0:T(8,128)(2,1)S(1)}, bf16[7,16,1024]{2,1,0:T(8,128)(2,1)}, u32[]{:S(2)}) copy-start(bf16[7,16,1024]{2,1,0:T(8,128)(2,1)} %species.3) | copy-start | bytes 688132
  4.0 7.4 %collective-permute-start.6 = (bf16[7,16,256]{2,1,0:T(8,128)(2,1)S(1)}, bf16[7,16,256]{2,1,0:T(8,128)(2,1)S(1)}, u32[]{:S(2)}, u32[]{:S(2)}) collective-permute-start(bf16[7,16,256]{2,1,0:T(8,128)(2,1)S(1)} %get-tuple-element.26), channel_id=1, source_target_pairs={{0,8},{8,16},{16,24},{24,0},{1,9},{9,17},{17,25},{25,1},{2,10},{10... | collective-permute-start | bytes 172040 | tf_op jit(solution)/shard_map/ppermute | solution.py:367
  5.7 4.8 %copy-start.11 = (bf16[8,64]{1,0:T(8,128)(2,1)S(1)}, bf16[8,64]{1,0:T(8,128)(2,1)}, u32[]{:S(2)}) copy-start(bf16[8,64]{1,0:T(8,128)(2,1)} %param.29) | copy-start | bytes 3076
  5.7 4.8 %copy-start.10 = (bf16[64,64]{1,0:T(8,128)(2,1)S(1)}, bf16[64,64]{1,0:T(8,128)(2,1)}, u32[]{:S(2)}) copy-start(bf16[64,64]{1,0:T(8,128)(2,1)} %param.26) | copy-start | bytes 24580
  5.7 7.1 %collective-permute-start.7 = (bf16[7,16,256]{2,1,0:T(8,128)(2,1)S(1)}, bf16[7,16,256]{2,1,0:T(8,128)(2,1)S(1)}, u32[]{:S(2)}, u32[]{:S(2)}) collective-permute-start(bf16[7,16,256]{2,1,0:T(8,128)(2,1)S(1)} %get-tuple-element.27), channel_id=1, source_target_pairs={{0,16},{8,24},{16,0},{24,8},{1,17},{9,25},{17,1},{25,9},{2,18},{10... | collective-permute-start | bytes 172040 | tf_op jit(solution)/shard_map/ppermute | solution.py:367
  8.2 2.9 %copy-start.4 = (f32[16,1024]{1,0:T(8,128)S(1)}, f32[16,1024]{1,0:T(8,128)}, u32[]{:S(2)}) copy-start(f32[16,1024]{1,0:T(8,128)} %own.1) | copy-start | bytes 196612
  8.2 4.5 %collective-permute-start.8 = (bf16[7,16,256]{2,1,0:T(8,128)(2,1)S(1)}, bf16[7,16,256]{2,1,0:T(8,128)(2,1)S(1)}, u32[]{:S(2)}, u32[]{:S(2)}) collective-permute-start(bf16[7,16,256]{2,1,0:T(8,128)(2,1)S(1)} %get-tuple-element.28), channel_id=1, source_target_pairs={{0,24},{8,0},{16,8},{24,16},{1,25},{9,1},{17,9},{25,17},{2,26},{10... | collective-permute-start | bytes 172040 | tf_op jit(solution)/shard_map/ppermute | solution.py:367
  10.4 0.7 %copy-start.12 = (bf16[8,64]{1,0:T(8,128)(2,1)S(1)}, bf16[8,64]{1,0:T(8,128)(2,1)}, u32[]{:S(2)}) copy-start(bf16[8,64]{1,0:T(8,128)(2,1)} %param.24) | copy-start | bytes 3076
  10.5 0.9 %copy-start.2 = (s32[4,1024]{1,0:T(4,128)S(1)}, s32[4,1024]{1,0:T(4,128)}, u32[]{:S(2)}) copy-start(s32[4,1024]{1,0:T(4,128)} %table.1) | copy-start | bytes 49156
  10.6 2.2 %copy-start.3 = (f32[4,1024]{1,0:T(4,128)S(1)}, f32[4,1024]{1,0:T(4,128)}, u32[]{:S(2)}) copy-start(f32[4,1024]{1,0:T(4,128)} %weight.1) | copy-start | bytes 49156
  11.1 4.3 %copy-start.14 = (f32[64]{0:T(128)S(1)}, f32[64]{0:T(128)}, u32[]{:S(2)}) copy-start(f32[64]{0:T(128)} %param.30) | copy-start | bytes 772
  11.1 5.0 %copy-start.6 = (bf16[1,1,256]{2,1,0:T(2,128)(2,1)S(1)}, bf16[1,1,256]{2,1,0:T(2,128)(2,1)}, u32[]{:S(2)}) copy-start(bf16[1,1,256]{2,1,0:T(2,128)(2,1)} %rest_4_.2) | copy-start | bytes 1540
  11.2 5.7 %collective-permute-start.1 = (f32[16,1024]{1,0:T(8,128)S(1)}, f32[16,1024]{1,0:T(8,128)S(1)}, u32[]{:S(2)}, u32[]{:S(2)}) collective-permute-start(f32[16,1024]{1,0:T(8,128)S(1)} %copy-done.4), channel_id=1, source_target_pairs={{0,7},{1,0},{2,1},{3,2},{4,3},{5,4},{6,5},{7,6},{8,15},{9,8},{10,9... | collective-permute-start | bytes 196616 | tf_op jit(solution)/shard_map/ppermute | solution.py:364
  11.4 5.2 %collective-permute-start.3 = (s32[4,1024]{1,0:T(4,128)S(1)}, s32[4,1024]{1,0:T(4,128)S(1)}, u32[]{:S(2)}, u32[]{:S(2)}) collective-permute-start(s32[4,1024]{1,0:T(4,128)S(1)} %copy-done.2), channel_id=1, source_target_pairs={{0,7},{1,0},{2,1},{3,2},{4,3},{5,4},{6,5},{7,6},{8,15},{9,8},{10,9... | collective-permute-start | bytes 49160 | tf_op jit(solution)/shard_map/ppermute | solution.py:364
  12.8 4.1 %collective-permute-start.4 = (f32[4,1024]{1,0:T(4,128)S(1)}, f32[4,1024]{1,0:T(4,128)S(1)}, u32[]{:S(2)}, u32[]{:S(2)}) collective-permute-start(f32[4,1024]{1,0:T(4,128)S(1)} %copy-done.3), channel_id=1, source_target_pairs={{0,1},{1,2},{2,3},{3,4},{4,5},{5,6},{6,7},{7,0},{8,9},{9,10},{10,1... | collective-permute-start | bytes 49160 | tf_op jit(solution)/shard_map/ppermute | solution.py:364
  12.8 4.1 %collective-permute-start.5 = (f32[4,1024]{1,0:T(4,128)S(1)}, f32[4,1024]{1,0:T(4,128)S(1)}, u32[]{:S(2)}, u32[]{:S(2)}) collective-permute-start(f32[4,1024]{1,0:T(4,128)S(1)} %copy-done.3), channel_id=1, source_target_pairs={{0,7},{1,0},{2,1},{3,2},{4,3},{5,4},{6,5},{7,6},{8,15},{9,8},{10,9... | collective-permute-start | bytes 49160 | tf_op jit(solution)/shard_map/ppermute | solution.py:364
  15.4 0.7 %copy-start.5 = (s32[1,1,256]{2,1,0:T(1,128)S(1)}, s32[1,1,256]{2,1,0:T(1,128)}, u32[]{:S(2)}) copy-start(s32[1,1,256]{2,1,0:T(1,128)} %rest_4_.3) | copy-start | bytes 3076
  16.7 6.1 %copy-start.7 = (bf16[64,256]{1,0:T(8,128)(2,1)S(1)}, bf16[64,256]{1,0:T(8,128)(2,1)}, u32[]{:S(2)}) copy-start(bf16[64,256]{1,0:T(8,128)(2,1)} %param.27) | copy-start | bytes 98308
  16.7 13.7 %collective-permute-start.12 = (bf16[528,128]{1,0:T(8,128)(2,1)S(1)}, bf16[528,128]{1,0:T(8,128)(2,1)S(1)}, u32[]{:S(2)}, u32[]{:S(2)}) collective-permute-start(bf16[528,128]{1,0:T(8,128)(2,1)S(1)} %get-tuple-element.38), channel_id=1, source_target_pairs={{0,1},{1,0},{2,3},{3,2},{4,5},{5,4},{6,7},{7,6},{8,9},{9,8},{10,11... | collective-permute-start | bytes 405512 | tf_op jit(solution)/shard_map/ppermute | solution.py:370
  19.6 4.6 %collective-permute-start.10 = (bf16[16,256]{1,0:T(8,128)(2,1)S(1)}, bf16[16,256]{1,0:T(8,128)(2,1)S(1)}, u32[]{:S(2)}, u32[]{:S(2)}) collective-permute-start(bf16[16,256]{1,0:T(8,128)(2,1)S(1)} %get-tuple-element.32), channel_id=1, source_target_pairs={{0,16},{8,24},{16,0},{24,8},{1,17},{9,25},{17,1},{25,9},{2,18},{10... | collective-permute-start | bytes 24584 | tf_op jit(solution)/shard_map/ppermute | solution.py:367
  20.7 2.0 %copy-start.15 = (f32[64]{0:T(128)S(1)}, f32[64]{0:T(128)}, u32[]{:S(2)}) copy-start(f32[64]{0:T(128)} %param.25) | copy-start | bytes 772
  20.7 3.7 %collective-permute-start.11 = (bf16[16,256]{1,0:T(8,128)(2,1)S(1)}, bf16[16,256]{1,0:T(8,128)(2,1)S(1)}, u32[]{:S(2)}, u32[]{:S(2)}) collective-permute-start(bf16[16,256]{1,0:T(8,128)(2,1)S(1)} %get-tuple-element.33), channel_id=1, source_target_pairs={{0,24},{8,0},{16,8},{24,16},{1,25},{9,1},{17,9},{25,17},{2,26},{10... | collective-permute-start | bytes 24584 | tf_op jit(solution)/shard_map/ppermute | solution.py:367
  22.7 5.4 %collective-permute-start.9 = (bf16[16,256]{1,0:T(8,128)(2,1)S(1)}, bf16[16,256]{1,0:T(8,128)(2,1)S(1)}, u32[]{:S(2)}, u32[]{:S(2)}) collective-permute-start(bf16[16,256]{1,0:T(8,128)(2,1)S(1)} %get-tuple-element.31), channel_id=1, source_target_pairs={{0,8},{8,16},{16,24},{24,0},{1,9},{9,17},{17,25},{25,1},{2,10},{10... | collective-permute-start | bytes 24584 | tf_op jit(solution)/shard_map/ppermute | solution.py:367
  22.8 0.8 %copy-start.8 = (bf16[64,256]{1,0:T(8,128)(2,1)S(1)}, bf16[64,256]{1,0:T(8,128)(2,1)}, u32[]{:S(2)}) copy-start(bf16[64,256]{1,0:T(8,128)(2,1)} %param.28) | copy-start | bytes 98308
  28.3 2.1 %collective-permute-start.13 = (bf16[64,128]{1,0:T(8,128)(2,1)S(1)}, bf16[64,128]{1,0:T(8,128)(2,1)S(1)}, u32[]{:S(2)}, u32[]{:S(2)}) collective-permute-start(bf16[64,128]{1,0:T(8,128)(2,1)S(1)} %get-tuple-element.39), channel_id=1, source_target_pairs={{0,1},{1,0},{2,3},{3,2},{4,5},{5,4},{6,7},{7,6},{8,9},{9,8},{10,11... | collective-permute-start | bytes 49160 | tf_op jit(solution)/shard_map/ppermute | solution.py:370
  28.5 0.7 %copy-start.13 = (f32[224]{0:T(256)S(1)}, f32[224]{0:T(256)}, u32[]{:S(2)}) copy-start(f32[224]{0:T(256)} %param.33) | copy-start | bytes 2692
  29.1 0.8 %copy-start.9 = (bf16[64,224]{1,0:T(8,128)(2,1)S(1)}, bf16[64,224]{1,0:T(8,128)(2,1)}, u32[]{:S(2)}) copy-start(bf16[64,224]{1,0:T(8,128)(2,1)} %param.32) | copy-start | bytes 86020
  38.3 10.8 %collective-permute-start.14 = (f32[64,128]{1,0:T(8,128)S(1)}, f32[64,128]{1,0:T(8,128)S(1)}, u32[]{:S(2)}, u32[]{:S(2)}) collective-permute-start(f32[64,128]{1,0:T(8,128)S(1)} %shard_map.169.work), channel_id=1, source_target_pairs={{0,1},{1,0},{2,3},{3,2},{4,5},{5,4},{6,7},{7,6},{8,9},{9,8},{10,11... | collective-permute-start | bytes 98312 | tf_op jit(solution)/shard_map/ppermute | solution.py:370
  59.6 5.6 %collective-permute-start.15 = (f32[16,256]{1,0:T(8,128)S(1)}, f32[16,256]{1,0:T(8,128)S(1)}, u32[]{:S(2)}, u32[]{:S(2)}) collective-permute-start(f32[16,256]{1,0:T(8,128)S(1)} %get-tuple-element.42), channel_id=1, source_target_pairs={{0,8},{8,16},{16,24},{24,0},{1,9},{9,17},{17,25},{25,1},{2,10},{10... | collective-permute-start | bytes 49160 | tf_op jit(solution)/shard_map/ppermute | solution.py:367
  59.6 5.5 %collective-permute-start.16 = (f32[16,256]{1,0:T(8,128)S(1)}, f32[16,256]{1,0:T(8,128)S(1)}, u32[]{:S(2)}, u32[]{:S(2)}) collective-permute-start(f32[16,256]{1,0:T(8,128)S(1)} %get-tuple-element.43), channel_id=1, source_target_pairs={{0,16},{8,24},{16,0},{24,8},{1,17},{9,25},{17,1},{25,9},{2,18},{10... | collective-permute-start | bytes 49160 | tf_op jit(solution)/shard_map/ppermute | solution.py:367
  60.2 5.5 %collective-permute-start.17 = (f32[16,256]{1,0:T(8,128)S(1)}, f32[16,256]{1,0:T(8,128)S(1)}, u32[]{:S(2)}, u32[]{:S(2)}) collective-permute-start(f32[16,256]{1,0:T(8,128)S(1)} %get-tuple-element.44), channel_id=1, source_target_pairs={{0,24},{8,0},{16,8},{24,16},{1,25},{9,1},{17,9},{25,17},{2,26},{10... | collective-permute-start | bytes 49160 | tf_op jit(solution)/shard_map/ppermute | solution.py:367

commit v2 on v1

--- a/solution.py
+++ b/solution.py
@@ -12,6 +12,7 @@
 LANES = 128
 SUBS = 8
 STEP_LEVELS = SUBS // 2
+TILE = 2 * LANES
 
 depth_scale = 0.1
 heat_scale = 12.0
@@ -80,21 +81,24 @@
     return [(r, m, m + t) for r, m, t in zip(groups, middle, total)]
 
 
-def sections_body(
-    n_group, me, left, own, right, nl, n0, nr, dl, d0, dr, third_out, *rest
-):
-    pieces, (frame, first, second) = rest[:n_group], rest[n_group:]
-    tile = own.shape[1]
+def sections_body(n_group, me, left, own, right, table, weight, third_out, *rest):
+    pieces, (frame, first, second, tables, weights) = rest[:n_group], rest[n_group:]
+    slab, tile = own.shape
+    near = table.shape[0]
     cols = tile // n_group
-    frame[:, 0:tile] = left[...]
+    for t, packed in ((0, left), (2, right)):
+        at = slice(t * tile, (t + 1) * tile)
+        frame[:, at] = packed[0:slab, :]
+        tables[t] = packed[slab : slab + near, :].astype(jnp.int32)
+        weights[t] = packed[slab + near : slab + 2 * near, :]
     frame[:, tile : 2 * tile] = own[...]
-    frame[:, 2 * tile :] = right[...]
-    tables, weights = (nl, n0, nr), (dl, d0, dr)
+    tables[1] = table[...]
+    weights[1] = weight[...]
 
     def run(src, src_at, halo, put):
         for at in range(tile - halo, 2 * tile + halo, LANES):
             t = at // tile
-            for r, _, value in diffused(src, src_at, tables[t], weights[t], at - t * tile, at):
+            for r, _, value in diffused(src, src_at, tables.at[t], weights.at[t], at - t * tile, at):
                 put(r, at, value)
 
     def put_first(r, at, value):
@@ -124,13 +128,6 @@
     for at in range(0, tile, LANES):
         for r, _, value in diffused(third, -HW, table, weight, at, at):
             out[r : r + SUBS, at : at + LANES] = value
-
-
-def gas_cut_body(n_group, me, species, *outs):
-    cols = outs[0].shape[2]
-    for s in range(1, n_group):
-        goal = lax.rem(me[0] + s, n_group)
-        outs[s - 1][...] = species[:, :, pl.ds(pl.multiple_of(goal * cols, LANES), cols)]
 
 
 def one_hots(listing, count):
@@ -146,26 +143,20 @@
 
 
 def gas_join_body(
-    n_group, me, count, species, *rest
+    me, count, gathered, listing, zenith, packed, outgoing, kept_x, kept_cos, slot_of, spread
 ):
-    arrived, rest = rest[: n_group - 1], rest[n_group - 1 :]
-    listing, zenith, packed, outgoing, kept_x, kept_cos, slot_of, spread = rest
-    gases, slab, _ = species.shape
+    n_group, gases, slab, _ = gathered.shape
     cols = packed.shape[2]
     half = cols // 2
     spread[...] = jnp.zeros_like(spread)
     for s in range(n_group):
-        source = lax.rem(me[0] + n_group - s, n_group)
         for lo in range(0, cols, LANES):
+            at = pl.multiple_of(me[0] * cols + lo, LANES)
             for f in range(gases):
-                if s == 0:
-                    at = pl.multiple_of(me[0] * cols + lo, LANES)
-                    value = species[f, :, pl.ds(at, LANES)]
-                else:
-                    value = arrived[s - 1][f, :, lo : lo + LANES]
+                value = gathered[s, f, :, pl.ds(at, LANES)]
                 spread[(f + 1) * slab : (f + 2) * slab, :] = value.astype(F32)
             for l in range(slab):
-                packed[source * slab + l, :, lo : lo + LANES] = spread[pl.ds(l, SUBS, stride=slab), :]
+                packed[s * slab + l, :, lo : lo + LANES] = spread[pl.ds(l, SUBS, stride=slab), :]
     hit_first, hit_last, kept, sent = one_hots(listing, count[0, 0])
     levels = packed.shape[0]
     flat = packed[...].reshape(levels * SUBS, cols).astype(BF16)
@@ -201,29 +192,48 @@
 
 
 def sweep(x_at, warm_at, first, bias, second, heads, gpts, rate, both, buffers, levels):
-    hid_a, hid_b, z_a, z_b, trans, parts = buffers
+    one_a, one_b, hid_a, hid_b, z_a, z_b, trans, parts = buffers
     steps = levels // STEP_LEVELS
     top = iota((SUBS, LANES), 0) == 0
-
-    def hidden(pair, odd, out):
+    wide = STEP_LEVELS * LANES
+    rows = heads.shape[0]
+    row_cut = rows // (4 if both else 2)
+
+    def first_tasks(pair, odd, out):
         pair = jnp.minimum(pair, steps // 2 - 1)
-        warm = warm_at(pl.multiple_of(pair * SUBS, SUBS))
-        tiles = []
-        for i in range(odd * STEP_LEVELS, (odd + 1) * STEP_LEVELS):
-            row = jnp.broadcast_to(warm[i : i + 1], (SUBS, LANES))
-            tiles.append(jnp.where(top, row, x_at(pair * SUBS + i)))
-        x = jnp.concatenate(tiles, axis=1).astype(BF16)
-        v = mm(first[...], x) + bias[...]
-        one = (v + v * jnp.tanh(v)).astype(BF16)
-        v = mm(second[...], one)
-        out[...] = (v + v * jnp.tanh(v)).astype(BF16)
-
-    def optics(hid, out):
-        out[...] = mm(heads[...], hid[...])
-
-    def consume(t, z):
-        total = [None] * STEP_LEVELS
-        for lo in range(0, gpts, SUBS):
+
+        def task(lo):
+            warm = warm_at(pl.multiple_of(pair * SUBS, SUBS))
+            tiles = []
+            for at in range(lo, lo + TILE, LANES):
+                i = odd * STEP_LEVELS + at // LANES
+                row = jnp.broadcast_to(warm[i : i + 1], (SUBS, LANES))
+                tiles.append(jnp.where(top, row, x_at(pair * SUBS + i)))
+            x = jnp.concatenate(tiles, axis=1).astype(BF16)
+            v = mm(first[...], x) + bias[...]
+            out[:, lo : lo + TILE] = (v + v * jnp.tanh(v)).astype(BF16)
+
+        return [functools.partial(task, lo) for lo in range(0, wide, TILE)]
+
+    def second_tasks(one, out):
+        def task(lo):
+            v = mm(second[...], one[:, lo : lo + TILE])
+            out[:, lo : lo + TILE] = (v + v * jnp.tanh(v)).astype(BF16)
+
+        return [functools.partial(task, lo) for lo in range(0, wide, TILE)]
+
+    def optics_tasks(hid, out):
+        def task(lo, r):
+            out[r : r + row_cut, lo : lo + TILE] = mm(heads[r : r + row_cut, :], hid[:, lo : lo + TILE])
+
+        return [
+            functools.partial(task, lo, r)
+            for lo in range(0, wide, TILE)
+            for r in range(0, rows, row_cut)
+        ]
+
+    def consume_tasks(t, z, total):
+        def task(lo):
             carry = trans[lo : lo + SUBS, :]
             for i in range(STEP_LEVELS):
                 at = i * LANES
@@ -235,22 +245,45 @@
                 total[i] = drop if total[i] is None else total[i] + drop
                 carry = following
             trans[lo : lo + SUBS, :] = carry
+
+        return [functools.partial(task, lo) for lo in range(0, gpts, SUBS)]
+
+    def woven(main, side):
+        done = 0
+        for n, task in enumerate(main):
+            while done < len(side) and done * len(main) <= n * len(side):
+                side[done]()
+                done += 1
+            task()
+        for task in side[done:]:
+            task()
+
+    def plain(tasks):
+        for task in tasks:
+            task()
+
+    def step(t, pair, odd, z, z_next, hid_next, hid_later, one_later, one_last):
+        total = [None] * STEP_LEVELS
+        side = (
+            optics_tasks(hid_next, z_next)
+            + second_tasks(one_later, hid_later)
+            + first_tasks(pair, odd, one_last)
+        )
+        woven(consume_tasks(t, z, total), side)
         for i in range(STEP_LEVELS):
             at = pl.multiple_of((t * STEP_LEVELS + i) * SUBS, SUBS)
             parts[pl.ds(at, SUBS), :] = total[i]
 
-    hidden(0, 0, hid_a)
-    optics(hid_a, z_a)
-    hidden(0, 1, hid_b)
+    plain(first_tasks(0, 0, one_a))
+    plain(second_tasks(one_a, hid_a))
+    plain(first_tasks(0, 1, one_b))
+    plain(optics_tasks(hid_a, z_a))
+    plain(second_tasks(one_b, hid_b))
+    plain(first_tasks(1, 0, one_a))
 
     def two(i, _):
-        t = 2 * i
-        consume(t, z_a)
-        optics(hid_b, z_b)
-        hidden(i + 1, 0, hid_a)
-        consume(t + 1, z_b)
-        optics(hid_a, z_a)
-        hidden(i + 1, 1, hid_b)
+        step(2 * i, i + 1, 1, z_a, z_b, hid_b, hid_a, one_a, one_b)
+        step(2 * i + 1, i + 2, 0, z_b, z_a, hid_a, hid_b, one_b, one_a)
         return 0
 
     lax.fori_loop(0, steps // 2, two, 0)
@@ -263,6 +296,8 @@
 def sweep_scratch(hid, rows, gpts, levels):
     wide = STEP_LEVELS * LANES
     return [
+        pltpu.VMEM((hid, wide), BF16),
+        pltpu.VMEM((hid, wide), BF16),
         pltpu.VMEM((hid, wide), BF16),
         pltpu.VMEM((hid, wide), BF16),
         pltpu.VMEM((rows, wide), F32),
@@ -275,7 +310,7 @@
 def longwave_part(lo, packed, warm, first, bias, second, heads, buffers):
     gpts = heads.shape[0] // 2
     levels = packed.shape[0]
-    buffers[4][...] = jnp.ones_like(buffers[4])
+    buffers[6][...] = jnp.ones_like(buffers[6])
     emitted = sweep(
         lambda l: packed[l, :, lo : lo + LANES],
         lambda l: warm[pl.ds(l, SUBS), lo : lo + LANES],
@@ -303,7 +338,7 @@
     work_warm[...] = kept_warm[...] + mm(in_warm[...], placed)
     cosine = kept_cos[...] + mm(in_x[cells:, :], placed)[0:SUBS]
     cosine = jnp.where(cosine > 0.0, cosine, 1.0)
-    buffers[4][...] = jnp.broadcast_to(flux[...], buffers[4].shape)
+    buffers[6][...] = jnp.broadcast_to(flux[...], buffers[6].shape)
     emitted = sweep(
         lambda l: work_x[pl.ds(pl.multiple_of(l * SUBS, SUBS), SUBS), :],
         lambda l: work_warm[pl.ds(l, SUBS), :],
@@ -355,7 +390,6 @@
     n_tile = lax.axis_size("tile")
     me = lax.axis_index("group").astype(jnp.int32).reshape(1)
     slab, tile = potential.shape
-    gases = species.shape[0]
     cols = tile // n_group
     half = cols // 2
     levels = slab * n_group
@@ -369,16 +403,10 @@
     def paired(value):
         return lax.ppermute(value, "tile", [(i, i ^ 1) for i in range(n_tile)])
 
-    framing = (potential, neighbours, diffusion)
-    left = [turned(a, 1) for a in framing]
-    right = [turned(a, -1) for a in framing]
-
-    cuts = call(
-        functools.partial(gas_cut_body, n_group),
-        [shaped((gases, slab, cols), BF16)] * (n_group - 1),
-        [me, species],
-    )
-    arrived = [along(c, s + 1) for s, c in enumerate(cuts)]
+    framing = jnp.concatenate([potential, neighbours.astype(F32), diffusion], axis=0)
+    left = turned(framing, 1)
+    right = turned(framing, -1)
+    gathered = lax.all_gather(species, "group")
 
     lw_one = (0.5 * lw_first).T
     lw_two = (0.5 * lw_second).T
@@ -396,14 +424,15 @@
     third, *warm_cuts = call(
         functools.partial(sections_body, n_group),
         [shaped((slab, tile + 2 * HW), F32)] + [shaped((slab, cols), BF16)] * n_group,
-        [me, left[0], potential, right[0], left[1], neighbours, right[1], left[2], diffusion, right[2]],
-        [pltpu.VMEM((slab, 3 * tile), F32)] * 3,
+        [me, left, potential, right, neighbours, diffusion],
+        [pltpu.VMEM((slab, 3 * tile), F32)] * 3
+        + [pltpu.VMEM((3, *neighbours.shape), jnp.int32), pltpu.VMEM((3, *diffusion.shape), F32)],
         flops=10_000_000,
     )
     warm_pieces = [warm_cuts[0]] + [along(c, s + 1) for s, c in enumerate(warm_cuts[1:])]
 
     packed, out_x, kept_x, kept_cos, slot_of = call(
-        functools.partial(gas_join_body, n_group),
+        gas_join_body,
         [
             shaped((levels, SUBS, cols), F32),
             shaped((levels * SUBS + 2 * SUBS, half), BF16),
@@ -411,7 +440,7 @@
             shaped((SUBS, half), F32),
             shaped((SUBS, cols), jnp.int32),
         ],
-        [me, day_count, species, *arrived, listing, zenith],
+        [me, day_count, gathered, listing, zenith],
         [pltpu.VMEM((SUBS * slab, LANES), F32)],
     )
     in_x = paired(out_x)

time: 66.8 us -> 75.8 us (1.13)
  blocking collectives: 0 us -> 22.3 us
  starting transfers between devices: 20.5 us -> 12.5 us
  Pallas kernels: 33.2 us -> 29.5 us
  waiting for transfers between devices: 6.44 us -> 3.91 us
  other arithmetic: 0.05 us -> 1.64 us
    all_gather x0 -> x1, blocking collectives: none -> 22.3 us  [per_device(): gathered = lax.all_gather(species, 'group')]
    ppermute x9 -> x6, starting transfers between devices: 12.6 us -> 8.36 us  [along(): lax.ppermute(value, 'group', [(i, (i + by) % n_group) for i in range(n_gr...]
    ppermute x6 -> x2, starting transfers between devices: 7.29 us -> 3.45 us  [turned(): lax.ppermute(value, 'tile', [(i, (i + by) % n_tile) for i in range(n_tile)])]
    pallas_call x9 -> x8, Pallas kernels: 33.2 us -> 29.5 us  [call(): pl.pallas_call(body, out_shape=outs, in_specs=specs or [SMEM if a.size ==...]
    ppermute x9 -> x6, waiting for transfers between devices: 6.32 us -> 3.9 us  [along(): lax.ppermute(value, 'group', [(i, (i + by) % n_group) for i in range(n_gr...]
    concatenate x0 -> x1, other arithmetic: none -> 0.85 us  [per_device(): jnp.concatenate([potential, neighbours.astype(F32), diffusion], axis=0)]
    unnamed x37 -> x35, local copies, waits for them, and re-layouts: 4.69 us -> 4.02 us
  transfers between devices with their start and end apart: 18 -> 11, of which waited for: 6 -> 5; matrix products, arithmetic and copies ran while one was open for 3% -> 1% of each run, Pallas kernels for 21% -> 17%
where the time goes in v2:
time: 75.8 us; the launch traced here: 75.3 us
  Pallas kernels  29.5 us (39%)
  blocking collectives  22.3 us (29%)
  starting transfers between devices  12.5 us (16%)
  local copies, waits for them, and re-layouts  4.53 us (6%)
  waiting for transfers between devices  3.91 us (5%)
  other arithmetic  1.64 us (2%)
  between operations  0.88 us (1%)
    pallas_call x8, Pallas kernels, call(): pl.pallas_call(body, out_shape=outs, in_specs=specs or [SMEM if a.size ==...  29.5 us
    all_gather x1, blocking collectives, per_device(): gathered = lax.all_gather(species, 'group')  22.3 us
    ppermute x6, starting transfers between devices, along(): lax.ppermute(value, 'group', [(i, (i + by) % n_group) for i in range(n_gr...  8.36 us
    unnamed x35, local copies, waits for them, and re-layouts  4.02 us
    ppermute x6, waiting for transfers between devices, along(): lax.ppermute(value, 'group', [(i, (i + by) % n_group) for i in range(n_gr...  3.9 us
    ppermute x2, starting transfers between devices, turned(): lax.ppermute(value, 'tile', [(i, (i + by) % n_tile) for i in range(n_tile)])  3.45 us
  transfers between devices with their start and end apart: 11, of which 5 were waited for; matrix products, arithmetic and copies ran while one was open for 1% of the time, Pallas kernels for 17%

profile of v2, /device:TPU:0, one launch (start us, length us, event | category | flops | bytes accessed | tf_op | source)
XLA Modules:
  0.0 75.3 jit_solution(8091557072343583787)
XLA Ops:
  0.0 0.7 convert_element_type.3
  0.7 0.9 %pad_maximum_fusion = f32[24,1024]{1,0:T(8,128)S(1)} fusion(f32[4,1024]{1,0:T(4,128)S(1)} %copy-done.1, f32[4,1024]{1,0:T(4,128)S(1)} %convert_element_type.3, f32[16,1024]{1,0:T(8,128)} %own.1), kind=kLoop, calls=%fused_computation.1 | loop fusion | flops 49152 | bytes 196608 | tf_op jit(solution)/shard_map/concatenate | solution.py:406
  1.6 0.5 collective-permute-start
  2.1 2.9 %collective-permute-start.1 = (f32[24,1024]{1,0:T(8,128)S(1)}, f32[24,1024]{1,0:T(8,128)S(1)}, u32[]{:S(2)}, u32[]{:S(2)}) collective-permute-start(f32[24,1024]{1,0:T(8,128)S(1)} %pad_maximum_fusion), channel_id=1, source_target_pairs={{0,7},{1,0},{2,1},{3,2},{4,3},{5,4},{6,5},{7,6},{8,15},{9,8},{10,9... | collective-permute-start | bytes 294920 | tf_op jit(solution)/shard_map/ppermute | solution.py:398
  5.7 0.0 copy-start.4
  5.7 22.3 %all-gather = bf16[28,16,1024]{2,1,0:T(8,128)(2,1)S(1)} all-gather(bf16[7,16,1024]{2,1,0:T(8,128)(2,1)} %param.18), channel_id=2, replica_groups=mesh['group'=4,'tile'=8] {'group'}, dimensions={0}, use_global_device_ids=true | all-gather | bytes 1146880 | tf_op jit(solution)/shard_map/all_gather | solution.py:409
  28.0 0.7 copy-done.3
  28.7 0.4 shard_map.165
  29.1 0.1 collective-permute-start.5
  29.2 0.2 copy-done.10
  29.3 0.0 copy-done.8
  29.4 0.1 copy.57
  29.5 0.1 copy.62
  29.6 0.0 copy-start.2
  29.6 0.6 copy-done.13
  30.3 0.1 copy-done.2
  30.4 2.7 %shard_map.163 = (f32[16,1536]{1,0:T(8,128)S(1)}, bf16[16,256]{1,0:T(8,128)(2,1)S(1)}, bf16[16,256]{1,0:T(8,128)(2,1)S(1)}, bf16[16,256]{1,0:T(8,128)(2,1)S(1)}, bf16[16,256]{1,0:T(8,128)(2,1)S(1)}) custom-call(s32[1]{0:T(128)} %bitcast.me, f32[24,1024]{1,0:T(8,128)S(1)} %collective-permute-done.left, f32[16,1024]{1,0:T(8,128)S(1)} %copy-done, ...), custom_call_target="tpu_custom_call" | custom-call | flops 10000000 | bytes 425988 | tf_op jit(solution)/shard_map/pallas_call | solution.py:29
  33.1 0.1 collective-permute-start.2
  33.2 1.8 %collective-permute-start.3 = (bf16[16,256]{1,0:T(8,128)(2,1)S(1)}, bf16[16,256]{1,0:T(8,128)(2,1)S(1)}, u32[]{:S(2)}, u32[]{:S(2)}) collective-permute-start(bf16[16,256]{1,0:T(8,128)(2,1)S(1)} %get-tuple-element.26), channel_id=1, source_target_pairs={{0,16},{8,24},{16,0},{24,8},{1,17},{9,25},{17,1},{25,9},{2,18},{10... | collective-permute-start | bytes 24584 | tf_op jit(solution)/shard_map/ppermute | solution.py:401
  34.9 2.0 %collective-permute-start.4 = (bf16[16,256]{1,0:T(8,128)(2,1)S(1)}, bf16[16,256]{1,0:T(8,128)(2,1)S(1)}, u32[]{:S(2)}, u32[]{:S(2)}) collective-permute-start(bf16[16,256]{1,0:T(8,128)(2,1)S(1)} %get-tuple-element.27), channel_id=1, source_target_pairs={{0,24},{8,0},{16,8},{24,16},{1,25},{9,1},{17,9},{25,17},{2,26},{10... | collective-permute-start | bytes 24584 | tf_op jit(solution)/shard_map/ppermute | solution.py:401
  37.0 0.1 copy.59
  37.1 0.6 copy-done.6
  37.8 0.1 copy.58
  37.9 0.7 collective-permute-done.2.rest_1_
  38.6 0.6 collective-permute-done.4.rest_3_
  39.2 0.1 shard_map.166
  39.3 0.1 collective-permute-start.6
  39.4 0.1 copy.56
  39.5 0.1 copy.66.bias
  39.6 0.1 copy.61
  39.7 0.1 copy.64.bias
  39.8 0.6 copy-done.7
  40.4 0.1 copy.63
  40.5 0.0 copy-start.12
  40.5 0.7 copy-done.12
  41.2 0.1 copy.65.flux
  41.4 6.3 %shard_map.168.work = f32[64,128]{1,0:T(8,128)S(1)} custom-call(s32[1,1]{1,0:T(1,128)S(6)} %copy.67.count, f32[512,128]{1,0:T(8,128)S(1)} %get-tuple-element.29.kept_x, f32[64,128]{1,0:T(8,128)S(1)} %get-tuple-element.30.kept_warm, f32[8,128]{1,0:T(8,128)S(1)} %get-tuple-element.31.kept_cos, bf16[528,128]{1,0:T(8,128)(2,1)S(1)} %collective-permute-done.5.in_x, ...), custom_call_target="tpu_custom_call" | custom-call | flops 234881024 | bytes 522372 | tf_op jit(solution)/shard_map/pallas_call | solution.py:29
  47.7 0.6 collective-permute-start.7
  48.3 9.3 %shard_map.167.long_first = f32[64,128]{1,0:T(8,128)S(1)} custom-call(f32[64,8,256]{2,1,0:T(8,128)S(1)} %get-tuple-element.23.packed, f32[64,256]{1,0:T(8,128)S(1)} %get-tuple-element.28.warm, bf16[64,8]{1,0:T(8,128)(2,1)S(1)} %bitcast.18, f32[64,1]{1,0:T(8,128)S(1)} %copy.66.bias, bf16[64,64]{1,0:T(8,128)(2,1)S(1)} %multiply_bitcast_fusion.1.second, ...), custom_call_target="tpu_custom_call" | custom-call | flops 536870912 | bytes 697600 | tf_op jit(solution)/shard_map/pallas_call | solution.py:29
  57.6 9.4 %shard_map.169 = (f32[16,256]{1,0:T(8,128)S(1)}, f32[16,256]{1,0:T(8,128)S(1)}, f32[16,256]{1,0:T(8,128)S(1)}, f32[16,256]{1,0:T(8,128)S(1)}) custom-call(s32[1]{0:T(128)} %bitcast.me, s32[1,1]{1,0:T(1,128)S(6)} %copy.67.count, f32[64,8,256]{2,1,0:T(8,128)S(1)} %get-tuple-element.23.packed, f32[64,256]{1,0:T(8,128)S(1)} %get-tuple-element.28.warm, ...), custom_call_target="tpu_custom_call" | custom-call | flops 536870912 | bytes 836872 | tf_op jit(solution)/shard_map/pallas_call | solution.py:29
  67.0 2.1 %collective-permute-start.8 = (f32[16,256]{1,0:T(8,128)S(1)}, f32[16,256]{1,0:T(8,128)S(1)}, u32[]{:S(2)}, u32[]{:S(2)}) collective-permute-start(f32[16,256]{1,0:T(8,128)S(1)} %get-tuple-element.36), channel_id=1, source_target_pairs={{0,8},{8,16},{16,24},{24,0},{1,9},{9,17},{17,25},{25,1},{2,10},{10... | collective-permute-start | bytes 49160 | tf_op jit(solution)/shard_map/ppermute | solution.py:401
  69.1 1.8 %collective-permute-start.9 = (f32[16,256]{1,0:T(8,128)S(1)}, f32[16,256]{1,0:T(8,128)S(1)}, u32[]{:S(2)}, u32[]{:S(2)}) collective-permute-start(f32[16,256]{1,0:T(8,128)S(1)} %get-tuple-element.37), channel_id=1, source_target_pairs={{0,16},{8,24},{16,0},{24,8},{1,17},{9,25},{17,1},{25,9},{2,18},{10... | collective-permute-start | bytes 49160 | tf_op jit(solution)/shard_map/ppermute | solution.py:401
  70.9 0.6 collective-permute-start.10
  71.5 0.5 shard_map.164.closed
  72.0 0.6 collective-permute-done.8.rest_1_
  72.7 1.0 %collective-permute-done.9.rest_2_ = f32[16,256]{1,0:T(8,128)S(1)} collective-permute-done((f32[16,256]{1,0:T(8,128)S(1)}, f32[16,256]{1,0:T(8,128)S(1)}, u32[]{:S(2)}, u32[]{:S(2)}) %collective-permute-start.9) | collective-permute-done | bytes 16416 | tf_op jit(solution)/shard_map/ppermute | solution.py:401
  73.7 0.9 %collective-permute-done.10.rest_3_ = f32[16,256]{1,0:T(8,128)S(1)} collective-permute-done((f32[16,256]{1,0:T(8,128)S(1)}, f32[16,256]{1,0:T(8,128)S(1)}, u32[]{:S(2)}, u32[]{:S(2)}) %collective-permute-start.10) | collective-permute-done | bytes 16416 | tf_op jit(solution)/shard_map/ppermute | solution.py:401
  74.6 0.6 shard_map.170
  (32 shorter events, 0.1 us)
Async XLA Ops:
  0.0 0.7 copy-start.1
  1.6 28.7 %collective-permute-start = (f32[24,1024]{1,0:T(8,128)S(1)}, f32[24,1024]{1,0:T(8,128)S(1)}, u32[]{:S(2)}, u32[]{:S(2)}) collective-permute-start(f32[24,1024]{1,0:T(8,128)S(1)} %pad_maximum_fusion), channel_id=1, source_target_pairs={{0,1},{1,2},{2,3},{3,4},{4,5},{5,6},{6,7},{7,0},{8,9},{9,10},{10,1... | collective-permute-start | bytes 294920 | tf_op jit(solution)/shard_map/ppermute | solution.py:398
  2.1 28.2 %collective-permute-start.1 = (f32[24,1024]{1,0:T(8,128)S(1)}, f32[24,1024]{1,0:T(8,128)S(1)}, u32[]{:S(2)}, u32[]{:S(2)}) collective-permute-start(f32[24,1024]{1,0:T(8,128)S(1)} %pad_maximum_fusion), channel_id=1, source_target_pairs={{0,7},{1,0},{2,1},{3,2},{4,3},{5,4},{6,5},{7,6},{8,15},{9,8},{10,9... | collective-permute-start | bytes 294920 | tf_op jit(solution)/shard_map/ppermute | solution.py:398
  5.7 22.3 %copy-start.4 = (bf16[1,1,256]{2,1,0:T(2,128)(2,1)S(1)}, bf16[1,1,256]{2,1,0:T(2,128)(2,1)}, u32[]{:S(2)}) copy-start(bf16[1,1,256]{2,1,0:T(2,128)(2,1)} %zenith.1) | copy-start | bytes 1540
  28.0 0.7 copy-start.3
  28.6 0.7 copy-start.10
  28.6 0.7 copy-start.8
  28.7 0.8 %copy-start.11 = (bf16[8,64]{1,0:T(8,128)(2,1)S(1)}, bf16[8,64]{1,0:T(8,128)(2,1)}, u32[]{:S(2)}) copy-start(bf16[8,64]{1,0:T(8,128)(2,1)} %param.29) | copy-start | bytes 3076
  28.7 0.9 %copy-start.9 = (bf16[64,64]{1,0:T(8,128)(2,1)S(1)}, bf16[64,64]{1,0:T(8,128)(2,1)}, u32[]{:S(2)}) copy-start(bf16[64,64]{1,0:T(8,128)(2,1)} %param.31) | copy-start | bytes 24580
  29.1 12.3 %collective-permute-start.5 = (bf16[528,128]{1,0:T(8,128)(2,1)S(1)}, bf16[528,128]{1,0:T(8,128)(2,1)S(1)}, u32[]{:S(2)}, u32[]{:S(2)}) collective-permute-start(bf16[528,128]{1,0:T(8,128)(2,1)S(1)} %get-tuple-element.32), channel_id=1, source_target_pairs={{0,1},{1,0},{2,3},{3,2},{4,5},{5,4},{6,7},{7,6},{8,9},{9,8},{10,11... | collective-permute-start | bytes 405512 | tf_op jit(solution)/shard_map/ppermute | solution.py:404
  29.4 0.9 %copy-start = (f32[16,1024]{1,0:T(8,128)S(1)}, f32[16,1024]{1,0:T(8,128)}, u32[]{:S(2)}) copy-start(f32[16,1024]{1,0:T(8,128)} %own.1) | copy-start | bytes 196612
  29.6 0.7 copy-start.13
  29.6 0.7 copy-start.2
  30.3 6.7 %copy-start.5 = (bf16[64,256]{1,0:T(8,128)(2,1)S(1)}, bf16[64,256]{1,0:T(8,128)(2,1)}, u32[]{:S(2)}) copy-start(bf16[64,256]{1,0:T(8,128)(2,1)} %param.28) | copy-start | bytes 98308
  33.1 5.5 %collective-permute-start.2 = (bf16[16,256]{1,0:T(8,128)(2,1)S(1)}, bf16[16,256]{1,0:T(8,128)(2,1)S(1)}, u32[]{:S(2)}, u32[]{:S(2)}) collective-permute-start(bf16[16,256]{1,0:T(8,128)(2,1)S(1)} %get-tuple-element.25), channel_id=1, source_target_pairs={{0,8},{8,16},{16,24},{24,0},{1,9},{9,17},{17,25},{25,1},{2,10},{10... | collective-permute-start | bytes 24584 | tf_op jit(solution)/shard_map/ppermute | solution.py:401
  33.2 3.8 %copy-start.14 = (f32[64]{0:T(128)S(1)}, f32[64]{0:T(128)}, u32[]{:S(2)}) copy-start(f32[64]{0:T(128)} %param.30) | copy-start | bytes 772
  33.2 5.4 %collective-permute-start.3 = (bf16[16,256]{1,0:T(8,128)(2,1)S(1)}, bf16[16,256]{1,0:T(8,128)(2,1)S(1)}, u32[]{:S(2)}, u32[]{:S(2)}) collective-permute-start(bf16[16,256]{1,0:T(8,128)(2,1)S(1)} %get-tuple-element.26), channel_id=1, source_target_pairs={{0,16},{8,24},{16,0},{24,8},{1,17},{9,25},{17,1},{25,9},{2,18},{10... | collective-permute-start | bytes 24584 | tf_op jit(solution)/shard_map/ppermute | solution.py:401
  34.9 4.2 %collective-permute-start.4 = (bf16[16,256]{1,0:T(8,128)(2,1)S(1)}, bf16[16,256]{1,0:T(8,128)(2,1)S(1)}, u32[]{:S(2)}, u32[]{:S(2)}) collective-permute-start(bf16[16,256]{1,0:T(8,128)(2,1)S(1)} %get-tuple-element.27), channel_id=1, source_target_pairs={{0,24},{8,0},{16,8},{24,16},{1,25},{9,1},{17,9},{25,17},{2,26},{10... | collective-permute-start | bytes 24584 | tf_op jit(solution)/shard_map/ppermute | solution.py:401
  37.0 0.8 %copy-start.6 = (bf16[64,256]{1,0:T(8,128)(2,1)S(1)}, bf16[64,256]{1,0:T(8,128)(2,1)}, u32[]{:S(2)}) copy-start(bf16[64,256]{1,0:T(8,128)(2,1)} %param.27) | copy-start | bytes 98308
  39.3 2.0 %collective-permute-start.6 = (bf16[64,128]{1,0:T(8,128)(2,1)S(1)}, bf16[64,128]{1,0:T(8,128)(2,1)S(1)}, u32[]{:S(2)}, u32[]{:S(2)}) collective-permute-start(bf16[64,128]{1,0:T(8,128)(2,1)S(1)} %get-tuple-element.33), channel_id=1, source_target_pairs={{0,1},{1,0},{2,3},{3,2},{4,5},{5,4},{6,7},{7,6},{8,9},{9,8},{10,11... | collective-permute-start | bytes 49160 | tf_op jit(solution)/shard_map/ppermute | solution.py:404
  39.6 0.8 %copy-start.7 = (bf16[64,224]{1,0:T(8,128)(2,1)S(1)}, bf16[64,224]{1,0:T(8,128)(2,1)}, u32[]{:S(2)}) copy-start(bf16[64,224]{1,0:T(8,128)(2,1)} %param.32) | copy-start | bytes 86020
  40.5 0.7 copy-start.12
  47.7 9.9 %collective-permute-start.7 = (f32[64,128]{1,0:T(8,128)S(1)}, f32[64,128]{1,0:T(8,128)S(1)}, u32[]{:S(2)}, u32[]{:S(2)}) collective-permute-start(f32[64,128]{1,0:T(8,128)S(1)} %shard_map.168.work), channel_id=1, source_target_pairs={{0,1},{1,0},{2,3},{3,2},{4,5},{5,4},{6,7},{7,6},{8,9},{9,8},{10,11... | collective-permute-start | bytes 98312 | tf_op jit(solution)/shard_map/ppermute | solution.py:404
  67.0 5.7 %collective-permute-start.8 = (f32[16,256]{1,0:T(8,128)S(1)}, f32[16,256]{1,0:T(8,128)S(1)}, u32[]{:S(2)}, u32[]{:S(2)}) collective-permute-start(f32[16,256]{1,0:T(8,128)S(1)} %get-tuple-element.36), channel_id=1, source_target_pairs={{0,8},{8,16},{16,24},{24,0},{1,9},{9,17},{17,25},{25,1},{2,10},{10... | collective-permute-start | bytes 49160 | tf_op jit(solution)/shard_map/ppermute | solution.py:401
  69.1 4.6 %collective-permute-start.9 = (f32[16,256]{1,0:T(8,128)S(1)}, f32[16,256]{1,0:T(8,128)S(1)}, u32[]{:S(2)}, u32[]{:S(2)}) collective-permute-start(f32[16,256]{1,0:T(8,128)S(1)} %get-tuple-element.37), channel_id=1, source_target_pairs={{0,16},{8,24},{16,0},{24,8},{1,17},{9,25},{17,1},{25,9},{2,18},{10... | collective-permute-start | bytes 49160 | tf_op jit(solution)/shard_map/ppermute | solution.py:401
  70.9 3.7 %collective-permute-start.10 = (f32[16,256]{1,0:T(8,128)S(1)}, f32[16,256]{1,0:T(8,128)S(1)}, u32[]{:S(2)}, u32[]{:S(2)}) collective-permute-start(f32[16,256]{1,0:T(8,128)S(1)} %get-tuple-element.38), channel_id=1, source_target_pairs={{0,24},{8,0},{16,8},{24,16},{1,25},{9,1},{17,9},{25,17},{2,26},{10... | collective-permute-start | bytes 49160 | tf_op jit(solution)/shard_map/ppermute | solution.py:401

commit v3 on v2

--- a/solution.py
+++ b/solution.py
@@ -12,7 +12,6 @@
 LANES = 128
 SUBS = 8
 STEP_LEVELS = SUBS // 2
-TILE = 2 * LANES
 
 depth_scale = 0.1
 heat_scale = 12.0
@@ -25,11 +24,19 @@
 PARAMS = pltpu.CompilerParams(vmem_limit_bytes=48 * 1024 * 1024)
 
 
-def call(body, outs, ins, scratch=(), flops=0, trans=0, specs=None):
+def call(body, outs, ins, scratch=(), flops=0, trans=0, after=None):
+    in_specs = [SMEM if a.size == 1 else VMEM for a in ins]
+    if after is not None:
+        whole, ins = body, [after, *ins]
+        in_specs = [pl.BlockSpec(memory_space=pl.ANY), *in_specs]
+
+        def body(_, *refs):
+            whole(*refs)
+
     return pl.pallas_call(
         body,
         out_shape=outs,
-        in_specs=specs or [SMEM if a.size == 1 else VMEM for a in ins],
+        in_specs=in_specs,
         out_specs=[VMEM for _ in outs],
         scratch_shapes=list(scratch),
         compiler_params=PARAMS,
@@ -81,16 +88,27 @@
     return [(r, m, m + t) for r, m, t in zip(groups, middle, total)]
 
 
-def sections_body(n_group, me, left, own, right, table, weight, third_out, *rest):
-    pieces, (frame, first, second, tables, weights) = rest[:n_group], rest[n_group:]
+def pack_body(own, table, weight, out):
+    slab = own.shape[0]
+    near = table.shape[0]
+    out[0:slab, :] = own[...]
+    out[slab : slab + near, :] = table[...].astype(F32)
+    out[slab + near :, :] = weight[...]
+
+
+def sections_body(
+    me, place, outer, inner, own, table, weight, third_out, leaving, staying,
+    frame, first, second, tables, weights,
+):
     slab, tile = own.shape
     near = table.shape[0]
-    cols = tile // n_group
-    for t, packed in ((0, left), (2, right)):
-        at = slice(t * tile, (t + 1) * tile)
+    cols = leaving.shape[2]
+    odd = place[0] & 1
+    for side, packed in ((odd, outer), (1 - odd, inner)):
+        at = pl.ds(pl.multiple_of(side * (2 * tile), LANES), tile)
         frame[:, at] = packed[0:slab, :]
-        tables[t] = packed[slab : slab + near, :].astype(jnp.int32)
-        weights[t] = packed[slab + near : slab + 2 * near, :]
+        tables[side * 2] = packed[slab : slab + near, :].astype(jnp.int32)
+        weights[side * 2] = packed[slab + near : slab + 2 * near, :]
     frame[:, tile : 2 * tile] = own[...]
     tables[1] = table[...]
     weights[1] = weight[...]
@@ -116,11 +134,10 @@
     run(frame, 0, 3 * HW, put_first)
     run(first, 0, 2 * HW, put_second)
     run(second, 0, HW, put_third)
-    mine = me[0]
-    for s in range(n_group):
-        goal = lax.rem(mine + s, n_group)
-        lo = pl.multiple_of(HW + goal * cols, LANES)
-        pieces[s][...] = third_out[:, pl.ds(lo, cols)].astype(BF16)
+    for out, bits in ((leaving, (1, 3)), (staying, (0, 2))):
+        for n, bit in enumerate(bits):
+            lo = pl.multiple_of(HW + (me[0] ^ bit) * cols, LANES)
+            out[n] = third_out[:, pl.ds(lo, cols)].astype(BF16)
 
 
 def closing_body(third, table, weight, out):
@@ -128,6 +145,41 @@
     for at in range(0, tile, LANES):
         for r, _, value in diffused(third, -HW, table, weight, at, at):
             out[r : r + SUBS, at : at + LANES] = value
+
+
+def gas_cut_body(me, species, leaving):
+    cols = leaving.shape[3]
+    for n, bit in enumerate((2, 3)):
+        leaving[n] = species[:, :, pl.ds(pl.multiple_of((me[0] ^ bit) * cols, LANES), cols)]
+
+
+def gas_turn_body(me, species, arrived, passing):
+    cols = passing.shape[3]
+    passing[0] = species[:, :, pl.ds(pl.multiple_of((me[0] ^ 1) * cols, LANES), cols)]
+    passing[1] = arrived[1]
+
+
+def turned_over(matrix):
+    return matrix.astype(F32).T
+
+
+def weights_body(
+    w1, b1, w2, wd, wf, v1, c1, v2, vd, flux,
+    w1_out, b1_out, w2_out, heads_out, v1_out, c1_out, v2_out, vd_out, flux_out,
+):
+    for weight, out in ((w1, w1_out), (w2, w2_out), (v1, v1_out), (v2, v2_out)):
+        out[...] = (0.5 * turned_over(weight[...])).astype(BF16)
+    gpts = wd.shape[1]
+    heads_out[0:gpts, :] = turned_over(wd[...]).astype(BF16)
+    heads_out[gpts:, :] = turned_over(wf[...]).astype(BF16)
+    vd_out[...] = turned_over(vd[...]).astype(BF16)
+    for row, out, scale in ((b1, b1_out, 0.5), (c1, c1_out, 0.5), (flux, flux_out, 1.0)):
+        out[...] = scale * jnp.broadcast_to(row[...], (LANES, row.shape[1])).T
+
+
+def turn_body(staying, arrived, passing):
+    passing[0] = staying[1]
+    passing[1] = arrived[1]
 
 
 def one_hots(listing, count):
@@ -143,20 +195,26 @@
 
 
 def gas_join_body(
-    me, count, gathered, listing, zenith, packed, outgoing, kept_x, kept_cos, slot_of, spread
+    me, count, species, near, far, listing, zenith,
+    packed, outgoing, kept_x, kept_cos, slot_of, spread,
 ):
-    n_group, gases, slab, _ = gathered.shape
+    gases, slab, _ = species.shape
     cols = packed.shape[2]
     half = cols // 2
     spread[...] = jnp.zeros_like(spread)
-    for s in range(n_group):
+    for bit in range(4):
+        source = me[0] ^ bit
         for lo in range(0, cols, LANES):
-            at = pl.multiple_of(me[0] * cols + lo, LANES)
             for f in range(gases):
-                value = gathered[s, f, :, pl.ds(at, LANES)]
+                if bit == 0:
+                    value = species[f, :, pl.ds(pl.multiple_of(me[0] * cols + lo, LANES), LANES)]
+                elif bit == 2:
+                    value = near[0, f, :, lo : lo + LANES]
+                else:
+                    value = far[bit // 2, f, :, lo : lo + LANES]
                 spread[(f + 1) * slab : (f + 2) * slab, :] = value.astype(F32)
             for l in range(slab):
-                packed[s * slab + l, :, lo : lo + LANES] = spread[pl.ds(l, SUBS, stride=slab), :]
+                packed[source * slab + l, :, lo : lo + LANES] = spread[pl.ds(l, SUBS, stride=slab), :]
     hit_first, hit_last, kept, sent = one_hots(listing, count[0, 0])
     levels = packed.shape[0]
     flat = packed[...].reshape(levels * SUBS, cols).astype(BF16)
@@ -174,13 +232,14 @@
     slot_of[...] = found[0:SUBS].astype(jnp.int32)
 
 
-def warm_join_body(n_group, me, count, *rest):
-    pieces, (listing, warm, outgoing, kept_warm) = rest[:n_group], rest[n_group:]
-    slab = pieces[0].shape[0]
-    for s in range(n_group):
-        source = lax.rem(me[0] + n_group - s, n_group)
-        lo = pl.multiple_of(source * slab, SUBS)
-        warm[pl.ds(lo, slab), :] = pieces[s][...].astype(F32)
+def sources(me, staying, near, far):
+    return ((me, staying[0]), (me ^ 1, near[0]), (me ^ 2, far[0]), (me ^ 3, far[1]))
+
+
+def warm_join_body(me, count, staying, near, far, listing, warm, outgoing, kept_warm):
+    slab = staying.shape[1]
+    for source, piece in sources(me[0], staying, near, far):
+        warm[pl.ds(pl.multiple_of(source * slab, SUBS), slab), :] = piece.astype(F32)
     _, _, kept, sent = one_hots(listing, count[0, 0])
     flat = warm[...].astype(BF16)
     outgoing[...] = mm(flat, sent).astype(BF16)
@@ -197,40 +256,39 @@
     top = iota((SUBS, LANES), 0) == 0
     wide = STEP_LEVELS * LANES
     rows = heads.shape[0]
-    row_cut = rows // (4 if both else 2)
+    row_cut = rows // (8 if both else 4)
+    units = first.shape[0]
+    unit_cut = units // 2
 
     def first_tasks(pair, odd, out):
         pair = jnp.minimum(pair, steps // 2 - 1)
 
-        def task(lo):
+        def task(r):
             warm = warm_at(pl.multiple_of(pair * SUBS, SUBS))
             tiles = []
-            for at in range(lo, lo + TILE, LANES):
-                i = odd * STEP_LEVELS + at // LANES
+            for i in range(odd * STEP_LEVELS, (odd + 1) * STEP_LEVELS):
                 row = jnp.broadcast_to(warm[i : i + 1], (SUBS, LANES))
                 tiles.append(jnp.where(top, row, x_at(pair * SUBS + i)))
             x = jnp.concatenate(tiles, axis=1).astype(BF16)
-            v = mm(first[...], x) + bias[...]
-            out[:, lo : lo + TILE] = (v + v * jnp.tanh(v)).astype(BF16)
-
-        return [functools.partial(task, lo) for lo in range(0, wide, TILE)]
+            v = mm(first[r : r + unit_cut, :], x)
+            shift = bias[r : r + unit_cut, :]
+            v = v + jnp.concatenate([shift] * STEP_LEVELS, axis=1)
+            out[r : r + unit_cut, :] = (v + v * jnp.tanh(v)).astype(BF16)
+
+        return [functools.partial(task, r) for r in range(0, units, unit_cut)]
 
     def second_tasks(one, out):
-        def task(lo):
-            v = mm(second[...], one[:, lo : lo + TILE])
-            out[:, lo : lo + TILE] = (v + v * jnp.tanh(v)).astype(BF16)
-
-        return [functools.partial(task, lo) for lo in range(0, wide, TILE)]
+        def task(r):
+            v = mm(second[r : r + unit_cut, :], one[...])
+            out[r : r + unit_cut, :] = (v + v * jnp.tanh(v)).astype(BF16)
+
+        return [functools.partial(task, r) for r in range(0, units, unit_cut)]
 
     def optics_tasks(hid, out):
-        def task(lo, r):
-            out[r : r + row_cut, lo : lo + TILE] = mm(heads[r : r + row_cut, :], hid[:, lo : lo + TILE])
-
-        return [
-            functools.partial(task, lo, r)
-            for lo in range(0, wide, TILE)
-            for r in range(0, rows, row_cut)
-        ]
+        def task(r):
+            out[r : r + row_cut, :] = mm(heads[r : r + row_cut, :], hid[...])
+
+        return [functools.partial(task, r) for r in range(0, rows, row_cut)]
 
     def consume_tasks(t, z, total):
         def task(lo):
@@ -338,7 +396,7 @@
     work_warm[...] = kept_warm[...] + mm(in_warm[...], placed)
     cosine = kept_cos[...] + mm(in_x[cells:, :], placed)[0:SUBS]
     cosine = jnp.where(cosine > 0.0, cosine, 1.0)
-    buffers[6][...] = jnp.broadcast_to(flux[...], buffers[6].shape)
+    buffers[6][...] = flux[...]
     emitted = sweep(
         lambda l: work_x[pl.ds(pl.multiple_of(l * SUBS, SUBS), SUBS), :],
         lambda l: work_warm[pl.ds(l, SUBS), :],
@@ -348,13 +406,12 @@
 
 
 def finish_body(
-    n_group, me, count, packed, warm, first, bias, second, heads, long_first, work, partner, slot_of,
-    *rest
+    me, count, packed, warm, first, bias, second, heads, long_first, work, partner, slot_of,
+    leaving, staying, heat, *buffers
 ):
-    pieces, heat, buffers = rest[:n_group], rest[n_group], rest[n_group + 1 :]
     levels, cols = heat.shape
     half = cols // 2
-    slab = pieces[0].shape[0]
+    slab = leaving.shape[1]
     sunlit = count[0, 0]
     long_last = longwave_part(half, packed, warm, first, bias, second, heads, buffers)
     for lo, long in ((0, long_first[...]), (half, long_last)):
@@ -367,18 +424,16 @@
             far = lane_take(partner[r : r + SUBS, :], place)
             short = jnp.where(lit, jnp.where(here, near, far), 0.0)
             heat[r : r + SUBS, lo : lo + half] = long[r : r + SUBS] + short
-    for s in range(n_group):
-        goal = lax.rem(me[0] + s, n_group)
-        pieces[s][...] = heat[pl.ds(pl.multiple_of(goal * slab, SUBS), slab), :]
-
-
-def add_body(n_group, me, closed, *rest):
-    pieces, out = rest[:n_group], rest[n_group]
-    cols = pieces[0].shape[1]
-    for s in range(n_group):
-        source = lax.rem(me[0] + n_group - s, n_group)
+    for out, bits in ((leaving, (1, 3)), (staying, (0, 2))):
+        for n, bit in enumerate(bits):
+            out[n] = heat[pl.ds(pl.multiple_of((me[0] ^ bit) * slab, SUBS), slab), :]
+
+
+def add_body(me, closed, staying, near, far, out):
+    cols = staying.shape[2]
+    for source, piece in sources(me[0], staying, near, far):
         at = pl.ds(pl.multiple_of(source * cols, LANES), cols)
-        out[:, at] = closed[:, at] + pieces[s][...]
+        out[:, at] = closed[:, at] + piece
 
 
 def per_device(
@@ -388,48 +443,77 @@
 ):
     n_group = lax.axis_size("group")
     n_tile = lax.axis_size("tile")
+    assert n_group == 4 and n_tile % 2 == 0
     me = lax.axis_index("group").astype(jnp.int32).reshape(1)
+    place = lax.axis_index("tile").astype(jnp.int32).reshape(1)
     slab, tile = potential.shape
+    gases = species.shape[0]
     cols = tile // n_group
     half = cols // 2
     levels = slab * n_group
-
-    def turned(value, by):
-        return lax.ppermute(value, "tile", [(i, (i + by) % n_tile) for i in range(n_tile)])
-
-    def along(value, by):
-        return lax.ppermute(value, "group", [(i, (i + by) % n_group) for i in range(n_group)])
+    hid = lw_first.shape[1]
+    lw_gpts = lw_depth.shape[1]
+    sw_gpts = sw_depth.shape[1]
+
+    def outward(value):
+        across = [(i, (i + 1 if i % 2 else i - 1) % n_tile) for i in range(n_tile)]
+        return lax.ppermute(value, "tile", across)
 
     def paired(value):
         return lax.ppermute(value, "tile", [(i, i ^ 1) for i in range(n_tile)])
 
-    framing = jnp.concatenate([potential, neighbours.astype(F32), diffusion], axis=0)
-    left = turned(framing, 1)
-    right = turned(framing, -1)
-    gathered = lax.all_gather(species, "group")
-
-    lw_one = (0.5 * lw_first).T
-    lw_two = (0.5 * lw_second).T
-    lw_heads = jnp.concatenate([lw_depth, lw_fraction], axis=1).T
-    lw_shift = (0.5 * lw_bias)[:, None]
-    sw_one = (0.5 * sw_first).T
-    sw_two = (0.5 * sw_second).T
-    sw_heads = sw_depth.T
-    sw_shift = (0.5 * sw_bias)[:, None]
-    flux = solar_flux[:, None]
-    hid = lw_first.shape[1]
-    long_weights = [lw_one, lw_shift, lw_two, lw_heads]
-    short_weights = [sw_one, sw_shift, sw_two, sw_heads, flux]
-
-    third, *warm_cuts = call(
-        functools.partial(sections_body, n_group),
-        [shaped((slab, tile + 2 * HW), F32)] + [shaped((slab, cols), BF16)] * n_group,
-        [me, left, potential, right, neighbours, diffusion],
+    def swapped(value, bit):
+        return lax.ppermute(value, "group", [(i, i ^ bit) for i in range(n_group)])
+
+    near = neighbours.shape[0]
+    (framing,) = call(
+        pack_body,
+        [shaped((slab + 2 * near, tile), F32)],
+        [potential, neighbours, diffusion],
+    )
+    outer = outward(framing)
+    inner = paired(framing)
+
+    gas_pair = shaped((2, gases, slab, cols), BF16)
+    (gas_leaving,) = call(gas_cut_body, [gas_pair], [me, species], after=inner)
+    gas_near = swapped(gas_leaving, 2)
+
+    warm_pair = shaped((2, slab, cols), BF16)
+    third, warm_leaving, warm_staying = call(
+        sections_body,
+        [shaped((slab, tile + 2 * HW), F32), warm_pair, warm_pair],
+        [me, place, outer, inner, potential, neighbours, diffusion],
         [pltpu.VMEM((slab, 3 * tile), F32)] * 3
         + [pltpu.VMEM((3, *neighbours.shape), jnp.int32), pltpu.VMEM((3, *diffusion.shape), F32)],
         flops=10_000_000,
     )
-    warm_pieces = [warm_cuts[0]] + [along(c, s + 1) for s, c in enumerate(warm_cuts[1:])]
+    warm_near = swapped(warm_leaving, 1)
+    (gas_passing,) = call(gas_turn_body, [gas_pair], [me, species, gas_near], after=warm_leaving)
+    gas_far = swapped(gas_passing, 1)
+    (warm_passing,) = call(turn_body, [warm_pair], [warm_staying, warm_near])
+    warm_far = swapped(warm_passing, 2)
+
+    lw_one, lw_shift, lw_two, lw_heads, sw_one, sw_shift, sw_two, sw_heads, flux = call(
+        weights_body,
+        [
+            shaped(lw_first.shape[::-1], BF16),
+            shaped((hid, LANES), F32),
+            shaped(lw_second.shape[::-1], BF16),
+            shaped((2 * lw_gpts, hid), BF16),
+            shaped(sw_first.shape[::-1], BF16),
+            shaped((hid, LANES), F32),
+            shaped(sw_second.shape[::-1], BF16),
+            shaped((sw_gpts, hid), BF16),
+            shaped((sw_gpts, LANES), F32),
+        ],
+        [
+            lw_first, lw_bias[None], lw_second, lw_depth, lw_fraction,
+            sw_first, sw_bias[None], sw_second, sw_depth, solar_flux[None],
+        ],
+        after=warm_passing,
+    )
+    long_weights = [lw_one, lw_shift, lw_two, lw_heads]
+    short_weights = [sw_one, sw_shift, sw_two, sw_heads, flux]
 
     packed, out_x, kept_x, kept_cos, slot_of = call(
         gas_join_body,
@@ -440,7 +524,7 @@
             shaped((SUBS, half), F32),
             shaped((SUBS, cols), jnp.int32),
         ],
-        [me, day_count, gathered, listing, zenith],
+        [me, day_count, species, gas_near, gas_far, listing, zenith],
         [pltpu.VMEM((SUBS * slab, LANES), F32)],
     )
     in_x = paired(out_x)
@@ -450,13 +534,13 @@
     )
 
     warm, out_warm, kept_warm = call(
-        functools.partial(warm_join_body, n_group),
+        warm_join_body,
         [
             shaped((levels, cols), F32),
             shaped((levels, half), BF16),
             shaped((levels, half), F32),
         ],
-        [me, day_count, *warm_pieces, listing],
+        [me, day_count, warm_staying, warm_near, warm_far, listing],
     )
     in_warm = paired(out_warm)
 
@@ -482,19 +566,22 @@
         trans=3 * lw_cells * sw_rows,
     )
     partner = paired(work)
-    heat_cuts = call(
-        functools.partial(finish_body, n_group),
-        [shaped((slab, cols), F32)] * n_group,
+    heat_pair = shaped((2, slab, cols), F32)
+    heat_leaving, heat_staying = call(
+        finish_body,
+        [heat_pair, heat_pair],
         [me, day_count, packed, warm, *long_weights, long_first, work, partner, slot_of],
         [pltpu.VMEM((levels, cols), F32)] + lw_scratch,
         flops=2 * lw_cells * hid * lw_rows,
         trans=5 * lw_cells * lw_rows // 2,
     )
-    heat_pieces = [heat_cuts[0]] + [along(c, s + 1) for s, c in enumerate(heat_cuts[1:])]
+    heat_near = swapped(heat_leaving, 1)
+    (heat_passing,) = call(turn_body, [heat_pair], [heat_staying, heat_near])
+    heat_far = swapped(heat_passing, 2)
     (evolved,) = call(
-        functools.partial(add_body, n_group),
+        add_body,
         [shaped((slab, tile), F32)],
-        [me, closed, *heat_pieces],
+        [me, closed, heat_staying, heat_near, heat_far],
     )
     return evolved
 

time: 75.8 us -> 68 us (0.90)
  blocking collectives: 22.3 us -> 0 us
  waiting for transfers between devices: 3.91 us -> 21.1 us
  other arithmetic: 1.64 us -> 0 us
    all_gather x1 -> x0, blocking collectives: 22.3 us -> none  [per_device(): gathered = lax.all_gather(species, 'group')]
    ppermute x8 -> x7, waiting for transfers between devices: 3.91 us -> 19.9 us  [the longest x6 16 us: swapped(): return lax.ppermute(value, 'group', [(i, i ^ bit) for i in range(n_group)])]
    ppermute x3 -> x4, waiting for transfers between devices: 0.01 us -> 1.18 us  [paired(): return lax.ppermute(value, 'tile', [(i, i ^ 1) for i in range(n_tile)])]
    ppermute x8 -> x7, starting transfers between devices: 11.8 us -> 10.9 us  [the longest x6 9.02 us: swapped(): return lax.ppermute(value, 'group', [(i, i ^ bit) for i in range(n_group)])]
    concatenate x1 -> x0, other arithmetic: 0.85 us -> none  [per_device(): jnp.concatenate([potential, neighbours.astype(F32), diffusion], axis=0)]
    pallas_call x8 -> x14, Pallas kernels: 29.5 us -> 29.8 us  [call(): pl.pallas_call(body, out_shape=outs, in_specs=in_specs, out_specs=[VMEM f...]
    unnamed x35 -> x40, local copies, waits for them, and re-layouts: 4.02 us -> 3.89 us
  transfers between devices with their start and end apart: 11 -> 11, of which waited for: 5 -> 8; matrix products, arithmetic and copies ran while one was open for 1% -> 0% of each run, Pallas kernels for 17% -> 19%
where the time goes in v3:
time: 68 us; the launch traced here: 67.6 us
  Pallas kernels  29.8 us (44%)
  waiting for transfers between devices  21.1 us (31%)
  starting transfers between devices  11.9 us (18%)
  local copies, waits for them, and re-layouts  3.89 us (6%)
  between operations  0.89 us (1%)
    pallas_call x14, Pallas kernels, call(): pl.pallas_call(body, out_shape=outs, in_specs=in_specs, out_specs=[VMEM f...  29.8 us
    ppermute x6, waiting for transfers between devices, swapped(): return lax.ppermute(value, 'group', [(i, i ^ bit) for i in range(n_group)])  16 us
    ppermute x6, starting transfers between devices, swapped(): return lax.ppermute(value, 'group', [(i, i ^ bit) for i in range(n_group)])  9.02 us
    ppermute x1, waiting for transfers between devices, outward(): return lax.ppermute(value, 'tile', across)  3.96 us
    unnamed x40, local copies, waits for them, and re-layouts  3.89 us
    ppermute x1, starting transfers between devices, outward(): return lax.ppermute(value, 'tile', across)  1.92 us
  transfers between devices with their start and end apart: 11, of which 8 were waited for; matrix products, arithmetic and copies ran while one was open for 0% of the time, Pallas kernels for 19%

profile of v3, /device:TPU:0, one launch (start us, length us, event | category | flops | bytes accessed | tf_op | source)
XLA Modules:
  0.0 67.6 jit_solution(5322967383291293178)
XLA Ops:
  0.0 0.8 %copy-done.2 = f32[16,1024]{1,0:T(8,128)S(1)} copy-done((f32[16,1024]{1,0:T(8,128)S(1)}, f32[16,1024]{1,0:T(8,128)}, u32[]{:S(2)}) %copy-start.2) | copy-done | bytes 65560
  0.8 0.7 %copy-done.4 = s32[4,1024]{1,0:T(4,128)S(1)} copy-done((s32[4,1024]{1,0:T(4,128)S(1)}, s32[4,1024]{1,0:T(4,128)}, u32[]{:S(2)}) %copy-start.4) | copy-done | bytes 16408
  1.6 0.7 %copy-done.6 = f32[4,1024]{1,0:T(4,128)S(1)} copy-done((f32[4,1024]{1,0:T(4,128)S(1)}, f32[4,1024]{1,0:T(4,128)}, u32[]{:S(2)}) %copy-start.6) | copy-done | bytes 16408
  2.3 0.5 collective-permute-start.1
  2.8 0.9 %collective-permute-done.1.inner._ = f32[24,1024]{1,0:T(8,128)S(1)} collective-permute-done((f32[24,1024]{1,0:T(8,128)S(1)}, f32[24,1024]{1,0:T(8,128)S(1)}, u32[]{:S(2)}, u32[]{:S(2)}) %collective-permute-start.1) | collective-permute-done | bytes 98336 | tf_op jit(solution)/shard_map/ppermute | solution.py:463
  3.8 0.9 %copy-done = bf16[7,16,1024]{2,1,0:T(8,128)(2,1)S(1)} copy-done((bf16[7,16,1024]{2,1,0:T(8,128)(2,1)S(1)}, bf16[7,16,1024]{2,1,0:T(8,128)(2,1)}, u32[]{:S(2)}) %copy-start) | copy-done | bytes 229400
  4.7 0.0 copy-start.1
  4.7 4.0 %collective-permute-start.2 = (bf16[2,7,16,256]{3,2,1,0:T(8,128)(2,1)S(1)}, bf16[2,7,16,256]{3,2,1,0:T(8,128)(2,1)S(1)}, u32[]{:S(2)}, u32[]{:S(2)}) collective-permute-start(bf16[2,7,16,256]{3,2,1,0:T(8,128)(2,1)S(1)} %shard_map.166), channel_id=1, source_target_pairs={{0,16},{8,24},{16,0},{24,8},{1,17},{9,25},{17,1},{25,9},{2,18},{10... | collective-permute-start | bytes 344072 | tf_op jit(solution)/shard_map/ppermute | solution.py:466
  8.7 1.9 %collective-permute-start = (f32[24,1024]{1,0:T(8,128)S(1)}, f32[24,1024]{1,0:T(8,128)S(1)}, u32[]{:S(2)}, u32[]{:S(2)}) collective-permute-start(f32[24,1024]{1,0:T(8,128)S(1)} %shard_map.163), channel_id=1, source_target_pairs={{0,7},{1,2},{2,1},{3,4},{4,3},{5,6},{6,5},{7,0},{8,15},{9,10},{10,... | collective-permute-start | bytes 294920 | tf_op jit(solution)/shard_map/ppermute | solution.py:460
  10.7 4.0 %collective-permute-done.outer = f32[24,1024]{1,0:T(8,128)S(1)} collective-permute-done((f32[24,1024]{1,0:T(8,128)S(1)}, f32[24,1024]{1,0:T(8,128)S(1)}, u32[]{:S(2)}, u32[]{:S(2)}) %collective-permute-start) | collective-permute-done | bytes 98336 | tf_op jit(solution)/shard_map/ppermute | solution.py:460
  14.6 0.0 copy-done.3
  14.6 0.0 copy-done.5
  14.6 2.7 %shard_map.164 = (f32[16,1536]{1,0:T(8,128)S(1)}, bf16[2,16,256]{2,1,0:T(8,128)(2,1)S(1)}, bf16[2,16,256]{2,1,0:T(8,128)(2,1)S(1)}) custom-call(s32[1]{0:T(128)} %bitcast.me.refs_0_, s32[1]{0:T(128)} %bitcast.1.place, f32[24,1024]{1,0:T(8,128)S(1)} %collective-permute-done.outer, f32[24,1024]{1,0:T(8,128)S(1)} %collective-permute-done.1.inner._, ...), custom_call_target="tpu_custom_call" | custom-call | flops 10000000 | bytes 425992 | tf_op jit(solution)/shard_map/pallas_call | solution.py:36
  17.4 0.0 collective-permute-done.2.refs_2_.near
  17.4 0.0 copy-start.16
  17.4 0.0 copy-start.13
  17.5 1.6 %collective-permute-start.3 = (bf16[2,7,16,256]{3,2,1,0:T(8,128)(2,1)S(1)}, bf16[2,7,16,256]{3,2,1,0:T(8,128)(2,1)S(1)}, u32[]{:S(2)}, u32[]{:S(2)}) collective-permute-start(bf16[2,7,16,256]{3,2,1,0:T(8,128)(2,1)S(1)} %shard_map.167), channel_id=1, source_target_pairs={{0,8},{8,0},{16,24},{24,16},{1,9},{9,1},{17,25},{25,17},{2,10},{10... | collective-permute-start | bytes 344072 | tf_op jit(solution)/shard_map/ppermute | solution.py:466
  19.7 2.6 %collective-permute-done.3.far = bf16[2,7,16,256]{3,2,1,0:T(8,128)(2,1)S(1)} collective-permute-done((bf16[2,7,16,256]{3,2,1,0:T(8,128)(2,1)S(1)}, bf16[2,7,16,256]{3,2,1,0:T(8,128)(2,1)S(1)}, u32[]{:S(2)}, u32[]{:S(2)}) %collective-permute-start.3) | collective-permute-done | bytes 114720 | tf_op jit(solution)/shard_map/ppermute | solution.py:466
  22.3 0.5 shard_map.168
  22.8 0.1 collective-permute-start.6
  22.9 1.6 %collective-permute-start.4 = (bf16[2,16,256]{2,1,0:T(8,128)(2,1)S(1)}, bf16[2,16,256]{2,1,0:T(8,128)(2,1)S(1)}, u32[]{:S(2)}, u32[]{:S(2)}) collective-permute-start(bf16[2,16,256]{2,1,0:T(8,128)(2,1)S(1)} %get-tuple-element.28._), channel_id=1, source_target_pairs={{0,8},{8,0},{16,24},{24,16},{1,9},{9,1},{17,25},{25,17},{2,10},{10... | collective-permute-start | bytes 49160 | tf_op jit(solution)/shard_map/ppermute | solution.py:466
  24.5 2.2 %collective-permute-done.4.arrived.near = bf16[2,16,256]{2,1,0:T(8,128)(2,1)S(1)} collective-permute-done((bf16[2,16,256]{2,1,0:T(8,128)(2,1)S(1)}, bf16[2,16,256]{2,1,0:T(8,128)(2,1)S(1)}, u32[]{:S(2)}, u32[]{:S(2)}) %collective-permute-start.4) | collective-permute-done | bytes 16416 | tf_op jit(solution)/shard_map/ppermute | solution.py:466
  26.7 0.1 collective-permute-start.5
  26.8 4.6 %collective-permute-done.5.far = bf16[2,16,256]{2,1,0:T(8,128)(2,1)S(1)} collective-permute-done((bf16[2,16,256]{2,1,0:T(8,128)(2,1)S(1)}, bf16[2,16,256]{2,1,0:T(8,128)(2,1)S(1)}, u32[]{:S(2)}, u32[]{:S(2)}) %collective-permute-start.5) | collective-permute-done | bytes 16416 | tf_op jit(solution)/shard_map/ppermute | solution.py:466
  31.4 0.1 shard_map.170
  31.6 0.1 collective-permute-start.7
  31.7 0.0 copy-start.15
  31.7 0.0 copy-start.14
  31.7 0.0 copy-start.17
  31.7 0.0 copy-start.18
  31.8 0.3 copy-done.19
  32.1 0.3 copy-done.15
  32.3 0.0 copy-done.14
  32.4 0.0 copy-done.17
  32.4 0.2 shard_map.171
  32.6 0.2 collective-permute-done.7.in_warm
  32.8 0.0 collective-permute-done.6.in_x
  32.8 6.4 %shard_map.173.work = f32[64,128]{1,0:T(8,128)S(1)} custom-call(s32[1,1]{1,0:T(1,128)S(6)} %copy.18.count, f32[512,128]{1,0:T(8,128)S(1)} %get-tuple-element.36.kept_x, f32[64,128]{1,0:T(8,128)S(1)} %get-tuple-element.37.kept_warm, f32[8,128]{1,0:T(8,128)S(1)} %get-tuple-element.38.kept_cos, bf16[528,128]{1,0:T(8,128)(2,1)S(1)} %collective-permute-done.6.in_x, ...), custom_call_target="tpu_custom_call" | custom-call | flops 234881024 | bytes 668676 | tf_op jit(solution)/shard_map/pallas_call | solution.py:36
  39.2 0.3 collective-permute-start.8
  39.6 9.3 %shard_map.172.long_first = f32[64,128]{1,0:T(8,128)S(1)} custom-call(f32[64,8,256]{2,1,0:T(8,128)S(1)} %get-tuple-element.29.packed, f32[64,256]{1,0:T(8,128)S(1)} %get-tuple-element.31.warm, bf16[64,8]{1,0:T(8,128)(2,1)S(1)} %get-tuple-element.32.first, f32[64,128]{1,0:T(8,128)S(1)} %get-tuple-element.33.bias, ...), custom_call_target="tpu_custom_call" | custom-call | flops 536870912 | bytes 730112 | tf_op jit(solution)/shard_map/pallas_call | solution.py:36
  48.8 0.0 collective-permute-done.8.partner
  48.8 9.4 %shard_map.174 = (f32[2,16,256]{2,1,0:T(8,128)S(1)}, f32[2,16,256]{2,1,0:T(8,128)S(1)}) custom-call(s32[1]{0:T(128)} %bitcast.me.refs_0_, s32[1,1]{1,0:T(1,128)S(6)} %copy.18.count, f32[64,8,256]{2,1,0:T(8,128)S(1)} %get-tuple-element.29.packed, f32[64,256]{1,0:T(8,128)S(1)} %get-tuple-element.31.warm, bf16[64,8]{1,0:T(8,128)(2,1)S(1)} %get-tuple-element.32.first, ...), custom_call_target="tpu_custom_call" | custom-call | flops 536870912 | bytes 869384 | tf_op jit(solution)/shard_map/pallas_call | solution.py:36
  58.2 1.7 %collective-permute-start.9 = (f32[2,16,256]{2,1,0:T(8,128)S(1)}, f32[2,16,256]{2,1,0:T(8,128)S(1)}, u32[]{:S(2)}, u32[]{:S(2)}) collective-permute-start(f32[2,16,256]{2,1,0:T(8,128)S(1)} %get-tuple-element.48), channel_id=1, source_target_pairs={{0,8},{8,0},{16,24},{24,16},{1,9},{9,1},{17,25},{25,17},{2,10},{10... | collective-permute-start | bytes 98312 | tf_op jit(solution)/shard_map/ppermute | solution.py:466
  59.9 2.3 %collective-permute-done.9.arrived.near = f32[2,16,256]{2,1,0:T(8,128)S(1)} collective-permute-done((f32[2,16,256]{2,1,0:T(8,128)S(1)}, f32[2,16,256]{2,1,0:T(8,128)S(1)}, u32[]{:S(2)}, u32[]{:S(2)}) %collective-permute-start.9) | collective-permute-done | bytes 32800 | tf_op jit(solution)/shard_map/ppermute | solution.py:466
  62.2 0.0 collective-permute-start.10
  62.2 0.5 shard_map.165.closed
  62.7 4.3 %collective-permute-done.10.far = f32[2,16,256]{2,1,0:T(8,128)S(1)} collective-permute-done((f32[2,16,256]{2,1,0:T(8,128)S(1)}, f32[2,16,256]{2,1,0:T(8,128)S(1)}, u32[]{:S(2)}, u32[]{:S(2)}) %collective-permute-start.10) | collective-permute-done | bytes 32800 | tf_op jit(solution)/shard_map/ppermute | solution.py:466
  67.0 0.6 shard_map.176
  (28 shorter events, 0.1 us)
Async XLA Ops:
  0.0 0.8 %copy-start.2 = (f32[16,1024]{1,0:T(8,128)S(1)}, f32[16,1024]{1,0:T(8,128)}, u32[]{:S(2)}) copy-start(f32[16,1024]{1,0:T(8,128)} %own.3) | copy-start | bytes 196612
  0.8 0.7 %copy-start.4 = (s32[4,1024]{1,0:T(4,128)S(1)}, s32[4,1024]{1,0:T(4,128)}, u32[]{:S(2)}) copy-start(s32[4,1024]{1,0:T(4,128)} %table.5) | copy-start | bytes 49156
  1.6 0.7 %copy-start.6 = (f32[4,1024]{1,0:T(4,128)S(1)}, f32[4,1024]{1,0:T(4,128)}, u32[]{:S(2)}) copy-start(f32[4,1024]{1,0:T(4,128)} %weight.5) | copy-start | bytes 49156
  2.3 1.5 %collective-permute-start.1 = (f32[24,1024]{1,0:T(8,128)S(1)}, f32[24,1024]{1,0:T(8,128)S(1)}, u32[]{:S(2)}, u32[]{:S(2)}) collective-permute-start(f32[24,1024]{1,0:T(8,128)S(1)} %shard_map.163), channel_id=1, source_target_pairs={{0,1},{1,0},{2,3},{3,2},{4,5},{5,4},{6,7},{7,6},{8,9},{9,8},{10,11... | collective-permute-start | bytes 294920 | tf_op jit(solution)/shard_map/ppermute | solution.py:463
  3.8 0.9 %copy-start = (bf16[7,16,1024]{2,1,0:T(8,128)(2,1)S(1)}, bf16[7,16,1024]{2,1,0:T(8,128)(2,1)}, u32[]{:S(2)}) copy-start(bf16[7,16,1024]{2,1,0:T(8,128)(2,1)} %species.1) | copy-start | bytes 688132
  4.7 9.9 %copy-start.3 = (f32[16,1024]{1,0:T(8,128)S(1)}, f32[16,1024]{1,0:T(8,128)}, u32[]{:S(2)}) copy-start(f32[16,1024]{1,0:T(8,128)} %own.3) | copy-start | bytes 196612
  4.7 9.9 %copy-start.5 = (s32[4,1024]{1,0:T(4,128)S(1)}, s32[4,1024]{1,0:T(4,128)}, u32[]{:S(2)}) copy-start(s32[4,1024]{1,0:T(4,128)} %table.5) | copy-start | bytes 49156
  4.7 9.9 %copy-start.7 = (f32[4,1024]{1,0:T(4,128)S(1)}, f32[4,1024]{1,0:T(4,128)}, u32[]{:S(2)}) copy-start(f32[4,1024]{1,0:T(4,128)} %weight.5) | copy-start | bytes 49156
  4.7 12.7 %copy-start.1 = (bf16[7,16,1024]{2,1,0:T(8,128)(2,1)S(1)}, bf16[7,16,1024]{2,1,0:T(8,128)(2,1)}, u32[]{:S(2)}) copy-start(bf16[7,16,1024]{2,1,0:T(8,128)(2,1)} %species.1) | copy-start | bytes 688132
  4.7 12.7 %collective-permute-start.2 = (bf16[2,7,16,256]{3,2,1,0:T(8,128)(2,1)S(1)}, bf16[2,7,16,256]{3,2,1,0:T(8,128)(2,1)S(1)}, u32[]{:S(2)}, u32[]{:S(2)}) collective-permute-start(bf16[2,7,16,256]{3,2,1,0:T(8,128)(2,1)S(1)} %shard_map.166), channel_id=1, source_target_pairs={{0,16},{8,24},{16,0},{24,8},{1,17},{9,25},{17,1},{25,9},{2,18},{10... | collective-permute-start | bytes 344072 | tf_op jit(solution)/shard_map/ppermute | solution.py:466
  8.7 5.9 %collective-permute-start = (f32[24,1024]{1,0:T(8,128)S(1)}, f32[24,1024]{1,0:T(8,128)S(1)}, u32[]{:S(2)}, u32[]{:S(2)}) collective-permute-start(f32[24,1024]{1,0:T(8,128)S(1)} %shard_map.163), channel_id=1, source_target_pairs={{0,7},{1,2},{2,1},{3,4},{4,3},{5,6},{6,5},{7,0},{8,15},{9,10},{10,... | collective-permute-start | bytes 294920 | tf_op jit(solution)/shard_map/ppermute | solution.py:460
  17.4 4.9 %copy-start.16 = (bf16[1,1,256]{2,1,0:T(2,128)(2,1)S(1)}, bf16[1,1,256]{2,1,0:T(2,128)(2,1)}, u32[]{:S(2)}) copy-start(bf16[1,1,256]{2,1,0:T(2,128)(2,1)} %zenith.1) | copy-start | bytes 1540
  17.4 4.9 %copy-start.13 = (s32[1,1,256]{2,1,0:T(1,128)S(1)}, s32[1,1,256]{2,1,0:T(1,128)}, u32[]{:S(2)}) copy-start(s32[1,1,256]{2,1,0:T(1,128)} %listing.3) | copy-start | bytes 3076
  17.5 4.9 %collective-permute-start.3 = (bf16[2,7,16,256]{3,2,1,0:T(8,128)(2,1)S(1)}, bf16[2,7,16,256]{3,2,1,0:T(8,128)(2,1)S(1)}, u32[]{:S(2)}, u32[]{:S(2)}) collective-permute-start(bf16[2,7,16,256]{3,2,1,0:T(8,128)(2,1)S(1)} %shard_map.167), channel_id=1, source_target_pairs={{0,8},{8,0},{16,24},{24,16},{1,9},{9,1},{17,25},{25,17},{2,10},{10... | collective-permute-start | bytes 344072 | tf_op jit(solution)/shard_map/ppermute | solution.py:466
  22.3 9.4 %copy-start.11 = (bf16[64,64]{1,0:T(8,128)(2,1)S(1)}, bf16[64,64]{1,0:T(8,128)(2,1)}, u32[]{:S(2)}) copy-start(bf16[64,64]{1,0:T(8,128)(2,1)} %refs_2_.1) | copy-start | bytes 24580
  22.3 9.4 %copy-start.12 = (bf16[64,64]{1,0:T(8,128)(2,1)S(1)}, bf16[64,64]{1,0:T(8,128)(2,1)}, u32[]{:S(2)}) copy-start(bf16[64,64]{1,0:T(8,128)(2,1)} %refs_7_.1) | copy-start | bytes 24580
  22.8 10.0 %collective-permute-start.6 = (bf16[528,128]{1,0:T(8,128)(2,1)S(1)}, bf16[528,128]{1,0:T(8,128)(2,1)S(1)}, u32[]{:S(2)}, u32[]{:S(2)}) collective-permute-start(bf16[528,128]{1,0:T(8,128)(2,1)S(1)} %get-tuple-element.39), channel_id=1, source_target_pairs={{0,1},{1,0},{2,3},{3,2},{4,5},{5,4},{6,7},{7,6},{8,9},{9,8},{10,11... | collective-permute-start | bytes 405512 | tf_op jit(solution)/shard_map/ppermute | solution.py:463
  22.9 3.8 %collective-permute-start.4 = (bf16[2,16,256]{2,1,0:T(8,128)(2,1)S(1)}, bf16[2,16,256]{2,1,0:T(8,128)(2,1)S(1)}, u32[]{:S(2)}, u32[]{:S(2)}) collective-permute-start(bf16[2,16,256]{2,1,0:T(8,128)(2,1)S(1)} %get-tuple-element.28._), channel_id=1, source_target_pairs={{0,8},{8,0},{16,24},{24,16},{1,9},{9,1},{17,25},{25,17},{2,10},{10... | collective-permute-start | bytes 49160 | tf_op jit(solution)/shard_map/ppermute | solution.py:466
  26.7 5.0 %copy-start.9 = (bf16[64,256]{1,0:T(8,128)(2,1)S(1)}, bf16[64,256]{1,0:T(8,128)(2,1)}, u32[]{:S(2)}) copy-start(bf16[64,256]{1,0:T(8,128)(2,1)} %refs_4_.1) | copy-start | bytes 98308
  26.7 5.0 %copy-start.10 = (bf16[64,224]{1,0:T(8,128)(2,1)S(1)}, bf16[64,224]{1,0:T(8,128)(2,1)}, u32[]{:S(2)}) copy-start(bf16[64,224]{1,0:T(8,128)(2,1)} %refs_8_.1) | copy-start | bytes 86020
  26.7 5.0 %copy-start.8 = (bf16[64,256]{1,0:T(8,128)(2,1)S(1)}, bf16[64,256]{1,0:T(8,128)(2,1)}, u32[]{:S(2)}) copy-start(bf16[64,256]{1,0:T(8,128)(2,1)} %refs_3_.1) | copy-start | bytes 98308
  26.7 4.7 %collective-permute-start.5 = (bf16[2,16,256]{2,1,0:T(8,128)(2,1)S(1)}, bf16[2,16,256]{2,1,0:T(8,128)(2,1)S(1)}, u32[]{:S(2)}, u32[]{:S(2)}) collective-permute-start(bf16[2,16,256]{2,1,0:T(8,128)(2,1)S(1)} %shard_map.169._), channel_id=1, source_target_pairs={{0,16},{8,24},{16,0},{24,8},{1,17},{9,25},{17,1},{25,9},{2,18},{10... | collective-permute-start | bytes 49160 | tf_op jit(solution)/shard_map/ppermute | solution.py:466
  31.4 0.7 copy-start.19
  31.6 1.2 %collective-permute-start.7 = (bf16[64,128]{1,0:T(8,128)(2,1)S(1)}, bf16[64,128]{1,0:T(8,128)(2,1)S(1)}, u32[]{:S(2)}, u32[]{:S(2)}) collective-permute-start(bf16[64,128]{1,0:T(8,128)(2,1)S(1)} %get-tuple-element.40), channel_id=1, source_target_pairs={{0,1},{1,0},{2,3},{3,2},{4,5},{5,4},{6,7},{7,6},{8,9},{9,8},{10,11... | collective-permute-start | bytes 49160 | tf_op jit(solution)/shard_map/ppermute | solution.py:463
  31.7 0.7 %copy-start.15 = (bf16[8,64]{1,0:T(8,128)(2,1)S(1)}, bf16[8,64]{1,0:T(8,128)(2,1)}, u32[]{:S(2)}) copy-start(bf16[8,64]{1,0:T(8,128)(2,1)} %refs_5_.1) | copy-start | bytes 3076
  31.7 0.7 %copy-start.14 = (bf16[8,64]{1,0:T(8,128)(2,1)S(1)}, bf16[8,64]{1,0:T(8,128)(2,1)}, u32[]{:S(2)}) copy-start(bf16[8,64]{1,0:T(8,128)(2,1)} %refs_0_.1) | copy-start | bytes 3076
  31.7 0.7 %copy-start.17 = (f32[224]{0:T(256)S(1)}, f32[224]{0:T(256)}, u32[]{:S(2)}) copy-start(f32[224]{0:T(256)} %param.33) | copy-start | bytes 2692
  31.7 0.7 %copy-start.18 = (f32[64]{0:T(128)S(1)}, f32[64]{0:T(128)}, u32[]{:S(2)}) copy-start(f32[64]{0:T(128)} %param.25) | copy-start | bytes 772
  39.2 9.6 %collective-permute-start.8 = (f32[64,128]{1,0:T(8,128)S(1)}, f32[64,128]{1,0:T(8,128)S(1)}, u32[]{:S(2)}, u32[]{:S(2)}) collective-permute-start(f32[64,128]{1,0:T(8,128)S(1)} %shard_map.173.work), channel_id=1, source_target_pairs={{0,1},{1,0},{2,3},{3,2},{4,5},{5,4},{6,7},{7,6},{8,9},{9,8},{10,11... | collective-permute-start | bytes 98312 | tf_op jit(solution)/shard_map/ppermute | solution.py:463
  58.2 4.0 %collective-permute-start.9 = (f32[2,16,256]{2,1,0:T(8,128)S(1)}, f32[2,16,256]{2,1,0:T(8,128)S(1)}, u32[]{:S(2)}, u32[]{:S(2)}) collective-permute-start(f32[2,16,256]{2,1,0:T(8,128)S(1)} %get-tuple-element.48), channel_id=1, source_target_pairs={{0,8},{8,0},{16,24},{24,16},{1,9},{9,1},{17,25},{25,17},{2,10},{10... | collective-permute-start | bytes 98312 | tf_op jit(solution)/shard_map/ppermute | solution.py:466
  62.2 4.8 %collective-permute-start.10 = (f32[2,16,256]{2,1,0:T(8,128)S(1)}, f32[2,16,256]{2,1,0:T(8,128)S(1)}, u32[]{:S(2)}, u32[]{:S(2)}) collective-permute-start(f32[2,16,256]{2,1,0:T(8,128)S(1)} %shard_map.175), channel_id=1, source_target_pairs={{0,16},{8,24},{16,0},{24,8},{1,17},{9,25},{17,1},{25,9},{2,18},{10... | collective-permute-start | bytes 98312 | tf_op jit(solution)/shard_map/ppermute | solution.py:466

commit v4 on v3

--- a/solution.py
+++ b/solution.py
@@ -16,19 +16,21 @@
 depth_scale = 0.1
 heat_scale = 12.0
 LOG2E = 1.4426950408889634
+LN2 = 0.6931471805599453
 
 F32 = jnp.float32
 BF16 = jnp.bfloat16
 VMEM = pl.BlockSpec(memory_space=pltpu.VMEM)
+ANY = pl.BlockSpec(memory_space=pl.ANY)
 SMEM = pl.BlockSpec(memory_space=pltpu.SMEM)
 PARAMS = pltpu.CompilerParams(vmem_limit_bytes=48 * 1024 * 1024)
 
 
-def call(body, outs, ins, scratch=(), flops=0, trans=0, after=None):
-    in_specs = [SMEM if a.size == 1 else VMEM for a in ins]
+def call(body, outs, ins, scratch=(), flops=0, trans=0, after=None, where=VMEM):
+    in_specs = [SMEM if a.size == 1 else where for a in ins]
     if after is not None:
         whole, ins = body, [after, *ins]
-        in_specs = [pl.BlockSpec(memory_space=pl.ANY), *in_specs]
+        in_specs = [ANY, *in_specs]
 
         def body(_, *refs):
             whole(*refs)
@@ -88,21 +90,29 @@
     return [(r, m, m + t) for r, m, t in zip(groups, middle, total)]
 
 
-def pack_body(own, table, weight, out):
+def pack_body(own, table, weight, out, table_here, weight_here, sems):
     slab = own.shape[0]
     near = table.shape[0]
-    out[0:slab, :] = own[...]
-    out[slab : slab + near, :] = table[...].astype(F32)
-    out[slab + near :, :] = weight[...]
+    moves = [
+        pltpu.make_async_copy(own, out.at[0:slab], sems.at[0]),
+        pltpu.make_async_copy(table, table_here, sems.at[1]),
+        pltpu.make_async_copy(weight, weight_here, sems.at[2]),
+    ]
+    for move in moves:
+        move.start()
+    for move in moves:
+        move.wait()
+    out[slab : slab + near, :] = table_here[...].astype(F32)
+    out[slab + near :, :] = weight_here[...]
 
 
 def sections_body(
-    me, place, outer, inner, own, table, weight, third_out, leaving, staying,
-    frame, first, second, tables, weights,
+    me, place, outer, inner, own, table, weight, third_out, *rest
 ):
+    pieces, (frame, first, second, tables, weights) = rest[:-5], rest[-5:]
     slab, tile = own.shape
     near = table.shape[0]
-    cols = leaving.shape[2]
+    cols = tile // len(pieces)
     odd = place[0] & 1
     for side, packed in ((odd, outer), (1 - odd, inner)):
         at = pl.ds(pl.multiple_of(side * (2 * tile), LANES), tile)
@@ -134,10 +144,9 @@
     run(frame, 0, 3 * HW, put_first)
     run(first, 0, 2 * HW, put_second)
     run(second, 0, HW, put_third)
-    for out, bits in ((leaving, (1, 3)), (staying, (0, 2))):
-        for n, bit in enumerate(bits):
-            lo = pl.multiple_of(HW + (me[0] ^ bit) * cols, LANES)
-            out[n] = third_out[:, pl.ds(lo, cols)].astype(BF16)
+    for bit, out in enumerate(pieces):
+        lo = pl.multiple_of(HW + (me[0] ^ bit) * cols, LANES)
+        out[...] = third_out[:, pl.ds(lo, cols)].astype(BF16)
 
 
 def closing_body(third, table, weight, out):
@@ -147,16 +156,10 @@
             out[r : r + SUBS, at : at + LANES] = value
 
 
-def gas_cut_body(me, species, leaving):
-    cols = leaving.shape[3]
-    for n, bit in enumerate((2, 3)):
-        leaving[n] = species[:, :, pl.ds(pl.multiple_of((me[0] ^ bit) * cols, LANES), cols)]
-
-
-def gas_turn_body(me, species, arrived, passing):
-    cols = passing.shape[3]
-    passing[0] = species[:, :, pl.ds(pl.multiple_of((me[0] ^ 1) * cols, LANES), cols)]
-    passing[1] = arrived[1]
+def gas_cut_body(me, species, *pieces):
+    cols = pieces[0].shape[2]
+    for bit, out in enumerate(pieces, 1):
+        out[...] = species[:, :, pl.ds(pl.multiple_of((me[0] ^ bit) * cols, LANES), cols)]
 
 
 def turned_over(matrix):
@@ -165,21 +168,21 @@
 
 def weights_body(
     w1, b1, w2, wd, wf, v1, c1, v2, vd, flux,
-    w1_out, b1_out, w2_out, heads_out, v1_out, c1_out, v2_out, vd_out, flux_out,
+    w1_out, b1_out, w2_out, heads_out, scaled_out, v1_out, c1_out, v2_out, vd_out, flux_out,
 ):
     for weight, out in ((w1, w1_out), (w2, w2_out), (v1, v1_out), (v2, v2_out)):
         out[...] = (0.5 * turned_over(weight[...])).astype(BF16)
     gpts = wd.shape[1]
     heads_out[0:gpts, :] = turned_over(wd[...]).astype(BF16)
     heads_out[gpts:, :] = turned_over(wf[...]).astype(BF16)
+    scaled = LOG2E * heads_out[...].astype(F32)
+    high = scaled.astype(BF16)
+    hid = wd.shape[0]
+    scaled_out[:, 0:hid] = high
+    scaled_out[:, hid:] = (scaled - high.astype(F32)).astype(BF16)
     vd_out[...] = turned_over(vd[...]).astype(BF16)
     for row, out, scale in ((b1, b1_out, 0.5), (c1, c1_out, 0.5), (flux, flux_out, 1.0)):
         out[...] = scale * jnp.broadcast_to(row[...], (LANES, row.shape[1])).T
-
-
-def turn_body(staying, arrived, passing):
-    passing[0] = staying[1]
-    passing[1] = arrived[1]
 
 
 def one_hots(listing, count):
@@ -195,23 +198,22 @@
 
 
 def gas_join_body(
-    me, count, species, near, far, listing, zenith,
-    packed, outgoing, kept_x, kept_cos, slot_of, spread,
+    me, count, species, *rest
 ):
+    arrived, rest = rest[:-8], rest[-8:]
+    listing, zenith, packed, outgoing, kept_x, kept_cos, slot_of, spread = rest
     gases, slab, _ = species.shape
     cols = packed.shape[2]
     half = cols // 2
     spread[...] = jnp.zeros_like(spread)
-    for bit in range(4):
+    for bit in range(len(arrived) + 1):
         source = me[0] ^ bit
         for lo in range(0, cols, LANES):
             for f in range(gases):
                 if bit == 0:
                     value = species[f, :, pl.ds(pl.multiple_of(me[0] * cols + lo, LANES), LANES)]
-                elif bit == 2:
-                    value = near[0, f, :, lo : lo + LANES]
                 else:
-                    value = far[bit // 2, f, :, lo : lo + LANES]
+                    value = arrived[bit - 1][f, :, lo : lo + LANES]
                 spread[(f + 1) * slab : (f + 2) * slab, :] = value.astype(F32)
             for l in range(slab):
                 packed[source * slab + l, :, lo : lo + LANES] = spread[pl.ds(l, SUBS, stride=slab), :]
@@ -232,14 +234,12 @@
     slot_of[...] = found[0:SUBS].astype(jnp.int32)
 
 
-def sources(me, staying, near, far):
-    return ((me, staying[0]), (me ^ 1, near[0]), (me ^ 2, far[0]), (me ^ 3, far[1]))
-
-
-def warm_join_body(me, count, staying, near, far, listing, warm, outgoing, kept_warm):
-    slab = staying.shape[1]
-    for source, piece in sources(me[0], staying, near, far):
-        warm[pl.ds(pl.multiple_of(source * slab, SUBS), slab), :] = piece.astype(F32)
+def warm_join_body(me, count, *rest):
+    pieces, (listing, warm, outgoing, kept_warm) = rest[:-4], rest[-4:]
+    slab = pieces[0].shape[0]
+    for bit, piece in enumerate(pieces):
+        at = pl.multiple_of((me[0] ^ bit) * slab, SUBS)
+        warm[pl.ds(at, slab), :] = piece[...].astype(F32)
     _, _, kept, sent = one_hots(listing, count[0, 0])
     flat = warm[...].astype(BF16)
     outgoing[...] = mm(flat, sent).astype(BF16)
@@ -250,13 +250,21 @@
     return jnp.maximum(z, jnp.log(1.0 + jnp.exp(jnp.minimum(z, 80.0))))
 
 
-def sweep(x_at, warm_at, first, bias, second, heads, gpts, rate, both, buffers, levels):
+def softplus_of_scaled(z):
+    power = jnp.exp2(jnp.minimum(z.astype(BF16), 120.0))
+    return jnp.maximum(z * LN2, jnp.log(1.0 + power.astype(F32)))
+
+
+def sweep(x_at, warm_at, first, bias, second, heads, gpts, rate, both, buffers, levels, scaled):
     one_a, one_b, hid_a, hid_b, z_a, z_b, trans, parts = buffers
     steps = levels // STEP_LEVELS
     top = iota((SUBS, LANES), 0) == 0
     wide = STEP_LEVELS * LANES
     rows = heads.shape[0]
-    row_cut = rows // (8 if both else 4)
+    row_cut = rows // (8 if both else 4) if scaled else rows
+    col_cut = wide if scaled else wide // 2
+    plus = softplus_of_scaled if scaled else softplus
+    chunk = 2 * SUBS if scaled else SUBS
     units = first.shape[0]
     unit_cut = units // 2
 
@@ -280,31 +288,40 @@
     def second_tasks(one, out):
         def task(r):
             v = mm(second[r : r + unit_cut, :], one[...])
-            out[r : r + unit_cut, :] = (v + v * jnp.tanh(v)).astype(BF16)
+            value = (v + v * jnp.tanh(v)).astype(BF16)
+            for at in range(0, out.shape[0], units):
+                out[at + r : at + r + unit_cut, :] = value
 
         return [functools.partial(task, r) for r in range(0, units, unit_cut)]
 
     def optics_tasks(hid, out):
-        def task(r):
-            out[r : r + row_cut, :] = mm(heads[r : r + row_cut, :], hid[...])
-
-        return [functools.partial(task, r) for r in range(0, rows, row_cut)]
+        def task(lo, r):
+            at = slice(lo, lo + col_cut)
+            out[r : r + row_cut, at] = mm(heads[r : r + row_cut, :], hid[:, at])
+
+        return [
+            functools.partial(task, lo, r)
+            for lo in range(0, wide, col_cut)
+            for r in range(0, rows, row_cut)
+        ]
 
     def consume_tasks(t, z, total):
         def task(lo):
-            carry = trans[lo : lo + SUBS, :]
+            carry = trans[lo : lo + chunk, :]
             for i in range(STEP_LEVELS):
                 at = i * LANES
-                depth = softplus(z[lo : lo + SUBS, at : at + LANES])
+                depth = plus(z[lo : lo + chunk, at : at + LANES])
                 following = carry * jnp.exp2(depth * rate)
                 drop = carry - following
                 if both:
-                    drop = drop * softplus(z[gpts + lo : gpts + lo + SUBS, at : at + LANES])
-                total[i] = drop if total[i] is None else total[i] + drop
+                    drop = drop * plus(z[gpts + lo : gpts + lo + chunk, at : at + LANES])
+                for r in range(0, chunk, SUBS):
+                    part = drop[r : r + SUBS]
+                    total[i] = part if total[i] is None else total[i] + part
                 carry = following
-            trans[lo : lo + SUBS, :] = carry
-
-        return [functools.partial(task, lo) for lo in range(0, gpts, SUBS)]
+            trans[lo : lo + chunk, :] = carry
+
+        return [functools.partial(task, lo) for lo in range(0, gpts, chunk)]
 
     def woven(main, side):
         done = 0
@@ -351,13 +368,13 @@
     return emitted
 
 
-def sweep_scratch(hid, rows, gpts, levels):
+def sweep_scratch(hid, depth, rows, gpts, levels):
     wide = STEP_LEVELS * LANES
     return [
         pltpu.VMEM((hid, wide), BF16),
         pltpu.VMEM((hid, wide), BF16),
-        pltpu.VMEM((hid, wide), BF16),
-        pltpu.VMEM((hid, wide), BF16),
+        pltpu.VMEM((depth, wide), BF16),
+        pltpu.VMEM((depth, wide), BF16),
         pltpu.VMEM((rows, wide), F32),
         pltpu.VMEM((rows, wide), F32),
         pltpu.VMEM((gpts, LANES), F32),
@@ -365,21 +382,21 @@
     ]
 
 
-def longwave_part(lo, packed, warm, first, bias, second, heads, buffers):
+def longwave_part(lo, packed, warm, first, bias, second, heads, buffers, scaled):
     gpts = heads.shape[0] // 2
     levels = packed.shape[0]
     buffers[6][...] = jnp.ones_like(buffers[6])
     emitted = sweep(
         lambda l: packed[l, :, lo : lo + LANES],
         lambda l: warm[pl.ds(l, SUBS), lo : lo + LANES],
-        first, bias, second, heads, gpts, -depth_scale * LOG2E, True, buffers, levels,
+        first, bias, second, heads, gpts, -depth_scale * LOG2E, True, buffers, levels, scaled,
     )
     planck = jnp.exp(0.25 * warm[:, lo : lo + LANES])
     return -(heat_scale / gpts) * planck * emitted
 
 
 def longwave_body(packed, warm, first, bias, second, heads, out, *buffers):
-    out[...] = longwave_part(0, packed, warm, first, bias, second, heads, buffers)
+    out[...] = longwave_part(0, packed, warm, first, bias, second, heads, buffers, True)
 
 
 def shortwave_body(
@@ -400,20 +417,21 @@
     emitted = sweep(
         lambda l: work_x[pl.ds(pl.multiple_of(l * SUBS, SUBS), SUBS), :],
         lambda l: work_warm[pl.ds(l, SUBS), :],
-        first, bias, second, heads, gpts, (-depth_scale * LOG2E) / cosine, False, buffers, levels,
+        first, bias, second, heads, gpts, (-depth_scale * LOG2E) / cosine, False, buffers, levels, False,
     )
     out[...] = (heat_scale / gpts) * cosine[0:1] * emitted
 
 
 def finish_body(
-    me, count, packed, warm, first, bias, second, heads, long_first, work, partner, slot_of,
-    leaving, staying, heat, *buffers
+    n_group, me, count, packed, warm, first, bias, second, heads, long_first, work, partner, slot_of,
+    *rest
 ):
+    pieces, heat, buffers = rest[:n_group], rest[n_group], rest[n_group + 1 :]
     levels, cols = heat.shape
     half = cols // 2
-    slab = leaving.shape[1]
+    slab = pieces[0].shape[0]
     sunlit = count[0, 0]
-    long_last = longwave_part(half, packed, warm, first, bias, second, heads, buffers)
+    long_last = longwave_part(half, packed, warm, first, bias, second, heads, buffers, False)
     for lo, long in ((0, long_first[...]), (half, long_last)):
         slot = slot_of[:, lo : lo + half]
         here = slot < half
@@ -424,16 +442,16 @@
             far = lane_take(partner[r : r + SUBS, :], place)
             short = jnp.where(lit, jnp.where(here, near, far), 0.0)
             heat[r : r + SUBS, lo : lo + half] = long[r : r + SUBS] + short
-    for out, bits in ((leaving, (1, 3)), (staying, (0, 2))):
-        for n, bit in enumerate(bits):
-            out[n] = heat[pl.ds(pl.multiple_of((me[0] ^ bit) * slab, SUBS), slab), :]
-
-
-def add_body(me, closed, staying, near, far, out):
-    cols = staying.shape[2]
-    for source, piece in sources(me[0], staying, near, far):
-        at = pl.ds(pl.multiple_of(source * cols, LANES), cols)
-        out[:, at] = closed[:, at] + piece
+    for bit, out in enumerate(pieces):
+        out[...] = heat[pl.ds(pl.multiple_of((me[0] ^ bit) * slab, SUBS), slab), :]
+
+
+def add_body(me, closed, *rest):
+    pieces, out = rest[:-1], rest[-1]
+    cols = pieces[0].shape[1]
+    for bit, piece in enumerate(pieces):
+        at = pl.ds(pl.multiple_of((me[0] ^ bit) * cols, LANES), cols)
+        out[:, at] = closed[:, at] + piece[...]
 
 
 def per_device(
@@ -443,7 +461,7 @@
 ):
     n_group = lax.axis_size("group")
     n_tile = lax.axis_size("tile")
-    assert n_group == 4 and n_tile % 2 == 0
+    assert n_group & (n_group - 1) == 0 and n_tile % 2 == 0
     me = lax.axis_index("group").astype(jnp.int32).reshape(1)
     place = lax.axis_index("tile").astype(jnp.int32).reshape(1)
     slab, tile = potential.shape
@@ -470,36 +488,39 @@
         pack_body,
         [shaped((slab + 2 * near, tile), F32)],
         [potential, neighbours, diffusion],
+        [
+            pltpu.VMEM(neighbours.shape, jnp.int32),
+            pltpu.VMEM(diffusion.shape, F32),
+            pltpu.SemaphoreType.DMA((3,)),
+        ],
+        where=ANY,
     )
     outer = outward(framing)
     inner = paired(framing)
 
-    gas_pair = shaped((2, gases, slab, cols), BF16)
-    (gas_leaving,) = call(gas_cut_body, [gas_pair], [me, species], after=inner)
-    gas_near = swapped(gas_leaving, 2)
-
-    warm_pair = shaped((2, slab, cols), BF16)
-    third, warm_leaving, warm_staying = call(
+    gas_cuts = call(
+        gas_cut_body, [shaped((gases, slab, cols), BF16)] * (n_group - 1), [me, species], after=framing
+    )
+    gas_arrived = [swapped(c, bit) for bit, c in enumerate(gas_cuts, 1)]
+
+    third, *warm_cuts = call(
         sections_body,
-        [shaped((slab, tile + 2 * HW), F32), warm_pair, warm_pair],
+        [shaped((slab, tile + 2 * HW), F32)] + [shaped((slab, cols), BF16)] * n_group,
         [me, place, outer, inner, potential, neighbours, diffusion],
         [pltpu.VMEM((slab, 3 * tile), F32)] * 3
         + [pltpu.VMEM((3, *neighbours.shape), jnp.int32), pltpu.VMEM((3, *diffusion.shape), F32)],
         flops=10_000_000,
     )
-    warm_near = swapped(warm_leaving, 1)
-    (gas_passing,) = call(gas_turn_body, [gas_pair], [me, species, gas_near], after=warm_leaving)
-    gas_far = swapped(gas_passing, 1)
-    (warm_passing,) = call(turn_body, [warm_pair], [warm_staying, warm_near])
-    warm_far = swapped(warm_passing, 2)
-
-    lw_one, lw_shift, lw_two, lw_heads, sw_one, sw_shift, sw_two, sw_heads, flux = call(
+    warm_pieces = [warm_cuts[0]] + [swapped(c, bit) for bit, c in enumerate(warm_cuts[1:], 1)]
+
+    lw_one, lw_shift, lw_two, lw_heads, lw_scaled, sw_one, sw_shift, sw_two, sw_heads, flux = call(
         weights_body,
         [
             shaped(lw_first.shape[::-1], BF16),
             shaped((hid, LANES), F32),
             shaped(lw_second.shape[::-1], BF16),
             shaped((2 * lw_gpts, hid), BF16),
+            shaped((2 * lw_gpts, 2 * hid), BF16),
             shaped(sw_first.shape[::-1], BF16),
             shaped((hid, LANES), F32),
             shaped(sw_second.shape[::-1], BF16),
@@ -510,9 +531,10 @@
             lw_first, lw_bias[None], lw_second, lw_depth, lw_fraction,
             sw_first, sw_bias[None], sw_second, sw_depth, solar_flux[None],
         ],
-        after=warm_passing,
+        after=third,
     )
     long_weights = [lw_one, lw_shift, lw_two, lw_heads]
+    scaled_weights = [lw_one, lw_shift, lw_two, lw_scaled]
     short_weights = [sw_one, sw_shift, sw_two, sw_heads, flux]
 
     packed, out_x, kept_x, kept_cos, slot_of = call(
@@ -524,8 +546,9 @@
             shaped((SUBS, half), F32),
             shaped((SUBS, cols), jnp.int32),
         ],
-        [me, day_count, species, gas_near, gas_far, listing, zenith],
+        [me, day_count, species, *gas_arrived, listing, zenith],
         [pltpu.VMEM((SUBS * slab, LANES), F32)],
+        after=third,
     )
     in_x = paired(out_x)
 
@@ -540,18 +563,18 @@
             shaped((levels, half), BF16),
             shaped((levels, half), F32),
         ],
-        [me, day_count, warm_staying, warm_near, warm_far, listing],
+        [me, day_count, *warm_pieces, listing],
     )
     in_warm = paired(out_warm)
 
     lw_rows = lw_heads.shape[0]
-    lw_scratch = sweep_scratch(hid, lw_rows, lw_rows // 2, levels)
+    lw_scratch = sweep_scratch(hid, hid, lw_rows, lw_rows // 2, levels)
     lw_cells = levels * half
     (long_first,) = call(
         longwave_body,
         [shaped((levels, half), F32)],
-        [packed, warm, *long_weights],
-        lw_scratch,
+        [packed, warm, *scaled_weights],
+        sweep_scratch(hid, 2 * hid, lw_rows, lw_rows // 2, levels),
         flops=2 * lw_cells * hid * lw_rows,
         trans=5 * lw_cells * lw_rows // 2,
     )
@@ -561,28 +584,21 @@
         [shaped((levels, half), F32)],
         [day_count, kept_x, kept_warm, kept_cos, in_x, in_warm, *short_weights],
         [pltpu.VMEM((levels * SUBS, half), F32), pltpu.VMEM((levels, half), F32)]
-        + sweep_scratch(hid, sw_rows, sw_rows, levels),
+        + sweep_scratch(hid, hid, sw_rows, sw_rows, levels),
         flops=2 * lw_cells * hid * sw_rows,
         trans=3 * lw_cells * sw_rows,
     )
     partner = paired(work)
-    heat_pair = shaped((2, slab, cols), F32)
-    heat_leaving, heat_staying = call(
-        finish_body,
-        [heat_pair, heat_pair],
+    heat_cuts = call(
+        functools.partial(finish_body, n_group),
+        [shaped((slab, cols), F32)] * n_group,
         [me, day_count, packed, warm, *long_weights, long_first, work, partner, slot_of],
         [pltpu.VMEM((levels, cols), F32)] + lw_scratch,
         flops=2 * lw_cells * hid * lw_rows,
         trans=5 * lw_cells * lw_rows // 2,
     )
-    heat_near = swapped(heat_leaving, 1)
-    (heat_passing,) = call(turn_body, [heat_pair], [heat_staying, heat_near])
-    heat_far = swapped(heat_passing, 2)
-    (evolved,) = call(
-        add_body,
-        [shaped((slab, tile), F32)],
-        [me, closed, heat_staying, heat_near, heat_far],
-    )
+    heat_pieces = [heat_cuts[0]] + [swapped(c, bit) for bit, c in enumerate(heat_cuts[1:], 1)]
+    (evolved,) = call(add_body, [shaped((slab, tile), F32)], [me, closed, *heat_pieces])
     return evolved
 
 

time: 68 us -> 62.1 us (0.913)
  waiting for transfers between devices: 21.1 us -> 9.03 us
  starting transfers between devices: 11.9 us -> 17.4 us
    ppermute x6 -> x9, waiting for transfers between devices: 16 us -> 8.96 us  [swapped(): return lax.ppermute(value, 'group', [(i, i ^ bit) for i in range(n_group)])]
    ppermute x6 -> x9, starting transfers between devices: 9.02 us -> 13.3 us  [swapped(): return lax.ppermute(value, 'group', [(i, i ^ bit) for i in range(n_group)])]
    ppermute x1, waiting for transfers between devices: 3.96 us -> 0.01 us  [outward(): return lax.ppermute(value, 'tile', across)]
    ppermute x1, starting transfers between devices: 1.92 us -> 3.4 us  [outward(): return lax.ppermute(value, 'tile', across)]
    ppermute x4, waiting for transfers between devices: 1.18 us -> 0.07 us  [paired(): return lax.ppermute(value, 'tile', [(i, i ^ 1) for i in range(n_tile)])]
    pallas_call x14 -> x11, Pallas kernels: 29.8 us -> 30.4 us  [call(): pl.pallas_call(body, out_shape=outs, in_specs=in_specs, out_specs=[VMEM f...]
  transfers between devices with their start and end apart: 11 -> 14, of which waited for: 8 -> 6; matrix products, arithmetic and copies ran while one was open for 0% -> 0% of each run, Pallas kernels for 19% -> 22%
where the time goes in v4:
time: 62.1 us; the launch traced here: 61.7 us
  Pallas kernels  30.4 us (49%)
  starting transfers between devices  17.4 us (28%)
  waiting for transfers between devices  9.03 us (15%)
  local copies, waits for them, and re-layouts  3.9 us (6%)
  between operations  0.97 us (2%)
    pallas_call x11, Pallas kernels, call(): pl.pallas_call(body, out_shape=outs, in_specs=in_specs, out_specs=[VMEM f...  30.4 us
    ppermute x9, starting transfers between devices, swapped(): return lax.ppermute(value, 'group', [(i, i ^ bit) for i in range(n_group)])  13.3 us
    ppermute x9, waiting for transfers between devices, swapped(): return lax.ppermute(value, 'group', [(i, i ^ bit) for i in range(n_group)])  8.96 us
    unnamed x40, local copies, waits for them, and re-layouts  3.9 us
    ppermute x1, starting transfers between devices, outward(): return lax.ppermute(value, 'tile', across)  3.4 us
  transfers between devices with their start and end apart: 14, of which 6 were waited for; matrix products, arithmetic and copies ran while one was open for 0% of the time, Pallas kernels for 22%

profile of v4, /device:TPU:0, one launch (start us, length us, event | category | flops | bytes accessed | tf_op | source)
XLA Modules:
  0.0 61.7 jit_solution(14642037539163941451)
XLA Ops:
  0.0 0.8 %copy-done.2 = f32[16,1024]{1,0:T(8,128)S(1)} copy-done((f32[16,1024]{1,0:T(8,128)S(1)}, f32[16,1024]{1,0:T(8,128)}, u32[]{:S(2)}) %copy-start.2) | copy-done | bytes 65560
  0.8 0.7 %copy-done.4 = s32[4,1024]{1,0:T(4,128)S(1)} copy-done((s32[4,1024]{1,0:T(4,128)S(1)}, s32[4,1024]{1,0:T(4,128)}, u32[]{:S(2)}) %copy-start.4) | copy-done | bytes 16408
  1.6 0.7 %copy-done.6 = f32[4,1024]{1,0:T(4,128)S(1)} copy-done((f32[4,1024]{1,0:T(4,128)S(1)}, f32[4,1024]{1,0:T(4,128)}, u32[]{:S(2)}) %copy-start.6) | copy-done | bytes 16408
  2.3 0.1 shard_map.163._
  2.4 3.4 %collective-permute-start = (f32[24,1024]{1,0:T(8,128)S(1)}, f32[24,1024]{1,0:T(8,128)S(1)}, u32[]{:S(2)}, u32[]{:S(2)}) collective-permute-start(f32[24,1024]{1,0:T(8,128)S(1)} %shard_map.163._), channel_id=1, source_target_pairs={{0,7},{1,2},{2,1},{3,4},{4,3},{5,6},{6,5},{7,0},{8,15},{9,10},{10,... | collective-permute-start | bytes 294920 | tf_op jit(solution)/shard_map/ppermute | solution.py:478
  5.8 0.0 collective-permute-start.1
  5.8 0.9 %copy-done = bf16[7,16,1024]{2,1,0:T(8,128)(2,1)S(1)} copy-done((bf16[7,16,1024]{2,1,0:T(8,128)(2,1)S(1)}, bf16[7,16,1024]{2,1,0:T(8,128)(2,1)}, u32[]{:S(2)}) %copy-start) | copy-done | bytes 229400
  6.8 0.0 copy-start.1
  6.8 1.6 %collective-permute-start.2 = (bf16[7,16,256]{2,1,0:T(8,128)(2,1)S(1)}, bf16[7,16,256]{2,1,0:T(8,128)(2,1)S(1)}, u32[]{:S(2)}, u32[]{:S(2)}) collective-permute-start(bf16[7,16,256]{2,1,0:T(8,128)(2,1)S(1)} %get-tuple-element.36), channel_id=1, source_target_pairs={{0,8},{8,0},{16,24},{24,16},{1,9},{9,1},{17,25},{25,17},{2,10},{10... | collective-permute-start | bytes 172040 | tf_op jit(solution)/shard_map/ppermute | solution.py:484
  8.4 2.6 %collective-permute-start.3 = (bf16[7,16,256]{2,1,0:T(8,128)(2,1)S(1)}, bf16[7,16,256]{2,1,0:T(8,128)(2,1)S(1)}, u32[]{:S(2)}, u32[]{:S(2)}) collective-permute-start(bf16[7,16,256]{2,1,0:T(8,128)(2,1)S(1)} %get-tuple-element.37), channel_id=1, source_target_pairs={{0,16},{8,24},{16,0},{24,8},{1,17},{9,25},{17,1},{25,9},{2,18},{10... | collective-permute-start | bytes 172040 | tf_op jit(solution)/shard_map/ppermute | solution.py:484
  11.0 0.2 collective-permute-start.4
  12.0 0.0 copy-start.16
  12.0 2.7 %shard_map.164 = (f32[16,1536]{1,0:T(8,128)S(1)}, bf16[16,256]{1,0:T(8,128)(2,1)S(1)}, bf16[16,256]{1,0:T(8,128)(2,1)S(1)}, bf16[16,256]{1,0:T(8,128)(2,1)S(1)}, bf16[16,256]{1,0:T(8,128)(2,1)S(1)}) custom-call(s32[1]{0:T(128)} %bitcast.me.refs_0_, s32[1]{0:T(128)} %bitcast.1.place, f32[24,1024]{1,0:T(8,128)S(1)} %collective-permute-done.outer, ...), custom_call_target="tpu_custom_call" | custom-call | flops 10000000 | bytes 425992 | tf_op jit(solution)/shard_map/pallas_call | solution.py:38
  14.7 0.0 copy-start.13
  14.7 0.3 collective-permute-done.3.refs_4_
  15.0 2.0 %collective-permute-done.4.refs_5_ = bf16[7,16,256]{2,1,0:T(8,128)(2,1)S(1)} collective-permute-done((bf16[7,16,256]{2,1,0:T(8,128)(2,1)S(1)}, bf16[7,16,256]{2,1,0:T(8,128)(2,1)S(1)}, u32[]{:S(2)}, u32[]{:S(2)}) %collective-permute-start.4) | collective-permute-done | bytes 57376 | tf_op jit(solution)/shard_map/ppermute | solution.py:484
  17.1 0.0 copy-start.9
  17.1 0.0 copy-start.10
  17.1 0.0 copy-start.12
  17.1 0.0 copy-start.15
  17.1 0.0 copy-start.18
  17.1 0.0 copy-start.19
  17.1 0.5 shard_map.167
  17.6 0.1 collective-permute-start.8
  17.7 0.7 %collective-permute-start.5 = (bf16[16,256]{1,0:T(8,128)(2,1)S(1)}, bf16[16,256]{1,0:T(8,128)(2,1)S(1)}, u32[]{:S(2)}, u32[]{:S(2)}) collective-permute-start(bf16[16,256]{1,0:T(8,128)(2,1)S(1)} %get-tuple-element.41), channel_id=1, source_target_pairs={{0,8},{8,0},{16,24},{24,16},{1,9},{9,1},{17,25},{25,17},{2,10},{10... | collective-permute-start | bytes 24584 | tf_op jit(solution)/shard_map/ppermute | solution.py:484
  18.5 1.8 %collective-permute-start.6 = (bf16[16,256]{1,0:T(8,128)(2,1)S(1)}, bf16[16,256]{1,0:T(8,128)(2,1)S(1)}, u32[]{:S(2)}, u32[]{:S(2)}) collective-permute-start(bf16[16,256]{1,0:T(8,128)(2,1)S(1)} %get-tuple-element.42), channel_id=1, source_target_pairs={{0,16},{8,24},{16,0},{24,8},{1,17},{9,25},{17,1},{25,9},{2,18},{10... | collective-permute-start | bytes 24584 | tf_op jit(solution)/shard_map/ppermute | solution.py:484
  20.2 1.9 %collective-permute-start.7 = (bf16[16,256]{1,0:T(8,128)(2,1)S(1)}, bf16[16,256]{1,0:T(8,128)(2,1)S(1)}, u32[]{:S(2)}, u32[]{:S(2)}) collective-permute-start(bf16[16,256]{1,0:T(8,128)(2,1)S(1)} %get-tuple-element.43), channel_id=1, source_target_pairs={{0,24},{8,16},{16,8},{24,0},{1,25},{9,17},{17,9},{25,1},{2,26},{10... | collective-permute-start | bytes 24584 | tf_op jit(solution)/shard_map/ppermute | solution.py:484
  22.2 0.9 %collective-permute-done.6.rest_2_ = bf16[16,256]{1,0:T(8,128)(2,1)S(1)} collective-permute-done((bf16[16,256]{1,0:T(8,128)(2,1)S(1)}, bf16[16,256]{1,0:T(8,128)(2,1)S(1)}, u32[]{:S(2)}, u32[]{:S(2)}) %collective-permute-start.6) | collective-permute-done | bytes 8224 | tf_op jit(solution)/shard_map/ppermute | solution.py:484
  23.1 2.6 %collective-permute-done.7.rest_3_ = bf16[16,256]{1,0:T(8,128)(2,1)S(1)} collective-permute-done((bf16[16,256]{1,0:T(8,128)(2,1)S(1)}, bf16[16,256]{1,0:T(8,128)(2,1)S(1)}, u32[]{:S(2)}, u32[]{:S(2)}) %collective-permute-start.7) | collective-permute-done | bytes 8224 | tf_op jit(solution)/shard_map/ppermute | solution.py:484
  25.7 0.1 shard_map.168
  25.9 0.1 collective-permute-start.9
  25.9 0.0 copy-start.14
  25.9 0.0 copy-start.17
  26.0 0.4 copy-done.11
  26.4 0.2 copy-done.14
  26.6 0.0 copy-done.17
  26.6 0.4 shard_map.169
  27.0 0.1 collective-permute-done.9.in_warm
  27.1 6.3 %shard_map.171.work = f32[64,128]{1,0:T(8,128)S(1)} custom-call(s32[1,1]{1,0:T(1,128)S(6)} %copy.18.refs_1_.count, f32[512,128]{1,0:T(8,128)S(1)} %get-tuple-element.50.kept_x, f32[64,128]{1,0:T(8,128)S(1)} %get-tuple-element.51.kept_warm, f32[8,128]{1,0:T(8,128)S(1)} %get-tuple-element.52.kept_cos, bf16[528,128]{1,0:T(8,128)(2,1)S(1)} %collective-permute-done.8.in_x, ...), custom_call_target="tpu_custom_call" | custom-call | flops 234881024 | bytes 668676 | tf_op jit(solution)/shard_map/pallas_call | solution.py:38
  33.4 0.5 collective-permute-start.10
  33.9 9.9 %shard_map.170.long_first = f32[64,128]{1,0:T(8,128)S(1)} custom-call(f32[64,8,256]{2,1,0:T(8,128)S(1)} %get-tuple-element.39.packed, f32[64,256]{1,0:T(8,128)S(1)} %get-tuple-element.44.warm, bf16[64,8]{1,0:T(8,128)(2,1)S(1)} %get-tuple-element.45.first, f32[64,128]{1,0:T(8,128)S(1)} %get-tuple-element.46.bias, ...), custom_call_target="tpu_custom_call" | custom-call | flops 536870912 | bytes 795648 | tf_op jit(solution)/shard_map/pallas_call | solution.py:38
  43.8 9.2 %shard_map.172 = (f32[16,256]{1,0:T(8,128)S(1)}, f32[16,256]{1,0:T(8,128)S(1)}, f32[16,256]{1,0:T(8,128)S(1)}, f32[16,256]{1,0:T(8,128)S(1)}) custom-call(s32[1]{0:T(128)} %bitcast.me.refs_0_, s32[1,1]{1,0:T(1,128)S(6)} %copy.18.refs_1_.count, f32[64,8,256]{2,1,0:T(8,128)S(1)} %get-tuple-element.39.packed, f32[64,256]{1,0:T(8,128)S(1)} %get-tuple-element.44.warm, ...), custom_call_target="tpu_custom_call" | custom-call | flops 536870912 | bytes 869384 | tf_op jit(solution)/shard_map/pallas_call | solution.py:38
  53.0 0.1 collective-permute-start.11
  53.0 2.5 %collective-permute-start.12 = (f32[16,256]{1,0:T(8,128)S(1)}, f32[16,256]{1,0:T(8,128)S(1)}, u32[]{:S(2)}, u32[]{:S(2)}) collective-permute-start(f32[16,256]{1,0:T(8,128)S(1)} %get-tuple-element.63), channel_id=1, source_target_pairs={{0,16},{8,24},{16,0},{24,8},{1,17},{9,25},{17,1},{25,9},{2,18},{10... | collective-permute-start | bytes 49160 | tf_op jit(solution)/shard_map/ppermute | solution.py:484
  55.5 1.9 %collective-permute-start.13 = (f32[16,256]{1,0:T(8,128)S(1)}, f32[16,256]{1,0:T(8,128)S(1)}, u32[]{:S(2)}, u32[]{:S(2)}) collective-permute-start(f32[16,256]{1,0:T(8,128)S(1)} %get-tuple-element.64), channel_id=1, source_target_pairs={{0,24},{8,16},{16,8},{24,0},{1,25},{9,17},{17,9},{25,1},{2,26},{10... | collective-permute-start | bytes 49160 | tf_op jit(solution)/shard_map/ppermute | solution.py:484
  57.4 0.5 shard_map.165.closed
  57.9 3.1 %collective-permute-done.13.rest_3_ = f32[16,256]{1,0:T(8,128)S(1)} collective-permute-done((f32[16,256]{1,0:T(8,128)S(1)}, f32[16,256]{1,0:T(8,128)S(1)}, u32[]{:S(2)}, u32[]{:S(2)}) %collective-permute-start.13) | collective-permute-done | bytes 16416 | tf_op jit(solution)/shard_map/ppermute | solution.py:484
  61.1 0.6 %shard_map.173 = f32[16,1024]{1,0:T(8,128)} custom-call(s32[1]{0:T(128)} %bitcast.me.refs_0_, f32[16,1024]{1,0:T(8,128)S(1)} %shard_map.165.closed, f32[16,256]{1,0:T(8,128)S(1)} %get-tuple-element.61.rest_0_, f32[16,256]{1,0:T(8,128)S(1)} %collective-permute-done.11.rest_1_, f32[16,256]{1,0:T(8,128)S(1)} %collective-permute-done.12.rest_2_, ...), custom_call_target="tpu_custom_call" | custom-call | bytes 196612 | tf_op jit(solution)/shard_map/pallas_call | solution.py:38
  (31 shorter events, 0.1 us)
Async XLA Ops:
  0.0 0.8 %copy-start.2 = (f32[16,1024]{1,0:T(8,128)S(1)}, f32[16,1024]{1,0:T(8,128)}, u32[]{:S(2)}) copy-start(f32[16,1024]{1,0:T(8,128)} %own.3) | copy-start | bytes 196612
  0.8 0.7 %copy-start.4 = (s32[4,1024]{1,0:T(4,128)S(1)}, s32[4,1024]{1,0:T(4,128)}, u32[]{:S(2)}) copy-start(s32[4,1024]{1,0:T(4,128)} %table.5) | copy-start | bytes 49156
  1.6 0.7 %copy-start.6 = (f32[4,1024]{1,0:T(4,128)S(1)}, f32[4,1024]{1,0:T(4,128)}, u32[]{:S(2)}) copy-start(f32[4,1024]{1,0:T(4,128)} %weight.5) | copy-start | bytes 49156
  2.4 9.5 %collective-permute-start = (f32[24,1024]{1,0:T(8,128)S(1)}, f32[24,1024]{1,0:T(8,128)S(1)}, u32[]{:S(2)}, u32[]{:S(2)}) collective-permute-start(f32[24,1024]{1,0:T(8,128)S(1)} %shard_map.163._), channel_id=1, source_target_pairs={{0,7},{1,2},{2,1},{3,4},{4,3},{5,6},{6,5},{7,0},{8,15},{9,10},{10,... | collective-permute-start | bytes 294920 | tf_op jit(solution)/shard_map/ppermute | solution.py:478
  5.8 6.1 %collective-permute-start.1 = (f32[24,1024]{1,0:T(8,128)S(1)}, f32[24,1024]{1,0:T(8,128)S(1)}, u32[]{:S(2)}, u32[]{:S(2)}) collective-permute-start(f32[24,1024]{1,0:T(8,128)S(1)} %shard_map.163._), channel_id=1, source_target_pairs={{0,1},{1,0},{2,3},{3,2},{4,5},{5,4},{6,7},{7,6},{8,9},{9,8},{10,11... | collective-permute-start | bytes 294920 | tf_op jit(solution)/shard_map/ppermute | solution.py:481
  5.8 0.9 %copy-start = (bf16[7,16,1024]{2,1,0:T(8,128)(2,1)S(1)}, bf16[7,16,1024]{2,1,0:T(8,128)(2,1)}, u32[]{:S(2)}) copy-start(bf16[7,16,1024]{2,1,0:T(8,128)(2,1)} %refs_2_.2) | copy-start | bytes 688132
  6.8 5.2 %copy-start.3 = (f32[16,1024]{1,0:T(8,128)S(1)}, f32[16,1024]{1,0:T(8,128)}, u32[]{:S(2)}) copy-start(f32[16,1024]{1,0:T(8,128)} %own.3) | copy-start | bytes 196612
  6.8 5.2 %copy-start.5 = (s32[4,1024]{1,0:T(4,128)S(1)}, s32[4,1024]{1,0:T(4,128)}, u32[]{:S(2)}) copy-start(s32[4,1024]{1,0:T(4,128)} %table.5) | copy-start | bytes 49156
  6.8 5.2 %copy-start.7 = (f32[4,1024]{1,0:T(4,128)S(1)}, f32[4,1024]{1,0:T(4,128)}, u32[]{:S(2)}) copy-start(f32[4,1024]{1,0:T(4,128)} %weight.5) | copy-start | bytes 49156
  6.8 10.3 %copy-start.1 = (bf16[7,16,1024]{2,1,0:T(8,128)(2,1)S(1)}, bf16[7,16,1024]{2,1,0:T(8,128)(2,1)}, u32[]{:S(2)}) copy-start(bf16[7,16,1024]{2,1,0:T(8,128)(2,1)} %refs_2_.2) | copy-start | bytes 688132
  6.8 7.9 %collective-permute-start.2 = (bf16[7,16,256]{2,1,0:T(8,128)(2,1)S(1)}, bf16[7,16,256]{2,1,0:T(8,128)(2,1)S(1)}, u32[]{:S(2)}, u32[]{:S(2)}) collective-permute-start(bf16[7,16,256]{2,1,0:T(8,128)(2,1)S(1)} %get-tuple-element.36), channel_id=1, source_target_pairs={{0,8},{8,0},{16,24},{24,16},{1,9},{9,1},{17,25},{25,17},{2,10},{10... | collective-permute-start | bytes 172040 | tf_op jit(solution)/shard_map/ppermute | solution.py:484
  8.4 6.6 %collective-permute-start.3 = (bf16[7,16,256]{2,1,0:T(8,128)(2,1)S(1)}, bf16[7,16,256]{2,1,0:T(8,128)(2,1)S(1)}, u32[]{:S(2)}, u32[]{:S(2)}) collective-permute-start(bf16[7,16,256]{2,1,0:T(8,128)(2,1)S(1)} %get-tuple-element.37), channel_id=1, source_target_pairs={{0,16},{8,24},{16,0},{24,8},{1,17},{9,25},{17,1},{25,9},{2,18},{10... | collective-permute-start | bytes 172040 | tf_op jit(solution)/shard_map/ppermute | solution.py:484
  11.0 6.0 %collective-permute-start.4 = (bf16[7,16,256]{2,1,0:T(8,128)(2,1)S(1)}, bf16[7,16,256]{2,1,0:T(8,128)(2,1)S(1)}, u32[]{:S(2)}, u32[]{:S(2)}) collective-permute-start(bf16[7,16,256]{2,1,0:T(8,128)(2,1)S(1)} %get-tuple-element.38), channel_id=1, source_target_pairs={{0,24},{8,16},{16,8},{24,0},{1,25},{9,17},{17,9},{25,1},{2,26},{10... | collective-permute-start | bytes 172040 | tf_op jit(solution)/shard_map/ppermute | solution.py:484
  12.0 5.1 %copy-start.16 = (bf16[1,1,256]{2,1,0:T(2,128)(2,1)S(1)}, bf16[1,1,256]{2,1,0:T(2,128)(2,1)}, u32[]{:S(2)}) copy-start(bf16[1,1,256]{2,1,0:T(2,128)(2,1)} %refs_7_.2) | copy-start | bytes 1540
  14.7 2.4 %copy-start.13 = (s32[1,1,256]{2,1,0:T(1,128)S(1)}, s32[1,1,256]{2,1,0:T(1,128)}, u32[]{:S(2)}) copy-start(s32[1,1,256]{2,1,0:T(1,128)} %rest_4_.1) | copy-start | bytes 3076
  17.1 8.9 %copy-start.9 = (bf16[64,256]{1,0:T(8,128)(2,1)S(1)}, bf16[64,256]{1,0:T(8,128)(2,1)}, u32[]{:S(2)}) copy-start(bf16[64,256]{1,0:T(8,128)(2,1)} %refs_4_.1) | copy-start | bytes 98308
  17.1 8.9 %copy-start.10 = (bf16[64,224]{1,0:T(8,128)(2,1)S(1)}, bf16[64,224]{1,0:T(8,128)(2,1)}, u32[]{:S(2)}) copy-start(bf16[64,224]{1,0:T(8,128)(2,1)} %refs_8_.1) | copy-start | bytes 86020
  17.1 8.9 %copy-start.12 = (bf16[64,64]{1,0:T(8,128)(2,1)S(1)}, bf16[64,64]{1,0:T(8,128)(2,1)}, u32[]{:S(2)}) copy-start(bf16[64,64]{1,0:T(8,128)(2,1)} %refs_7_.3) | copy-start | bytes 24580
  17.1 8.9 %copy-start.15 = (bf16[8,64]{1,0:T(8,128)(2,1)S(1)}, bf16[8,64]{1,0:T(8,128)(2,1)}, u32[]{:S(2)}) copy-start(bf16[8,64]{1,0:T(8,128)(2,1)} %refs_5_.1) | copy-start | bytes 3076
  17.1 8.9 %copy-start.18 = (f32[64]{0:T(128)S(1)}, f32[64]{0:T(128)}, u32[]{:S(2)}) copy-start(f32[64]{0:T(128)} %param.25) | copy-start | bytes 772
  17.1 8.9 %copy-start.19 = (f32[64]{0:T(128)S(1)}, f32[64]{0:T(128)}, u32[]{:S(2)}) copy-start(f32[64]{0:T(128)} %param.30) | copy-start | bytes 772
  17.6 8.4 %copy-start.8 = (bf16[64,256]{1,0:T(8,128)(2,1)S(1)}, bf16[64,256]{1,0:T(8,128)(2,1)}, u32[]{:S(2)}) copy-start(bf16[64,256]{1,0:T(8,128)(2,1)} %refs_3_.1) | copy-start | bytes 98308
  17.6 9.5 %collective-permute-start.8 = (bf16[528,128]{1,0:T(8,128)(2,1)S(1)}, bf16[528,128]{1,0:T(8,128)(2,1)S(1)}, u32[]{:S(2)}, u32[]{:S(2)}) collective-permute-start(bf16[528,128]{1,0:T(8,128)(2,1)S(1)} %get-tuple-element.53), channel_id=1, source_target_pairs={{0,1},{1,0},{2,3},{3,2},{4,5},{5,4},{6,7},{7,6},{8,9},{9,8},{10,11... | collective-permute-start | bytes 405512 | tf_op jit(solution)/shard_map/ppermute | solution.py:481
  17.7 4.5 %collective-permute-start.5 = (bf16[16,256]{1,0:T(8,128)(2,1)S(1)}, bf16[16,256]{1,0:T(8,128)(2,1)S(1)}, u32[]{:S(2)}, u32[]{:S(2)}) collective-permute-start(bf16[16,256]{1,0:T(8,128)(2,1)S(1)} %get-tuple-element.41), channel_id=1, source_target_pairs={{0,8},{8,0},{16,24},{24,16},{1,9},{9,1},{17,25},{25,17},{2,10},{10... | collective-permute-start | bytes 24584 | tf_op jit(solution)/shard_map/ppermute | solution.py:484
  18.5 4.6 %collective-permute-start.6 = (bf16[16,256]{1,0:T(8,128)(2,1)S(1)}, bf16[16,256]{1,0:T(8,128)(2,1)S(1)}, u32[]{:S(2)}, u32[]{:S(2)}) collective-permute-start(bf16[16,256]{1,0:T(8,128)(2,1)S(1)} %get-tuple-element.42), channel_id=1, source_target_pairs={{0,16},{8,24},{16,0},{24,8},{1,17},{9,25},{17,1},{25,9},{2,18},{10... | collective-permute-start | bytes 24584 | tf_op jit(solution)/shard_map/ppermute | solution.py:484
  20.2 5.4 %collective-permute-start.7 = (bf16[16,256]{1,0:T(8,128)(2,1)S(1)}, bf16[16,256]{1,0:T(8,128)(2,1)S(1)}, u32[]{:S(2)}, u32[]{:S(2)}) collective-permute-start(bf16[16,256]{1,0:T(8,128)(2,1)S(1)} %get-tuple-element.43), channel_id=1, source_target_pairs={{0,24},{8,16},{16,8},{24,0},{1,25},{9,17},{17,9},{25,1},{2,26},{10... | collective-permute-start | bytes 24584 | tf_op jit(solution)/shard_map/ppermute | solution.py:484
  25.7 0.7 %copy-start.11 = (bf16[64,64]{1,0:T(8,128)(2,1)S(1)}, bf16[64,64]{1,0:T(8,128)(2,1)}, u32[]{:S(2)}) copy-start(bf16[64,64]{1,0:T(8,128)(2,1)} %refs_2_.3) | copy-start | bytes 24580
  25.9 1.2 %collective-permute-start.9 = (bf16[64,128]{1,0:T(8,128)(2,1)S(1)}, bf16[64,128]{1,0:T(8,128)(2,1)S(1)}, u32[]{:S(2)}, u32[]{:S(2)}) collective-permute-start(bf16[64,128]{1,0:T(8,128)(2,1)S(1)} %get-tuple-element.54), channel_id=1, source_target_pairs={{0,1},{1,0},{2,3},{3,2},{4,5},{5,4},{6,7},{7,6},{8,9},{9,8},{10,11... | collective-permute-start | bytes 49160 | tf_op jit(solution)/shard_map/ppermute | solution.py:481
  25.9 0.7 %copy-start.14 = (bf16[8,64]{1,0:T(8,128)(2,1)S(1)}, bf16[8,64]{1,0:T(8,128)(2,1)}, u32[]{:S(2)}) copy-start(bf16[8,64]{1,0:T(8,128)(2,1)} %refs_0_.1) | copy-start | bytes 3076
  25.9 0.7 %copy-start.17 = (f32[224]{0:T(256)S(1)}, f32[224]{0:T(256)}, u32[]{:S(2)}) copy-start(f32[224]{0:T(256)} %param.33) | copy-start | bytes 2692
  33.4 10.4 %collective-permute-start.10 = (f32[64,128]{1,0:T(8,128)S(1)}, f32[64,128]{1,0:T(8,128)S(1)}, u32[]{:S(2)}, u32[]{:S(2)}) collective-permute-start(f32[64,128]{1,0:T(8,128)S(1)} %shard_map.171.work), channel_id=1, source_target_pairs={{0,1},{1,0},{2,3},{3,2},{4,5},{5,4},{6,7},{7,6},{8,9},{9,8},{10,11... | collective-permute-start | bytes 98312 | tf_op jit(solution)/shard_map/ppermute | solution.py:481
  53.0 5.0 %collective-permute-start.11 = (f32[16,256]{1,0:T(8,128)S(1)}, f32[16,256]{1,0:T(8,128)S(1)}, u32[]{:S(2)}, u32[]{:S(2)}) collective-permute-start(f32[16,256]{1,0:T(8,128)S(1)} %get-tuple-element.62), channel_id=1, source_target_pairs={{0,8},{8,0},{16,24},{24,16},{1,9},{9,1},{17,25},{25,17},{2,10},{10... | collective-permute-start | bytes 49160 | tf_op jit(solution)/shard_map/ppermute | solution.py:484
  53.0 4.9 %collective-permute-start.12 = (f32[16,256]{1,0:T(8,128)S(1)}, f32[16,256]{1,0:T(8,128)S(1)}, u32[]{:S(2)}, u32[]{:S(2)}) collective-permute-start(f32[16,256]{1,0:T(8,128)S(1)} %get-tuple-element.63), channel_id=1, source_target_pairs={{0,16},{8,24},{16,0},{24,8},{1,17},{9,25},{17,1},{25,9},{2,18},{10... | collective-permute-start | bytes 49160 | tf_op jit(solution)/shard_map/ppermute | solution.py:484
  55.5 5.5 %collective-permute-start.13 = (f32[16,256]{1,0:T(8,128)S(1)}, f32[16,256]{1,0:T(8,128)S(1)}, u32[]{:S(2)}, u32[]{:S(2)}) collective-permute-start(f32[16,256]{1,0:T(8,128)S(1)} %get-tuple-element.64), channel_id=1, source_target_pairs={{0,24},{8,16},{16,8},{24,0},{1,25},{9,17},{17,9},{25,1},{2,26},{10... | collective-permute-start | bytes 49160 | tf_op jit(solution)/shard_map/ppermute | solution.py:484
